TPU v7x, 32 devices: a whole 2x2x4 slice. The times are simulated.
32 devices in a mesh: gx: 4 (over x, core), gy: 4 (over z), fsdp: 2 (over y).
Axes of the slice: x: 2, y: 2, z: 4, core: 2. Of those that a mesh axis runs over, the one named last changes fastest.
Arguments:
- tokens: bfloat16 [16384, 512], P(('gx', 'gy', 'fsdp')), may hold values from -6 to 6
- gain_one: float32 [512], replicated, may hold values from 0.1 to 1.9
- gain_two: float32 [512], replicated, may hold values from 0.1 to 1.9
- w_qkv: bfloat16 [1536, 512], P('fsdp'), may hold values from -1 to 1
- w_out: bfloat16 [512, 512], P('fsdp'), may hold values from -0.25 to 0.25
- w_in: bfloat16 [2048, 512], P('fsdp'), may hold values from -0.25 to 0.25
- w_down: bfloat16 [2048, 512], P('fsdp'), may hold values from -0.125 to 0.125
- send_x: int32 [4096], P(('gx', 'gy', 'fsdp')), may hold values from 0 to 511
- send_y: int32 [4096], P(('gx', 'gy', 'fsdp')), may hold values from 0 to 511
- context: int32 [128, 128], P(('gx', 'gy', 'fsdp')), may hold values from 0 to 767
- lengths: int32 [128], P(('gx', 'gy', 'fsdp')), may hold values from 1 to 128
Outputs:
- output: bfloat16 [16384, 512], P(('gx', 'gy', 'fsdp'))
Inputs may be any that keep to these rules, and one draw needn't show every extreme that they name: `send_x`: row numbers inside the sending piece. `send_y`: row numbers inside the sending piece. `context`: row numbers inside the window's pool.
All inputs are finite; a program needn't handle non-finite values.
Results may differ from a plain program's by a relative error of at most 0.0094.
Values may be sent and summed in bfloat16 or wider, within the bound.
No kernel may reach another device: no remote copies, remote signals or barrier semaphores. Data moves between devices by JAX's collectives and lax.ppermute only.
A program may use at most 64 MiB of HBM per device.

v0:
```python
import jax
import jax.numpy as jnp
from jax import lax
from jax.sharding import PartitionSpec as P

HEADS = 16
WIN = 128
CTX = 128


EPSILON = 1e-05


def shifted(value, axis, steps):
    count = lax.axis_size(axis)
    initial, last = (max(0, -steps), min(count, count - steps))
    return lax.ppermute(value, axis, [(source, source + steps) for source in range(initial, last)])


def layer_norm(values, gain):
    values = values.astype(jnp.float32)
    center = values - jnp.mean(values, axis=-1, keepdims=True)
    spread = jnp.mean(center * center, axis=-1, keepdims=True)
    return (center * lax.rsqrt(spread + EPSILON) * gain).astype(jnp.bfloat16)


def plain_finish(product):
    return product


def round_finish(product):
    return product.astype(jnp.bfloat16)


def gelu_finish(product):
    return jax.nn.gelu(product).astype(jnp.bfloat16)


def project_with(inputs, finish, piece):
    results = []
    for first in range(0, piece.shape[0], 512):
        weight_rows = piece[first : first + 512]
        product = lax.dot_general(
            inputs, weight_rows, (((1,), (1,)), ((), ())), preferred_element_type=jnp.float32
        )
        results.append(finish(product))
    return jnp.concatenate(results, axis=1)


def attend(projected, pool, chosen, window_lengths):
    width = projected.shape[1] // 3
    count = projected.shape[0] // WIN
    head_size = width // HEADS
    group = max(1, min(HEADS, 128 // head_size))
    queries = projected[:, :width].reshape(count, WIN, width)
    gathered = jnp.take(pool, chosen, axis=0)
    pairs = jnp.concatenate([projected[:, width:].reshape(count, WIN, 2 * width), gathered], axis=1)
    keep = jnp.concatenate(
        [jnp.arange(WIN)[None, :] < window_lengths[:, None], jnp.ones((count, CTX), dtype=bool)],
        axis=1,
    )
    results = []
    for first in range(0, HEADS, group):
        low = first * head_size
        high = (first + group) * head_size
        query_part = queries[..., low:high].reshape(count, WIN, group, head_size)
        key_part = pairs[..., low:high].reshape(count, WIN + CTX, group, head_size)
        value_part = pairs[..., width + low : width + high].reshape(
            count, WIN + CTX, group, head_size
        )
        scores = jnp.einsum(
            "wqhe,wkhe->whqk", query_part, key_part, preferred_element_type=jnp.float32
        ) * head_size ** (-0.5)
        scores = jnp.where(keep[:, None, None, :], scores, -1e30)
        largest = jnp.max(scores, axis=-1, keepdims=True)
        expo = jnp.exp(scores - largest)
        total = jnp.sum(expo, axis=-1, keepdims=True)
        probs = (expo / total).astype(jnp.bfloat16)
        mixed = jnp.einsum("whqk,wkhe->wqhe", probs, value_part, preferred_element_type=jnp.float32)
        results.append(mixed.reshape(count, WIN, group * head_size))
    return jnp.concatenate(results, axis=-1).reshape(count * WIN, width).astype(jnp.bfloat16)


def body(tokens, gain_one, gain_two, w_qkv, w_out, w_in, w_down, send_x, send_y, context, lengths):
    width = tokens.shape[1]
    normed = layer_norm(tokens, gain_one)
    projected = project_with(
        normed, round_finish, lax.all_gather(w_qkv, "fsdp", axis=0, tiled=True)
    )
    own_pairs = projected[:, width:]
    halo_x = shifted(jnp.take(own_pairs, send_x, axis=0), "gx", 1)
    halo_y = shifted(jnp.take(own_pairs, send_y, axis=0), "gy", 1)
    pool = jnp.concatenate([own_pairs, halo_x, halo_y], axis=0)
    mixed = attend(projected, pool, context, lengths)
    attended = project_with(mixed, plain_finish, lax.all_gather(w_out, "fsdp", axis=0, tiled=True))
    middle = tokens.astype(jnp.float32) + attended
    second = layer_norm(middle, gain_two)
    hidden = project_with(second, gelu_finish, lax.all_gather(w_in, "fsdp", axis=0, tiled=True))
    feed = jnp.dot(
        hidden,
        lax.all_gather(w_down, "fsdp", axis=0, tiled=True),
        preferred_element_type=jnp.float32,
    )
    return (middle + feed).astype(jnp.bfloat16)


def solution(mesh):
    in_specs = (
        P(("gx", "gy", "fsdp"), None),
        P(),
        P(),
        P("fsdp", None),
        P("fsdp", None),
        P("fsdp", None),
        P("fsdp", None),
        P(("gx", "gy", "fsdp")),
        P(("gx", "gy", "fsdp")),
        P(("gx", "gy", "fsdp"), None),
        P(("gx", "gy", "fsdp")),
    )
    out_specs = P(("gx", "gy", "fsdp"), None)
    return jax.shard_map(body, mesh=mesh, in_specs=in_specs, out_specs=out_specs, check_vma=False)
```

profile of v0, /device:TPU:0, one launch (start us, length us, event | category | flops | bytes accessed | tf_op | source)
XLA Modules:
  0.0 118.9 jit_solution(17315402878651402700)
XLA Ops:
  6.5 0.0 all-gather.4.cloned.1.call-start
  6.6 0.7 all-gather.4.cloned.1.call-update
  7.3 0.0 all-gather.6.cloned.1.call-start
  7.3 0.7 all-gather.6.cloned.1.call-update
  8.1 0.0 all-gather.8.cloned.1.call-start
  8.1 0.7 all-gather.8.cloned.1.call-update
  8.9 0.2 copy.33
  9.1 0.1 convert_reduce_fusion
  9.3 0.2 fusion.28
  9.5 0.1 iota_compare_fusion
  9.6 10.0 %all_gather.13 = bf16[512,512]{1,0:T(8,128)(2,1)} all-gather(bf16[256,512]{1,0:T(8,128)(2,1)S(1)} %copy-done.9), channel_id=1, replica_groups=mesh['gx'=4,'gy'=4,'fsdp'=2] {'fsdp'}, dimensions={0}, use_global_device_ids=true | all-gather | bytes 786432 | tf_op jit(solution)/shard_map/all_gather | solution.py:95
  19.6 19.3 %all-gather.4.cloned.1.call-done = bf16[1536,512]{1,0:T(8,128)(2,1)} async-done(((bf16[768,512]{1,0:T(8,128)(2,1)}), bf16[1536,512]{1,0:T(8,128)(2,1)}) %all-gather.4.cloned.1.call-update) | async-done | bytes 1572880 | tf_op jit(solution)/shard_map/all_gather | solution.py:88
  38.9 1.6 %convolution_convert_fusion.1 = bf16[512,512]{0,1:T(8,128)(2,1)S(1)} fusion(bf16[1536,512]{1,0:T(8,128)(2,1)} %all-gather.4.cloned.1.call-done, bf16[512,512]{0,1:T(8,128)(2,1)S(1)} %copy.33, f32[512]{0:T(512)S(1)} %copy-done.16, f32[512]{0:T(512)S(1)} %add_rsqrt_fusion.1, f32[512]{0:T(512)S(1)} %broadcast_multiply_fusion.1), kind=kOutput, calls=%fused_computation.55 | convolution fusion | flops 270008320 | bytes 1579008 | tf_op jit(solution)/shard_map/dot_general | solution.py:43
  40.4 1.7 %convolution_convert_fusion = bf16[512,512]{0,1:T(8,128)(2,1)S(1)} fusion(bf16[1536,512]{1,0:T(8,128)(2,1)} %all-gather.4.cloned.1.call-done, bf16[512,512]{0,1:T(8,128)(2,1)S(1)} %copy.33, f32[512]{0:T(512)S(1)} %copy-done.16, f32[512]{0:T(512)S(1)} %add_rsqrt_fusion.1, f32[512]{0:T(512)S(1)} %broadcast_multiply_fusion.1), kind=kOutput, calls=%fused_computation.54 | convolution fusion | flops 270008320 | bytes 1579008 | tf_op jit(solution)/shard_map/dot_general | solution.py:43
  42.2 0.8 copy-done.5
  43.0 0.1 pad_maximum_fusion.1
  43.1 0.5 copy.34
  43.6 0.9 gather_fusion.1
  44.5 0.2 copy.35
  44.6 0.7 broadcast_select_fusion.2
  45.4 1.7 %collective-permute-start = (bf16[128,1024]{0,1:T(8,128)(2,1)}, bf16[128,1024]{0,1:T(8,128)(2,1)S(1)}, u32[]{:S(2)}, u32[]{:S(2)}) collective-permute-start(bf16[128,1024]{0,1:T(8,128)(2,1)} %broadcast_select_fusion.2), channel_id=1, source_target_pairs={{0,8},{8,16},{16,24},{1,9},{9,17},{17,25},{2,10},{10,18},{18,26},{... | collective-permute-start | bytes 786440 | tf_op jit(solution)/shard_map/ppermute | solution.py:17
  47.1 0.9 gather_fusion.2
  48.0 0.2 copy.37
  48.2 0.7 broadcast_select_fusion.1
  48.9 4.1 %collective-permute-start.1 = (bf16[128,1024]{0,1:T(8,128)(2,1)}, bf16[128,1024]{0,1:T(8,128)(2,1)}, u32[]{:S(2)}, u32[]{:S(2)}) collective-permute-start(bf16[128,1024]{0,1:T(8,128)(2,1)} %broadcast_select_fusion.1), channel_id=1, source_target_pairs={{0,2},{2,4},{4,6},{1,3},{3,5},{5,7},{8,10},{10,12},{12,14},{9,11},... | collective-permute-start | bytes 786440 | tf_op jit(solution)/shard_map/ppermute | solution.py:17
  53.0 1.7 %convolution_convert_fusion.2 = bf16[512,512]{1,0:T(8,128)(2,1)S(1)} fusion(bf16[1536,512]{1,0:T(8,128)(2,1)} %all-gather.4.cloned.1.call-done, bf16[512,512]{0,1:T(8,128)(2,1)S(1)} %copy.33, f32[512]{0:T(512)S(1)} %copy-done.16, f32[512]{0:T(512)S(1)} %add_rsqrt_fusion.1, f32[512]{0:T(512)S(1)} %broadcast_multiply_fusion.1), kind=kOutput, calls=%fused_computation.56 | convolution fusion | flops 270008320 | bytes 1579008 | tf_op jit(solution)/shard_map/dot_general | solution.py:43
  54.7 1.1 reshape.105
  55.8 0.1 fusion.150
  55.9 0.8 copy.41
  56.7 0.8 copy.45
  57.5 0.8 copy.49
  58.2 0.1 copy.53
  58.4 0.2 collective-permute-done.1
  58.5 1.1 pad_maximum_fusion
  59.6 0.8 copy.38
  60.4 2.1 %gather_fusion = bf16[512,1024]{1,0:T(8,128)(2,1)S(1)} fusion(bf16[768,1024]{1,0:T(8,128)(2,1)S(1)} %copy.38, s32[1024]{0:T(1024)S(1)} %pad_clamp_fusion), kind=kCustom, calls=%fused_computation.2 | custom fusion | bytes 2099200 | tf_op jit(solution)/shard_map/jit(_take)/gather | solution.py:56
  62.4 0.8 copy.39
  63.2 0.5 broadcast_select_fusion
  63.7 0.8 copy-done.2
  64.4 1.7 %fusion.103 = (bf16[4,256,128]{1,0,2:T(4,128)(2,1)S(1)}, bf16[4,256,128]{1,0,2:T(4,128)(2,1)S(1)}, bf16[4,256,128]{1,0,2:T(4,128)(2,1)S(1)}, bf16[4,256,128]{1,0...) fusion(bf16[4,128,1024]{1,0,2:T(4,128)(2,1)S(1)} %copy-done.2, ...), kind=kLoop, calls=%fused_computation.139 | loop fusion | flops 4194304 | bytes 4194304 | tf_op jit(solution)/shard_map/concatenate | solution.py:57
  66.2 0.9 fusion.154
  67.1 1.1 fusion.24
  68.2 0.1 copy.43
  68.4 0.9 fusion.153
  69.4 1.1 fusion.25
  70.5 0.1 copy.47
  70.7 0.9 fusion.152
  71.6 1.1 fusion.26
  72.7 0.1 copy.51
  72.9 0.9 fusion.151
  73.8 1.1 fusion.27
  74.9 0.1 copy.55
  75.2 0.5 fusion.155
  75.6 0.2 multiply_reduce_fusion
  75.8 0.0 copy-done.14
  75.8 0.1 multiply_convert_fusion
  76.0 0.0 all-gather.6.cloned.1.call-done
  76.0 1.8 %fusion.38 = bf16[512,512]{0,1:T(8,128)(2,1)S(1)} fusion(bf16[512,512]{0,1:T(8,128)(2,1)S(1)} %multiply_convert_fusion, bf16[2048,512]{1,0:T(8,128)(2,1)} %all-gather.6.cloned.1.call-done), kind=kOutput, calls=%fused_computation.78 | convolution fusion | flops 270794752 | bytes 1572864 | tf_op jit(solution)/shard_map/dot_general | solution.py:43
  77.9 0.6 fusion.46
  78.5 0.6 fusion.54
  79.2 1.4 %fusion.62 = bf16[512,512]{0,1:T(8,128)(2,1)} fusion(bf16[512,512]{0,1:T(8,128)(2,1)S(1)} %multiply_convert_fusion, bf16[2048,512]{1,0:T(8,128)(2,1)S(1)} %copy-done.15), kind=kOutput, calls=%fused_computation.102 | convolution fusion | flops 270794752 | bytes 1572864 | tf_op jit(solution)/shard_map/dot_general | solution.py:43
  80.6 27.7 %all-gather.8.cloned.1.call-done = bf16[2048,512]{1,0:T(8,128)(2,1)} async-done(((bf16[1024,512]{1,0:T(8,128)(2,1)}), bf16[2048,512]{1,0:T(8,128)(2,1)}) %all-gather.8.cloned.1.call-update) | async-done | bytes 2097168 | tf_op jit(solution)/shard_map/all_gather | solution.py:101
  108.3 3.1 %fusion.19 = bf16[512,512]{0,1:T(8,128)(2,1)S(1)} fusion(f32[512,512]{0,1:T(8,128)S(1)} %get-tuple-element.19, bf16[2048,512]{1,0:T(8,128)(2,1)} %all-gather.8.cloned.1.call-done, bf16[512,512]{0,1:T(8,128)(2,1)} %fusion.62, bf16[512,512]{0,1:T(8,128)(2,1)S(1)} %fusion.54, bf16[512,512]{0,1:T(8,128)(2,1)S(1)} %fusion.46, bf16[512,512]{0,1:T(8,128)(2,1)S(1)} %fusion.38), kind=kOutput, calls=%fused_computation.57 | convolution fusion | flops 1082654720 | bytes 5767168 | tf_op jit(solution)/shard_map/dot_general | solution.py:99
  111.3 1.0 copy.57
  (62 shorter events, 0.5 us)
Async XLA Ops:
  6.5 2.3 %copy-start.17 = (s32[128]{0:T(128)S(1)}, s32[128]{0:T(128)}, u32[]{:S(2)}) copy-start(s32[128]{0:T(128)} %param.20) | copy-start | bytes 1540
  6.5 2.3 %copy-start.18 = (s32[128]{0:T(128)S(1)}, s32[128]{0:T(128)}, u32[]{:S(2)}) copy-start(s32[128]{0:T(128)} %param.21) | copy-start | bytes 1540
  6.5 2.3 %copy-start.13 = (s32[4,128]{1,0:T(4,128)S(1)}, s32[4,128]{1,0:T(4,128)}, u32[]{:S(2)}) copy-start(s32[4,128]{1,0:T(4,128)} %param.22) | copy-start | bytes 6148
  6.5 2.4 %copy-start.8 = (bf16[512,512]{1,0:T(8,128)(2,1)S(1)}, bf16[512,512]{1,0:T(8,128)(2,1)}, u32[]{:S(2)}) copy-start(bf16[512,512]{1,0:T(8,128)(2,1)} %param.13) | copy-start | bytes 1572868
  6.5 32.3 %all-gather.4.cloned.1.call-start = ((), (), s32[]{:S(2)}) async-start(), calls=%async_computation | async-start | bytes 2359296 | tf_op jit(solution)/shard_map/all_gather | solution.py:88
  7.3 2.2 %copy-start.19 = (s32[4]{0:T(128)S(1)}, s32[4]{0:T(128)}, u32[]{:S(2)}) copy-start(s32[4]{0:T(128)} %param.23) | copy-start | bytes 52
  7.3 2.3 %copy-start.9 = (bf16[256,512]{1,0:T(8,128)(2,1)S(1)}, bf16[256,512]{1,0:T(8,128)(2,1)}, u32[]{:S(2)}) copy-start(bf16[256,512]{1,0:T(8,128)(2,1)} %param.17) | copy-start | bytes 786436
  7.3 68.7 %all-gather.6.cloned.1.call-start = ((), (), s32[]{:S(2)}) async-start(), calls=%async_computation.1 | async-start | bytes 3145728 | tf_op jit(solution)/shard_map/all_gather | solution.py:98
  8.0 30.8 %copy-start.16 = (f32[512]{0:T(512)S(1)}, f32[512]{0:T(512)}, u32[]{:S(2)}) copy-start(f32[512]{0:T(512)} %param.14) | copy-start | bytes 6148
  8.1 100.2 %all-gather.8.cloned.1.call-start = ((), (), s32[]{:S(2)}) async-start(), calls=%async_computation.2 | async-start | bytes 3145728 | tf_op jit(solution)/shard_map/all_gather | solution.py:101
  9.1 43.9 %copy-start = (bf16[512,512]{0,1:T(8,128)(2,1)}, bf16[512,512]{0,1:T(8,128)(2,1)S(1)}, u32[]{:S(2)}) copy-start(bf16[512,512]{0,1:T(8,128)(2,1)S(1)} %copy.33) | copy-start | bytes 1572868
  40.4 1.8 %copy-start.3 = (bf16[512,512]{0,1:T(8,128)(2,1)}, bf16[512,512]{0,1:T(8,128)(2,1)S(1)}, u32[]{:S(2)}) copy-start(bf16[512,512]{0,1:T(8,128)(2,1)S(1)} %convolution_convert_fusion.1) | copy-start | bytes 1572868
  42.2 0.8 copy-start.5
  45.4 13.0 %collective-permute-start = (bf16[128,1024]{0,1:T(8,128)(2,1)}, bf16[128,1024]{0,1:T(8,128)(2,1)S(1)}, u32[]{:S(2)}, u32[]{:S(2)}) collective-permute-start(bf16[128,1024]{0,1:T(8,128)(2,1)} %broadcast_select_fusion.2), channel_id=1, source_target_pairs={{0,8},{8,16},{16,24},{1,9},{9,17},{17,25},{2,10},{10,18},{18,26},{... | collective-permute-start | bytes 786440 | tf_op jit(solution)/shard_map/ppermute | solution.py:17
  48.9 9.6 %collective-permute-start.1 = (bf16[128,1024]{0,1:T(8,128)(2,1)}, bf16[128,1024]{0,1:T(8,128)(2,1)}, u32[]{:S(2)}, u32[]{:S(2)}) collective-permute-start(bf16[128,1024]{0,1:T(8,128)(2,1)} %broadcast_select_fusion.1), channel_id=1, source_target_pairs={{0,2},{2,4},{4,6},{1,3},{3,5},{5,7},{8,10},{10,12},{12,14},{9,11},... | collective-permute-start | bytes 786440 | tf_op jit(solution)/shard_map/ppermute | solution.py:17
  54.6 3.9 %copy-start.4 = (bf16[512,512]{0,1:T(8,128)(2,1)S(1)}, bf16[512,512]{0,1:T(8,128)(2,1)}, u32[]{:S(2)}) copy-start(bf16[512,512]{0,1:T(8,128)(2,1)} %copy-done.3) | copy-start | bytes 1572868
  54.7 3.9 %copy-start.6 = (bf16[512,512]{0,1:T(8,128)(2,1)S(1)}, bf16[512,512]{0,1:T(8,128)(2,1)}, u32[]{:S(2)}) copy-start(bf16[512,512]{0,1:T(8,128)(2,1)} %copy-done.5) | copy-start | bytes 1572868
  63.2 1.2 %copy-start.2 = (bf16[4,128,1024]{1,0,2:T(4,128)(2,1)S(1)}, bf16[4,128,1024]{1,0,2:T(4,128)(2,1)}, u32[]{:S(2)}) copy-start(bf16[4,128,1024]{1,0,2:T(4,128)(2,1)} %reshape.105) | copy-start | bytes 3145732
  64.4 1.7 %copy-start.12 = (bf16[4,128,128]{1,2,0:T(8,128)(2,1)S(1)}, bf16[4,128,128]{1,2,0:T(8,128)(2,1)}, u32[]{:S(2)}) copy-start(bf16[4,128,128]{1,2,0:T(8,128)(2,1)} %copy.41) | copy-start | bytes 393220
  67.1 1.3 %copy-start.11 = (bf16[4,128,128]{1,2,0:T(8,128)(2,1)S(1)}, bf16[4,128,128]{1,2,0:T(8,128)(2,1)}, u32[]{:S(2)}) copy-start(bf16[4,128,128]{1,2,0:T(8,128)(2,1)} %copy.45) | copy-start | bytes 393220
  69.4 1.3 %copy-start.10 = (bf16[4,128,128]{1,2,0:T(8,128)(2,1)S(1)}, bf16[4,128,128]{1,2,0:T(8,128)(2,1)}, u32[]{:S(2)}) copy-start(bf16[4,128,128]{1,2,0:T(8,128)(2,1)} %copy.49) | copy-start | bytes 393220
  73.8 1.3 %copy-start.1 = (bf16[512,512]{0,1:T(8,128)(2,1)S(1)}, bf16[512,512]{0,1:T(8,128)(2,1)}, u32[]{:S(2)}) copy-start(bf16[512,512]{0,1:T(8,128)(2,1)} %copy-done) | copy-start | bytes 1572868
  73.8 1.3 %copy-start.7 = (bf16[512,512]{1,0:T(8,128)(2,1)S(1)}, bf16[512,512]{1,0:T(8,128)(2,1)}, u32[]{:S(2)}) copy-start(bf16[512,512]{1,0:T(8,128)(2,1)} %all_gather.13) | copy-start | bytes 1572868
  75.2 0.7 copy-start.14
  76.0 1.8 %copy-start.15 = (bf16[2048,512]{1,0:T(8,128)(2,1)S(1)}, bf16[2048,512]{1,0:T(8,128)(2,1)}, u32[]{:S(2)}) copy-start(bf16[2048,512]{1,0:T(8,128)(2,1)} %all-gather.6.cloned.1.call-done) | copy-start | bytes 6291460
Sparse Core Ops, SparseCore 0:
  8.9 29.8 all-gather.3
  40.4 33.1 all-gather.5
  75.1 33.1 all-gather.7
where the time goes:
time: 119 us
  waiting for transfers between devices  49.2 us (41%)
  matrix products  21.1 us (18%)
  between operations  13.7 us (12%)
  local copies, waits for them, and re-layouts  13.5 us (11%)
  blocking collectives  10 us (8%)
  starting transfers between devices  5.94 us (5%)
  other arithmetic  5.48 us (5%)
    all_gather x1, waiting for transfers between devices, body(): lax.all_gather(w_down, 'fsdp', axis=0, tiled=True)  27.7 us
    all_gather x1, waiting for transfers between devices, body(): lax.all_gather(w_qkv, 'fsdp', axis=0, tiled=True)  19.3 us
    all_gather x1, blocking collectives, body(): lax.all_gather(w_out, 'fsdp', axis=0, tiled=True)  10 us
    dot_general x8, matrix products, project_with(): lax.dot_general(inputs, weight_rows, (((1,), (1,)), ((), ())), preferred_...  9.93 us
    ppermute x2, starting transfers between devices, shifted(): lax.ppermute(value, axis, [(source, source + steps) for source in range(i...  5.83 us
    dot_general x4, matrix products, attend(): jnp.einsum('whqk,wkhe->wqhe', probs, value_part, preferred_element_type=j...  4.39 us
    sub x4, matrix products, attend(): expo = jnp.exp(scores - largest)  3.72 us
    dot_general x1, matrix products, body(): jnp.dot(hidden, lax.all_gather(w_down, 'fsdp', axis=0, tiled=True), prefe...  3.06 us
  transfers between devices with their start and end apart: 5, of which 3 were waited for; matrix products, arithmetic and copies ran while one was open for 29% of the time, Pallas kernels for 0%

commit v1 on v0

v1 whole, which is shorter than its diff:
```python
import jax
import jax.numpy as jnp
from jax import lax
from jax.experimental import pallas as pl
from jax.experimental.pallas import tpu as pltpu
from jax.sharding import PartitionSpec as P

HEADS = 16
WIN = 128
CTX = 128
LANES = 128
EPSILON = 1e-05
LOG2E = 1.4426950408889634

VMEM = pl.BlockSpec(memory_space=pltpu.VMEM)
SMEM = pl.BlockSpec(memory_space=pltpu.SMEM)
ANY = pl.BlockSpec(memory_space=pl.ANY)
PARAMS = pltpu.CompilerParams(vmem_limit_bytes=40 * 1024 * 1024)


def shifted(value, axis, steps):
    count = lax.axis_size(axis)
    initial, last = (max(0, -steps), min(count, count - steps))
    return lax.ppermute(value, axis, [(source, source + steps) for source in range(initial, last)])


def dot_nt(left, right):
    return lax.dot_general(left, right, (((1,), (1,)), ((), ())), preferred_element_type=jnp.float32)


def dot_nn(left, right):
    return jnp.dot(left, right, preferred_element_type=jnp.float32)


def layer_norm(values, gain):
    values = values.astype(jnp.float32)
    center = values - jnp.mean(values, axis=-1, keepdims=True)
    spread = jnp.mean(center * center, axis=-1, keepdims=True)
    return (center * lax.rsqrt(spread + EPSILON) * gain).astype(jnp.bfloat16)


def pick_rows(indices, count):
    column = jnp.broadcast_to(indices.astype(jnp.float32), (LANES, LANES)).T
    lane = lax.broadcasted_iota(jnp.int32, (LANES, LANES), 1).astype(jnp.float32)
    blocks = [
        jnp.where(column == lane + float(first), 1.0, 0.0).astype(jnp.bfloat16)
        for first in range(0, count, LANES)
    ]
    return jnp.concatenate(blocks, axis=1)


def norm_kernel(tokens, gain, send_x, send_y, out_x, out_y, normed):
    rows = tokens.shape[0]
    block = tokens[...]
    out_x[...] = dot_nn(pick_rows(send_x[...], rows), block).astype(jnp.bfloat16)
    out_y[...] = dot_nn(pick_rows(send_y[...], rows), block).astype(jnp.bfloat16)
    normed[...] = layer_norm(block, gain[...])


def context_kernel(normed, halo_x, halo_y, gain, context, chosen):
    pool = jnp.concatenate(
        [normed[...], layer_norm(halo_x[...], gain[...]), layer_norm(halo_y[...], gain[...])], axis=0
    )
    for window in range(context.shape[0]):
        picked = dot_nn(pick_rows(context[pl.ds(window, 1), :], pool.shape[0]), pool)
        chosen[pl.ds(window * CTX, CTX), :] = picked.astype(jnp.bfloat16)


def load_pieces(places, pieces, target, sems):
    copies = []
    for number, piece in enumerate(pieces):
        rows = piece.shape[0]
        start = pl.multiple_of(places[number], 16)
        copy = pltpu.make_async_copy(piece, target.at[pl.ds(start, rows), :], sems.at[number])
        copy.start()
        copies.append(copy)
    return copies


def attention_kernel(count, *refs):
    lengths, qkv_places, out_places, normed, chosen, tokens, gain = refs[:7]
    qkv_pieces = refs[7 : 7 + count]
    out_pieces = refs[7 + count : 7 + 2 * count]
    middle, second, w_qkv, w_out, mixed, sems = refs[7 + 2 * count :]
    width = tokens.shape[1]
    head_size = width // HEADS
    group = LANES // head_size
    qkv_copies = load_pieces(qkv_places, qkv_pieces, w_qkv, sems.at[0])
    out_copies = load_pieces(out_places, out_pieces, w_out, sems.at[1])
    for copy in qkv_copies:
        copy.wait()
    own, ctx = normed[...], chosen[...]
    w_q, w_k, w_v = (w_qkv[pl.ds(part * width, width), :] for part in range(3))
    queries = dot_nt(w_q, own).astype(jnp.bfloat16)
    own_keys = dot_nt(own, w_k).astype(jnp.bfloat16)
    ctx_keys = dot_nt(ctx, w_k).astype(jnp.bfloat16)
    own_values = dot_nt(w_v, own).astype(jnp.bfloat16)
    ctx_values = dot_nt(w_v, ctx).astype(jnp.bfloat16)
    scale = head_size ** (-0.5) * LOG2E
    for window in range(tokens.shape[0] // WIN):
        low, high = window * WIN, (window + 1) * WIN
        length = lengths[window]
        row = lax.broadcasted_iota(jnp.int32, (WIN, 1), 0)
        keys = jnp.concatenate(
            [
                jnp.where(row < length, own_keys[low:high], ctx_keys[low : low + 1]),
                ctx_keys[low:high],
            ],
            axis=0,
        )
        slot = lax.broadcasted_iota(jnp.int32, (1, WIN), 1)
        values = jnp.concatenate(
            [
                jnp.where(slot < length, own_values[:, low:high], jnp.zeros((), jnp.bfloat16)),
                ctx_values[:, low:high],
            ],
            axis=1,
        )
        slots = lax.broadcasted_iota(jnp.int32, (16, WIN + CTX), 1)
        ones = jnp.where((slots < length) | (slots >= WIN), 1.0, 0.0).astype(jnp.bfloat16)
        for first in range(0, width, LANES):
            group_queries = queries[first : first + LANES, low:high]
            parts = []
            for head in range(group):
                pad = [jnp.zeros((head_size, WIN), jnp.bfloat16)] * group
                pad[head] = group_queries[head * head_size : (head + 1) * head_size]
                parts.append(jnp.concatenate(pad, axis=0))
            scores = dot_nn(keys[:, first : first + LANES], jnp.concatenate(parts, axis=1))
            largest = jnp.max(scores, axis=0, keepdims=True)
            probs = jnp.exp2((scores - largest) * scale).astype(jnp.bfloat16)
            outs = []
            for head in range(0, group, 2):
                top = first + head * head_size
                weights = jnp.concatenate([values[top : top + 2 * head_size], ones], axis=0)
                sums = dot_nn(weights, probs[:, head * WIN : (head + 2) * WIN])
                for part in range(2):
                    block = sums[:, part * WIN : (part + 1) * WIN]
                    outs.append(
                        block[part * head_size : (part + 1) * head_size]
                        * (1.0 / block[2 * head_size : 2 * head_size + 1])
                    )
            mixed[low:high, first : first + LANES] = jnp.concatenate(outs, axis=0).T.astype(jnp.bfloat16)
    for copy in out_copies:
        copy.wait()
    total = tokens[...].astype(jnp.float32) + dot_nt(mixed[...], w_out[...])
    middle[...] = total
    second[...] = layer_norm(total, gain[...])


def feed_kernel(count, middle, second, *refs):
    output = refs[2 * count]
    total = middle[...]
    for number in range(count):
        hidden = jax.nn.gelu(dot_nt(second[...], refs[number][...])).astype(jnp.bfloat16)
        total = total + dot_nn(hidden, refs[count + number][...])
    output[...] = total.astype(output.dtype)


def gather_pieces(weights):
    ranks, cores = lax.axis_size("fsdp"), lax.axis_size("gx")
    if ranks != 2 or cores % 2:
        return [
            ([lax.all_gather(weight, "fsdp", axis=0, tiled=True)], jnp.zeros((1,), jnp.int32))
            for weight in weights
        ]
    rank = lax.axis_index("fsdp")
    core = lax.axis_index("gx") % 2
    swap = [(core_index, core_index ^ 1) for core_index in range(cores)]
    results = []
    for weight in weights:
        rows = weight.shape[0]
        half = rows // 2
        mine = lax.dynamic_slice_in_dim(weight, core * half, half, 0)
        theirs = lax.ppermute(mine, "fsdp", [(0, 1), (1, 0)])
        rest = lax.ppermute(theirs, "gx", swap)
        base = (1 - rank) * rows
        places = jnp.stack([rank * rows, base + core * half, base + (1 - core) * half])
        results.append(([weight, theirs, rest], places.astype(jnp.int32)))
    return results


def body(tokens, gain_one, gain_two, w_qkv, w_out, w_in, w_down, send_x, send_y, context, lengths):
    rows, width = tokens.shape
    halo = send_x.shape[0]
    gain_one, gain_two = gain_one[None, :], gain_two[None, :]
    gathered = gather_pieces([w_qkv, w_out, w_in, w_down])
    (qkv, qkv_places), (out, out_places), (into, _), (down, _) = gathered
    half = jax.ShapeDtypeStruct((rows, width), jnp.bfloat16)
    full = jax.ShapeDtypeStruct((rows, width), jnp.float32)
    edge = jax.ShapeDtypeStruct((halo, width), jnp.bfloat16)
    out_x, out_y, normed = pl.pallas_call(
        norm_kernel, out_shape=(edge, edge, half), in_specs=[VMEM] * 4, out_specs=(VMEM,) * 3,
        compiler_params=PARAMS, name="norm",
    )(tokens, gain_one, send_x[None, :], send_y[None, :])
    halo_x = shifted(out_x, "gx", 1)
    halo_y = shifted(out_y, "gy", 1)
    chosen = pl.pallas_call(
        context_kernel, out_shape=half, in_specs=[VMEM] * 5, out_specs=VMEM,
        compiler_params=PARAMS, name="context",
    )(normed, halo_x, halo_y, gain_one, context)
    count = len(qkv)
    middle, second = pl.pallas_call(
        lambda *refs: attention_kernel(count, *refs),
        out_shape=(full, half),
        in_specs=[SMEM] * 3 + [VMEM] * 4 + [ANY] * (2 * count),
        out_specs=(VMEM, VMEM),
        scratch_shapes=[
            pltpu.VMEM((3 * width, width), jnp.bfloat16),
            pltpu.VMEM((width, width), jnp.bfloat16),
            pltpu.VMEM((rows, width), jnp.bfloat16),
            pltpu.SemaphoreType.DMA((2, count)),
        ],
        compiler_params=PARAMS, name="attention",
    )(lengths, qkv_places, out_places, normed, chosen, tokens, gain_two, *qkv, *out)

    def feed(total, first, last, dtype):
        number = last - first
        return pl.pallas_call(
            lambda *refs: feed_kernel(number, *refs),
            out_shape=jax.ShapeDtypeStruct((rows, width), dtype),
            in_specs=[VMEM] * (2 + 2 * number), out_specs=VMEM,
            compiler_params=PARAMS, name="feed",
        )(total, second, *into[first:last], *down[first:last])

    if count == 1:
        return feed(middle, 0, 1, jnp.bfloat16)
    partial = feed(middle, 0, 1, jnp.float32)
    return feed(partial, 1, count, jnp.bfloat16)


def solution(mesh):
    in_specs = (
        P(("gx", "gy", "fsdp"), None),
        P(),
        P(),
        P("fsdp", None),
        P("fsdp", None),
        P("fsdp", None),
        P("fsdp", None),
        P(("gx", "gy", "fsdp")),
        P(("gx", "gy", "fsdp")),
        P(("gx", "gy", "fsdp"), None),
        P(("gx", "gy", "fsdp")),
    )
    out_specs = P(("gx", "gy", "fsdp"), None)
    return jax.shard_map(body, mesh=mesh, in_specs=in_specs, out_specs=out_specs, check_vma=False)
```

time: 119 us -> 68.6 us (0.58)
  matrix products: 21.1 us -> 0 us
  waiting for transfers between devices: 49.2 us -> 32 us
  Pallas kernels: 0 us -> 17.2 us
  between operations: 13.7 us -> 0.15 us
  blocking collectives: 10 us -> 0 us
  local copies, waits for them, and re-layouts: 13.5 us -> 4.97 us
  starting transfers between devices: 5.94 us -> 13.9 us
  other arithmetic: 5.48 us -> 0.08 us
    all_gather x3 -> x0, waiting for transfers between devices: 47 us -> none  [the longest x1 27.7 us: body(): lax.all_gather(w_down, 'fsdp', axis=0, tiled=True)]
    ppermute x0 -> x8, waiting for transfers between devices: none -> 29.9 us  [the longest x4 29.9 us: gather_pieces(): theirs = lax.ppermute(mine, 'fsdp', [(0, 1), (1, 0)])]
    dot_general x13 -> x0, matrix products: 17.4 us -> none  [the longest x8 9.93 us: project_with(): lax.dot_general(inputs, weight_rows, (((1,), (1,)), ((), ())), preferred_...]
    pallas_call x0 -> x5, Pallas kernels: none -> 17.2 us  [the longest x1 9.1 us: body(): pl.pallas_call(lambda *refs: attention_kernel(count, *refs), out_shape=(f...]
    all_gather x1 -> x0, blocking collectives: 10 us -> none  [body(): lax.all_gather(w_out, 'fsdp', axis=0, tiled=True)]
    ppermute x0 -> x8, starting transfers between devices: none -> 7.47 us  [the longest x4 6.89 us: gather_pieces(): theirs = lax.ppermute(mine, 'fsdp', [(0, 1), (1, 0)])]
    gather x6 -> x0, local copies, waits for them, and re-layouts: 4.88 us -> none  [the longest x2 2.81 us: attend(): gathered = jnp.take(pool, chosen, axis=0)]
    sub x4 -> x0, matrix products: 3.72 us -> none  [attend(): expo = jnp.exp(scores - largest)]
  transfers between devices with their start and end apart: 5 -> 10, of which waited for: 3 -> 5; matrix products, arithmetic and copies ran while one was open for 29% -> 0% of each run, Pallas kernels for 0% -> 20%
where the time goes in v1:
time: 68.6 us; the launch traced here: 68.3 us
  waiting for transfers between devices  32 us (47%)
  Pallas kernels  17.2 us (25%)
  starting transfers between devices  13.9 us (20%)
  local copies, waits for them, and re-layouts  4.97 us (7%)
    ppermute x4, waiting for transfers between devices, gather_pieces(): theirs = lax.ppermute(mine, 'fsdp', [(0, 1), (1, 0)])  29.9 us
    pallas_call x1, Pallas kernels, body(): pl.pallas_call(lambda *refs: attention_kernel(count, *refs), out_shape=(f...  9.1 us
    ppermute x4, starting transfers between devices, gather_pieces(): theirs = lax.ppermute(mine, 'fsdp', [(0, 1), (1, 0)])  6.89 us
    ppermute x2, starting transfers between devices, shifted(): lax.ppermute(value, axis, [(source, source + steps) for source in range(i...  6.47 us
    pallas_call x2, Pallas kernels, feed(): pl.pallas_call(lambda *refs: feed_kernel(number, *refs), out_shape=jax.Sh...  5.29 us
    unnamed x26, local copies, waits for them, and re-layouts  2.93 us
    ppermute x2, waiting for transfers between devices, shifted(): lax.ppermute(value, axis, [(source, source + steps) for source in range(i...  2.12 us
    dynamic_slice x4, local copies, waits for them, and re-layouts, gather_pieces(): mine = lax.dynamic_slice_in_dim(weight, core * half, half, 0)  2.03 us
  transfers between devices with their start and end apart: 10, of which 5 were waited for; matrix products, arithmetic and copies ran while one was open for 0% of the time, Pallas kernels for 20%

profile of v1, /device:TPU:0, one launch (start us, length us, event | category | flops | bytes accessed | tf_op | source)
XLA Modules:
  0.0 68.3 jit_solution(11570090792277151416)
XLA Ops:
  0.0 0.0 copy-start.1
  0.0 2.0 %constant_dynamic-slice_fusion.1 = bf16[512,512]{1,0:T(8,128)(2,1)} fusion(bf16[1024,512]{1,0:T(8,128)(2,1)} %refs_2_.1, s32[]{:T(128)S(6)} %select_n.20), kind=kLoop, calls=%fused_computation.1 | loop fusion | bytes 1048580 | tf_op jit(solution)/shard_map/dynamic_slice | solution.py:173
  2.0 0.0 copy-start.3
  2.0 3.0 %collective-permute-start.6 = (bf16[512,512]{1,0:T(8,128)(2,1)}, bf16[512,512]{1,0:T(8,128)(2,1)}, u32[]{:S(2)}, u32[]{:S(2)}) collective-permute-start(bf16[512,512]{1,0:T(8,128)(2,1)} %constant_dynamic-slice_fusion.1), channel_id=1, source_target_pairs={{0,1},{1,0},{2,3},{3,2},{4,5},{5,4},{6,7},{7,6},{8,9},{9,8},{10,11... | collective-permute-start | bytes 1572872 | tf_op jit(solution)/shard_map/ppermute | solution.py:174
  4.9 0.0 copy-done.1
  5.0 0.1 collective-permute-start.8
  5.1 0.0 copy-done.3
  5.1 0.0 copy-start.4
  5.1 0.0 copy-start.2
  5.1 2.0 %collective-permute-start.2 = (bf16[384,512]{1,0:T(8,128)(2,1)S(1)}, bf16[384,512]{1,0:T(8,128)(2,1)S(1)}, u32[]{:S(2)}, u32[]{:S(2)}) collective-permute-start(bf16[384,512]{1,0:T(8,128)(2,1)S(1)} %constant_dynamic-slice_fusion.3), channel_id=1, source_target_pairs={{0,1},{1,0},{2,3},{3,2},{4,5},{5,4},{6,7},{7,6},{8,9},{9,8},{10,11... | collective-permute-start | bytes 1179656 | tf_op jit(solution)/shard_map/ppermute | solution.py:174
  7.2 10.8 %collective-permute-done.6.refs_2_ = bf16[512,512]{1,0:T(8,128)(2,1)} collective-permute-done((bf16[512,512]{1,0:T(8,128)(2,1)}, bf16[512,512]{1,0:T(8,128)(2,1)}, u32[]{:S(2)}, u32[]{:S(2)}) %collective-permute-start.6) | collective-permute-done | bytes 524320 | tf_op jit(solution)/shard_map/ppermute | solution.py:174
  18.0 0.0 collective-permute-start.7
  18.0 11.2 %collective-permute-done.8.refs_4_ = bf16[512,512]{1,0:T(8,128)(2,1)} collective-permute-done((bf16[512,512]{1,0:T(8,128)(2,1)S(1)}, bf16[512,512]{1,0:T(8,128)(2,1)}, u32[]{:S(2)}, u32[]{:S(2)}) %collective-permute-start.8) | collective-permute-done | bytes 524320 | tf_op jit(solution)/shard_map/ppermute | solution.py:174
  29.2 0.0 collective-permute-start.9
  29.2 7.5 %collective-permute-done.2.refs_8_ = bf16[384,512]{1,0:T(8,128)(2,1)S(1)} collective-permute-done((bf16[384,512]{1,0:T(8,128)(2,1)S(1)}, bf16[384,512]{1,0:T(8,128)(2,1)S(1)}, u32[]{:S(2)}, u32[]{:S(2)}) %collective-permute-start.2) | collective-permute-done | bytes 393248 | tf_op jit(solution)/shard_map/ppermute | solution.py:174
  36.7 0.0 collective-permute-start.3
  36.7 0.0 copy-done.4
  36.7 1.8 %collective-permute-start.4 = (bf16[128,512]{1,0:T(8,128)(2,1)S(1)}, bf16[128,512]{1,0:T(8,128)(2,1)}, u32[]{:S(2)}, u32[]{:S(2)}) collective-permute-start(bf16[128,512]{1,0:T(8,128)(2,1)S(1)} %constant_dynamic-slice_fusion.2), channel_id=1, source_target_pairs={{0,1},{1,0},{2,3},{3,2},{4,5},{5,4},{6,7},{7,6},{8,9},{9,8},{10,11... | collective-permute-start | bytes 393224 | tf_op jit(solution)/shard_map/ppermute | solution.py:174
  38.6 0.0 copy-start.7
  38.6 0.0 copy-start.11
  38.6 0.0 copy-start.12
  38.6 0.0 copy-done.2
  38.6 0.7 copy-done.7
  39.2 0.0 copy-done.11
  39.2 0.0 copy-done.12
  39.2 1.1 %norm.1 = (bf16[128,512]{1,0:T(8,128)(2,1)S(1)}, bf16[128,512]{1,0:T(8,128)(2,1)}, bf16[512,512]{1,0:T(8,128)(2,1)S(1)}) custom-call(bf16[512,512]{1,0:T(8,128)(2,1)S(1)} %copy-done.2, f32[1,512]{1,0:T(1,128)S(1)} %bitcast.10, s32[1,128]{1,0:T(1,128)S(1)} %bitcast.13, s32[1,128]{1,0:T(1,128)S(1)} %bitcast.14), custom_call_target="tpu_custom_call" | custom-call | tf_op jit(solution)/shard_map/norm/pallas_call | solution.py:191
  40.4 2.1 %collective-permute-start = (bf16[128,512]{1,0:T(8,128)(2,1)S(1)}, bf16[128,512]{1,0:T(8,128)(2,1)S(1)}, u32[]{:S(2)}, u32[]{:S(2)}) collective-permute-start(bf16[128,512]{1,0:T(8,128)(2,1)S(1)} %get-tuple-element.11), channel_id=1, source_target_pairs={{0,8},{8,16},{16,24},{1,9},{9,17},{17,25},{2,10},{10,18},{18,26},{... | collective-permute-start | bytes 393224 | tf_op jit(solution)/shard_map/ppermute | solution.py:24
  42.5 0.3 collective-permute-done.4.refs_11_
  42.8 4.3 %collective-permute-start.1 = (bf16[128,512]{1,0:T(8,128)(2,1)}, bf16[128,512]{1,0:T(8,128)(2,1)}, u32[]{:S(2)}, u32[]{:S(2)}) collective-permute-start(bf16[128,512]{1,0:T(8,128)(2,1)} %get-tuple-element.12), channel_id=1, source_target_pairs={{0,2},{2,4},{4,6},{1,3},{3,5},{5,7},{8,10},{10,12},{12,14},{9,11},... | collective-permute-start | bytes 393224 | tf_op jit(solution)/shard_map/ppermute | solution.py:24
  47.2 0.0 collective-permute-done.halo_x
  47.2 0.0 copy-start.5
  47.2 0.6 copy-done.5
  47.8 0.6 collective-permute-start.5
  48.4 0.0 copy-start.8
  48.4 0.1 pad_add_fusion
  48.5 2.1 %collective-permute-done.1.halo_y = bf16[128,512]{1,0:T(8,128)(2,1)} collective-permute-done((bf16[128,512]{1,0:T(8,128)(2,1)}, bf16[128,512]{1,0:T(8,128)(2,1)}, u32[]{:S(2)}, u32[]{:S(2)}) %collective-permute-start.1) | collective-permute-done | bytes 131104 | tf_op jit(solution)/shard_map/ppermute | solution.py:24
  50.6 0.0 copy-done.8
  50.6 0.0 copy-start.6
  50.6 0.9 %copy-done.6 = bf16[128,512]{1,0:T(8,128)(2,1)S(1)} copy-done((bf16[128,512]{1,0:T(8,128)(2,1)S(1)}, bf16[128,512]{1,0:T(8,128)(2,1)}, u32[]{:S(2)}) %copy-start.6) | copy-done | bytes 131096
  51.5 1.7 %context.2.refs_4_ = bf16[512,512]{1,0:T(8,128)(2,1)S(1)} custom-call(bf16[512,512]{1,0:T(8,128)(2,1)S(1)} %get-tuple-element.10.normed.refs_3_, bf16[128,512]{1,0:T(8,128)(2,1)S(1)} %copy-done.6, bf16[128,512]{1,0:T(8,128)(2,1)} %collective-permute-done.1.halo_y, f32[1,512]{1,0:T(1,128)S(1)} %bitcast.11, s32[4,128]{1,0:T(4,128)S(1)} %copy-done.8), custom_call_target="tpu_custom_call" | custom-call | tf_op jit(solution)/shard_map/context/pallas_call | solution.py:197
  53.2 0.0 collective-permute-done.5.refs_12_
  53.2 0.0 collective-permute-done.3.refs_9_
  53.2 0.0 copy-start.9
  53.2 0.0 copy-start.10
  53.2 0.7 copy-done.9
  53.9 0.0 copy-done.10
  53.9 0.0 copy-start
  53.9 9.1 %attention.1 = (f32[512,512]{1,0:T(8,128)S(1)}, bf16[512,512]{1,0:T(8,128)(2,1)S(1)}) custom-call(s32[4]{0:T(128)S(1)} %copy-done.10, s32[3]{0:T(128)S(1)} %get-tuple-element.15.refs_1_, s32[3]{0:T(128)S(1)} %get-tuple-element.16.refs_2_, bf16[512,512]{1,0:T(8,128)(2,1)S(1)} %get-tuple-element.10.normed.refs_3_, bf16[512,512]{1,0:T(8,128)(2,1)S(1)} %context.2.refs_4_, ...), custom_call_target="tpu_custom_call" | custom-call | tf_op jit(solution)/shard_map/attention/pallas_call | solution.py:202
  63.0 0.0 copy-done
  63.0 1.5 %feed.2.refs_0_ = f32[512,512]{1,0:T(8,128)S(1)} custom-call(f32[512,512]{1,0:T(8,128)S(1)} %get-tuple-element.13.refs_0_, bf16[512,512]{1,0:T(8,128)(2,1)S(1)} %get-tuple-element.14.refs_1_, bf16[1024,512]{1,0:T(8,128)(2,1)S(1)} %copy-done, bf16[1024,512]{1,0:T(8,128)(2,1)S(1)} %copy-done.1), custom_call_target="tpu_custom_call" | custom-call | tf_op jit(solution)/shard_map/feed/pallas_call | solution.py:218
  64.5 0.0 collective-permute-done.7.refs_3_
  64.5 0.0 collective-permute-done.9.refs_5_
  64.5 3.8 %feed.3 = bf16[512,512]{1,0:T(8,128)(2,1)} custom-call(f32[512,512]{1,0:T(8,128)S(1)} %feed.2.refs_0_, bf16[512,512]{1,0:T(8,128)(2,1)S(1)} %get-tuple-element.14.refs_1_, bf16[512,512]{1,0:T(8,128)(2,1)} %collective-permute-done.6.refs_2_, bf16[512,512]{1,0:T(8,128)(2,1)} %collective-permute-done.7.refs_3_, ...), custom_call_target="tpu_custom_call" | custom-call | tf_op jit(solution)/shard_map/feed/pallas_call | solution.py:218
  (3 shorter events, 0.1 us)
Async XLA Ops:
  0.0 4.9 %copy-start.1 = (bf16[1024,512]{1,0:T(8,128)(2,1)S(1)}, bf16[1024,512]{1,0:T(8,128)(2,1)}, u32[]{:S(2)}) copy-start(bf16[1024,512]{1,0:T(8,128)(2,1)} %refs_3_.1) | copy-start | bytes 3145732
  2.0 3.1 %copy-start.3 = (bf16[768,512]{1,0:T(8,128)(2,1)S(1)}, bf16[768,512]{1,0:T(8,128)(2,1)}, u32[]{:S(2)}) copy-start(bf16[768,512]{1,0:T(8,128)(2,1)} %refs_7_.1) | copy-start | bytes 2359300
  2.0 16.0 %collective-permute-start.6 = (bf16[512,512]{1,0:T(8,128)(2,1)}, bf16[512,512]{1,0:T(8,128)(2,1)}, u32[]{:S(2)}, u32[]{:S(2)}) collective-permute-start(bf16[512,512]{1,0:T(8,128)(2,1)} %constant_dynamic-slice_fusion.1), channel_id=1, source_target_pairs={{0,1},{1,0},{2,3},{3,2},{4,5},{5,4},{6,7},{7,6},{8,9},{9,8},{10,11... | collective-permute-start | bytes 1572872 | tf_op jit(solution)/shard_map/ppermute | solution.py:174
  5.0 24.3 %collective-permute-start.8 = (bf16[512,512]{1,0:T(8,128)(2,1)S(1)}, bf16[512,512]{1,0:T(8,128)(2,1)}, u32[]{:S(2)}, u32[]{:S(2)}) collective-permute-start(bf16[512,512]{1,0:T(8,128)(2,1)S(1)} %constant_dynamic-slice_fusion), channel_id=1, source_target_pairs={{0,1},{1,0},{2,3},{3,2},{4,5},{5,4},{6,7},{7,6},{8,9},{9,8},{10,11... | collective-permute-start | bytes 1572872 | tf_op jit(solution)/shard_map/ppermute | solution.py:174
  5.1 31.7 %copy-start.4 = (bf16[256,512]{1,0:T(8,128)(2,1)S(1)}, bf16[256,512]{1,0:T(8,128)(2,1)}, u32[]{:S(2)}) copy-start(bf16[256,512]{1,0:T(8,128)(2,1)} %refs_10_.1) | copy-start | bytes 786436
  5.1 33.5 %copy-start.2 = (bf16[512,512]{1,0:T(8,128)(2,1)S(1)}, bf16[512,512]{1,0:T(8,128)(2,1)}, u32[]{:S(2)}) copy-start(bf16[512,512]{1,0:T(8,128)(2,1)} %refs_5_.1) | copy-start | bytes 1572868
  5.1 31.6 %collective-permute-start.2 = (bf16[384,512]{1,0:T(8,128)(2,1)S(1)}, bf16[384,512]{1,0:T(8,128)(2,1)S(1)}, u32[]{:S(2)}, u32[]{:S(2)}) collective-permute-start(bf16[384,512]{1,0:T(8,128)(2,1)S(1)} %constant_dynamic-slice_fusion.3), channel_id=1, source_target_pairs={{0,1},{1,0},{2,3},{3,2},{4,5},{5,4},{6,7},{7,6},{8,9},{9,8},{10,11... | collective-permute-start | bytes 1179656 | tf_op jit(solution)/shard_map/ppermute | solution.py:174
  18.0 46.5 %collective-permute-start.7 = (bf16[512,512]{1,0:T(8,128)(2,1)}, bf16[512,512]{1,0:T(8,128)(2,1)}, u32[]{:S(2)}, u32[]{:S(2)}) collective-permute-start(bf16[512,512]{1,0:T(8,128)(2,1)} %collective-permute-done.6.refs_2_), channel_id=1, source_target_pairs={{0,8},{8,0},{16,24},{24,16},{1,9},{9,1},{17,25},{25,17},{2,10},{10... | collective-permute-start | bytes 1572872 | tf_op jit(solution)/shard_map/ppermute | solution.py:175
  29.2 35.3 %collective-permute-start.9 = (bf16[512,512]{1,0:T(8,128)(2,1)}, bf16[512,512]{1,0:T(8,128)(2,1)}, u32[]{:S(2)}, u32[]{:S(2)}) collective-permute-start(bf16[512,512]{1,0:T(8,128)(2,1)} %collective-permute-done.8.refs_4_), channel_id=1, source_target_pairs={{0,8},{8,0},{16,24},{24,16},{1,9},{9,1},{17,25},{25,17},{2,10},{10... | collective-permute-start | bytes 1572872 | tf_op jit(solution)/shard_map/ppermute | solution.py:175
  36.7 16.5 %collective-permute-start.3 = (bf16[384,512]{1,0:T(8,128)(2,1)S(1)}, bf16[384,512]{1,0:T(8,128)(2,1)}, u32[]{:S(2)}, u32[]{:S(2)}) collective-permute-start(bf16[384,512]{1,0:T(8,128)(2,1)S(1)} %collective-permute-done.2.refs_8_), channel_id=1, source_target_pairs={{0,8},{8,0},{16,24},{24,16},{1,9},{9,1},{17,25},{25,17},{2,10},{10... | collective-permute-start | bytes 1179656 | tf_op jit(solution)/shard_map/ppermute | solution.py:175
  36.7 6.1 %collective-permute-start.4 = (bf16[128,512]{1,0:T(8,128)(2,1)S(1)}, bf16[128,512]{1,0:T(8,128)(2,1)}, u32[]{:S(2)}, u32[]{:S(2)}) collective-permute-start(bf16[128,512]{1,0:T(8,128)(2,1)S(1)} %constant_dynamic-slice_fusion.2), channel_id=1, source_target_pairs={{0,1},{1,0},{2,3},{3,2},{4,5},{5,4},{6,7},{7,6},{8,9},{9,8},{10,11... | collective-permute-start | bytes 393224 | tf_op jit(solution)/shard_map/ppermute | solution.py:174
  38.6 0.7 copy-start.7
  38.6 0.7 copy-start.11
  38.6 0.7 copy-start.12
  40.4 6.8 %collective-permute-start = (bf16[128,512]{1,0:T(8,128)(2,1)S(1)}, bf16[128,512]{1,0:T(8,128)(2,1)S(1)}, u32[]{:S(2)}, u32[]{:S(2)}) collective-permute-start(bf16[128,512]{1,0:T(8,128)(2,1)S(1)} %get-tuple-element.11), channel_id=1, source_target_pairs={{0,8},{8,16},{16,24},{1,9},{9,17},{17,25},{2,10},{10,18},{18,26},{... | collective-permute-start | bytes 393224 | tf_op jit(solution)/shard_map/ppermute | solution.py:24
  42.8 7.8 %collective-permute-start.1 = (bf16[128,512]{1,0:T(8,128)(2,1)}, bf16[128,512]{1,0:T(8,128)(2,1)}, u32[]{:S(2)}, u32[]{:S(2)}) collective-permute-start(bf16[128,512]{1,0:T(8,128)(2,1)} %get-tuple-element.12), channel_id=1, source_target_pairs={{0,2},{2,4},{4,6},{1,3},{3,5},{5,7},{8,10},{10,12},{12,14},{9,11},... | collective-permute-start | bytes 393224 | tf_op jit(solution)/shard_map/ppermute | solution.py:24
  47.2 0.7 copy-start.5
  47.8 5.4 %collective-permute-start.5 = (bf16[128,512]{1,0:T(8,128)(2,1)}, bf16[128,512]{1,0:T(8,128)(2,1)}, u32[]{:S(2)}, u32[]{:S(2)}) collective-permute-start(bf16[128,512]{1,0:T(8,128)(2,1)} %collective-permute-done.4.refs_11_), channel_id=1, source_target_pairs={{0,8},{8,0},{16,24},{24,16},{1,9},{9,1},{17,25},{25,17},{2,10},{10... | collective-permute-start | bytes 393224 | tf_op jit(solution)/shard_map/ppermute | solution.py:175
  48.4 2.2 %copy-start.8 = (s32[4,128]{1,0:T(4,128)S(1)}, s32[4,128]{1,0:T(4,128)}, u32[]{:S(2)}) copy-start(s32[4,128]{1,0:T(4,128)} %context.3) | copy-start | bytes 6148
  50.6 0.9 %copy-start.6 = (bf16[128,512]{1,0:T(8,128)(2,1)S(1)}, bf16[128,512]{1,0:T(8,128)(2,1)}, u32[]{:S(2)}) copy-start(bf16[128,512]{1,0:T(8,128)(2,1)} %copy-done.5) | copy-start | bytes 393220
  53.2 0.7 %copy-start.9 = (f32[512]{0:T(512)S(1)}, f32[512]{0:T(512)}, u32[]{:S(2)}) copy-start(f32[512]{0:T(512)} %param.13) | copy-start | bytes 6148
  53.2 0.7 copy-start.10
  53.9 9.1 %copy-start = (bf16[1024,512]{1,0:T(8,128)(2,1)S(1)}, bf16[1024,512]{1,0:T(8,128)(2,1)}, u32[]{:S(2)}) copy-start(bf16[1024,512]{1,0:T(8,128)(2,1)} %refs_2_.1) | copy-start | bytes 3145732

commit v2 on v1

v2 whole, which is shorter than its diff:
```python
import typing

import jax
import jax.numpy as jnp
from jax import lax
from jax.experimental import pallas as pl
from jax.experimental.pallas import tpu as pltpu
from jax.sharding import PartitionSpec as P

HEADS = 16
WIN = 128
CTX = 128
LANES = 128
EPSILON = 1e-05
LOG2E = 1.4426950408889634

VMEM = pl.BlockSpec(memory_space=pltpu.VMEM)
SMEM = pl.BlockSpec(memory_space=pltpu.SMEM)
HBM = pl.BlockSpec(memory_space=pltpu.HBM)
PARAMS = pltpu.CompilerParams(vmem_limit_bytes=16 * 1024 * 1024)


def ring(value, axis):
    count = lax.axis_size(axis)
    return lax.ppermute(value, axis, [(source, (source + 1) % count) for source in range(count)])


def swap(value, axis, bit):
    count = lax.axis_size(axis)
    return lax.ppermute(value, axis, [(source, source ^ bit) for source in range(count)])


def dot_nt(left, right):
    return lax.dot_general(left, right, (((1,), (1,)), ((), ())), preferred_element_type=jnp.float32)


def dot_nn(left, right):
    return jnp.dot(left, right, preferred_element_type=jnp.float32)


def layer_norm(values, gain):
    values = values.astype(jnp.float32)
    center = values - jnp.mean(values, axis=-1, keepdims=True)
    spread = jnp.mean(center * center, axis=-1, keepdims=True)
    return (center * lax.rsqrt(spread + EPSILON) * gain).astype(jnp.bfloat16)


def pick_rows(indices, count):
    column = jnp.broadcast_to(indices.astype(jnp.float32), (LANES, LANES)).T
    lane = lax.broadcasted_iota(jnp.int32, (LANES, LANES), 1).astype(jnp.float32)
    blocks = [
        jnp.where(column == lane + float(first), 1.0, 0.0).astype(jnp.bfloat16)
        for first in range(0, count, LANES)
    ]
    return jnp.concatenate(blocks, axis=1)


def norm_kernel(tokens, gain, send_x, send_y, out_x, out_y, normed):
    rows = tokens.shape[0]
    block = tokens[...]
    out_x[...] = dot_nn(pick_rows(send_x[...], rows), block).astype(jnp.bfloat16)
    out_y[...] = dot_nn(pick_rows(send_y[...], rows), block).astype(jnp.bfloat16)
    normed[...] = layer_norm(block, gain[...])


def present(halo, axis):
    return jnp.where(lax.axis_index(axis) > 0, halo[...].astype(jnp.float32), 0.0)


def context_kernel(lengths, normed, halo_x, halo_y, gain, context, chosen, filled):
    parts = [layer_norm(present(halo_x, "gx"), gain[...]), layer_norm(present(halo_y, "gy"), gain[...])]
    pool = jnp.concatenate([normed[...]] + parts, axis=0)
    for window in range(context.shape[0]):
        picked = dot_nn(pick_rows(context[pl.ds(window, 1), :], pool.shape[0]), pool)
        chosen[pl.ds(window * CTX, CTX), :] = picked.astype(jnp.bfloat16)
        filled[pl.ds(window, 1), :] = jnp.full((1, LANES), lengths[window], jnp.int32)


class Share(typing.NamedTuple):
    base: int
    axis: str
    stride: int
    rows: int

    def start(self, flip):
        core = lax.axis_index("gx") % 2
        index = {
            "core": lambda: core,
            "gx": lambda: lax.axis_index("gx"),
            "gy": lambda: (lax.axis_index("gy") % 2) * 2 + core,
        }[self.axis]()
        return self.base + (index ^ flip) * self.stride


def slice_kernel(shares, *refs):
    count = len(shares)
    shards, parts, sems = refs[:count], refs[count : 2 * count], refs[2 * count]
    copies = []
    for number, share in enumerate(shares):
        start = pl.multiple_of(share.start(0), 32)
        copies.append(
            pltpu.make_async_copy(shards[number].at[pl.ds(start, share.rows), :], parts[number], sems.at[number])
        )
    for copy in copies:
        copy.start()
    for copy in copies:
        copy.wait()


def prepare_kernel(shares, *refs):
    count = len(shares)
    sources, shards, refs = refs[:4], refs[4 : 4 + count], refs[4 + count :]
    (held, out_x, out_y, normed), parts, scratch, sems = refs[:4], refs[4 : 4 + count], refs[4 + count : -1], refs[-1]
    copies = []
    for source, target in zip(sources, (held, *scratch)):
        copies.append(pltpu.make_async_copy(source, target, sems.at[len(copies)]))
    for number, share in enumerate(shares):
        start = pl.multiple_of(share.start(0), 32)
        copies.append(
            pltpu.make_async_copy(shards[number].at[pl.ds(start, share.rows), :], parts[number], sems.at[len(copies)])
        )
    for copy in copies:
        copy.start()
    for copy in copies[:4]:
        copy.wait()
    norm_kernel(held, *scratch, out_x, out_y, normed)
    for copy in copies[4:]:
        copy.wait()


def assemble(whole, own, pieces):
    if not pieces:
        whole[...] = own[...]
        return
    rank = lax.axis_index("fsdp")
    rows = own.shape[0]
    whole[pl.ds(pl.multiple_of(rank * rows, rows), rows), :] = own[...]
    for share, flip, value in pieces:
        start = pl.multiple_of((1 - rank) * rows + share.start(flip), 32)
        whole[pl.ds(start, share.rows), :] = value[...]


def project_kernel(plan, normed, chosen, shard, *refs):
    pieces = refs[: len(plan)]
    queries, own_keys, ctx_keys, own_values, ctx_values, w_qkv = refs[len(plan) :]
    width = normed.shape[1]
    assemble(w_qkv, shard, [(*where, piece) for where, piece in zip(plan, pieces)])
    own, ctx = normed[...], chosen[...]
    w_q, w_k, w_v = (w_qkv[pl.ds(part * width, width), :] for part in range(3))
    queries[...] = dot_nt(w_q, own).astype(jnp.bfloat16)
    own_keys[...] = dot_nt(own, w_k).astype(jnp.bfloat16)
    ctx_keys[...] = dot_nt(ctx, w_k).astype(jnp.bfloat16)
    own_values[...] = dot_nt(w_v, own).astype(jnp.bfloat16)
    ctx_values[...] = dot_nt(w_v, ctx).astype(jnp.bfloat16)


def attend_kernel(windows, filled, queries, own_keys, ctx_keys, own_values, ctx_values, mixed):
    width = queries.shape[0]
    head_size = width // HEADS
    group = LANES // head_size
    scale = head_size ** (-0.5) * LOG2E
    for window in windows:
        low, high = window * WIN, (window + 1) * WIN
        base = low - windows[0] * WIN
        length = filled[window : window + 1, :]
        row_full = lax.broadcasted_iota(jnp.int32, (WIN, LANES), 0) < length
        row_full = jnp.concatenate([row_full] * (width // LANES), axis=1)
        keys = jnp.concatenate(
            [
                jnp.where(row_full, own_keys[low:high, :], ctx_keys[low : low + 1, :]),
                ctx_keys[low:high, :],
            ],
            axis=0,
        )
        slot_full = lax.broadcasted_iota(jnp.int32, (1, WIN), 1) < length
        values = jnp.concatenate(
            [
                jnp.where(slot_full, own_values[:, low:high], jnp.zeros((), jnp.bfloat16)),
                ctx_values[:, low:high],
            ],
            axis=1,
        )
        slots = lax.broadcasted_iota(jnp.int32, (16, WIN), 1) < length
        ones = jnp.concatenate([jnp.where(slots, 1.0, 0.0), jnp.ones((16, CTX), jnp.float32)], axis=1).astype(jnp.bfloat16)
        for first in range(0, width, LANES):
            group_queries = queries[first : first + LANES, low:high]
            parts = []
            for head in range(group):
                pad = [jnp.zeros((head_size, WIN), jnp.bfloat16)] * group
                pad[head] = group_queries[head * head_size : (head + 1) * head_size]
                parts.append(jnp.concatenate(pad, axis=0))
            scores = dot_nn(keys[:, first : first + LANES], jnp.concatenate(parts, axis=1))
            largest = jnp.max(scores, axis=0, keepdims=True)
            probs = jnp.exp2((scores - largest) * scale).astype(jnp.bfloat16)
            outs = []
            for head in range(0, group, 2):
                top = first + head * head_size
                weights = jnp.concatenate([values[top : top + 2 * head_size], ones], axis=0)
                sums = dot_nn(weights, probs[:, head * WIN : (head + 2) * WIN])
                for part in range(2):
                    block = sums[:, part * WIN : (part + 1) * WIN]
                    outs.append(
                        block[part * head_size : (part + 1) * head_size]
                        * (1.0 / block[2 * head_size : 2 * head_size + 1])
                    )
            mixed[base : base + WIN, first : first + LANES] = (
                jnp.concatenate(outs, axis=0).T.astype(jnp.bfloat16)
            )


def finish_kernel(parts, plan, tokens, gain, shard, *refs):
    mixed, pieces = refs[:parts], refs[parts : parts + len(plan)]
    middle, second, w_out = refs[parts + len(plan) :]
    assemble(w_out, shard, [(*where, piece) for where, piece in zip(plan, pieces)])
    low = 0
    for block in mixed:
        rows = slice(low, low + block.shape[0])
        total = tokens[rows, :].astype(jnp.float32) + dot_nt(block[...], w_out[...])
        middle[rows, :] = total
        second[rows, :] = layer_norm(total, gain[...])
        low += block.shape[0]


def columns_of(plan, number, piece):
    if not plan:
        return slice(None)
    share, flip = plan[number]
    return pl.ds(pl.multiple_of(share.start(flip), LANES), share.rows)


def hidden_kernel(plan, second, *refs):
    hidden = refs[-1]
    for number, piece in enumerate(refs[:-1]):
        units = jax.nn.gelu(dot_nt(second[...], piece[...])).astype(jnp.bfloat16)
        hidden[:, columns_of(plan, number, piece)] = units


def down_kernel(plan, start, hidden, *refs):
    output = refs[-1]
    total = start[...]
    for number, piece in enumerate(refs[:-1]):
        total = total + dot_nn(hidden[:, columns_of(plan, number, piece)], piece[...])
    output[...] = total.astype(output.dtype)


def last_kernel(plan, start, hidden, *refs):
    pieces, output, held, sems = refs[: len(plan)], refs[-3], refs[-2], refs[-1]
    blocks = start.shape[0] // WIN
    copies = []
    for block in range(blocks):
        rows = slice(block * WIN, (block + 1) * WIN)
        total = start[rows, :]
        for number, piece in enumerate(pieces):
            total = total + dot_nn(hidden[rows, columns_of(plan, number, piece)], piece[...])
        held[rows, :] = total.astype(output.dtype)
        copies.append(pltpu.make_async_copy(held.at[rows, :], output.at[rows, :], sems.at[block]))
        copies[-1].start()
    for copy in copies:
        copy.wait()


COSTS = {"norm": 1, "slices": 1, "prepare": 1, "context": 1, "project": 1, "attend": 1, "finish": 1, "hidden": 1, "down": 1}


def call(kernel, outs, operands, name, scratch=(), specs=None, result=VMEM):
    specs = specs or [VMEM] * len(operands)
    placed = [
        pltpu.with_memory_space_constraint(operand, pltpu.HBM) if spec is HBM else operand
        for operand, spec in zip(operands, specs)
    ]
    if result is VMEM:
        outs = [pltpu.VMEM(out.shape, out.dtype) for out in outs]
    return pl.pallas_call(
        kernel,
        out_shape=tuple(outs),
        in_specs=specs,
        out_specs=tuple(result or VMEM for _ in outs),
        scratch_shapes=list(scratch),
        compiler_params=PARAMS,
        name=name,
        cost_estimate=pl.CostEstimate(flops=COSTS[name] * 10**7, bytes_accessed=0, transcendentals=0),
    )(*placed)


def struct(rows, width, dtype=jnp.bfloat16):
    return jax.ShapeDtypeStruct((rows, width), dtype)


def body(tokens, gain_one, gain_two, w_qkv, w_out, w_in, w_down, send_x, send_y, context, lengths):
    rows, width = tokens.shape
    halo = send_x.shape[0]
    gain_one, gain_two = gain_one[None, :], gain_two[None, :]
    send_x, send_y = send_x[None, :], send_y[None, :]
    after = lax.optimization_barrier
    paired = lax.axis_size("fsdp") == 2 and lax.axis_size("gx") == 4 and lax.axis_size("gy") % 2 == 0
    edges = [struct(halo, width), struct(halo, width), struct(rows, width)]

    if not paired:
        qkv, out, into, down = (
            lax.all_gather(weight, "fsdp", axis=0, tiled=True) for weight in (w_qkv, w_out, w_in, w_down)
        )
        out_x, out_y, normed = call(norm_kernel, edges, (tokens, gain_one, send_x, send_y), "norm")
    else:
        qkv, out, into, down = w_qkv, w_out, w_in, w_down
        size = qkv.shape[0] // 4
        share_qkv = [Share(chunk * size, "core", 2 * size, size) for chunk in range(2)]
        share_out = Share(0, "core", out.shape[0] // 2, out.shape[0] // 2)
        share_in = Share(0, "gy", into.shape[0] // 4, into.shape[0] // 4)
        size = down.shape[0] // 8
        share_early = Share(0, "gx", size, size)
        share_late = Share(4 * size, "core", 2 * size, 2 * size)
        tokens, out_x, out_y, normed, *parts_qkv = call(
            lambda *refs: prepare_kernel(share_qkv, *refs),
            [struct(rows, width)] + edges + [struct(share.rows, width) for share in share_qkv],
            (tokens, gain_one, send_x, send_y, qkv, qkv), "prepare",
            [
                pltpu.VMEM(gain_one.shape, gain_one.dtype), pltpu.VMEM(send_x.shape, send_x.dtype),
                pltpu.VMEM(send_y.shape, send_y.dtype), pltpu.SemaphoreType.DMA((6,)),
            ],
            [HBM] * 6,
        )
        y_qkv = [swap(part, "fsdp", 1) for part in parts_qkv]
        shares = [share_in, share_out, share_early, share_late]
        later, normed = after(((w_in, w_out, w_down), normed))
        parts = call(
            lambda *refs: slice_kernel(shares, *refs), [struct(share.rows, width) for share in shares],
            (later[0], later[1], later[2], later[2]), "slices", [pltpu.SemaphoreType.DMA((4,))], [HBM] * 4,
        )
        y_in, y_out, y_early, y_late = (swap(part, "fsdp", 1) for part in parts)

    def crossed(share, near, flip=0):
        return [(share, flip, near), (share, flip + 1, swap(near, "gx", 1))]

    def arrays(pieces):
        return [piece[2] for piece in pieces]

    def plan(pieces):
        return [piece[:2] for piece in pieces]

    halo_x = ring(out_x, "gx")
    halo_y = ring(out_y, "gy")
    if paired:
        y_qkv[1], halo_x, halo_y = after((y_qkv[1], halo_x, halo_y))
    chosen, filled = call(
        context_kernel, [struct(rows, width), struct(*context.shape, jnp.int32)],
        (lengths, normed, halo_x, halo_y, gain_one, context), "context", specs=[SMEM] + [VMEM] * 5,
    )
    pieces = []
    if paired:
        for share, piece in zip(share_qkv, y_qkv):
            pieces += crossed(share, piece)
    projected = call(
        lambda *refs, plan=plan(pieces): project_kernel(plan, *refs), [struct(rows, width)] * 5,
        (normed, chosen, qkv, *arrays(pieces)), "project", [pltpu.VMEM((3 * width, width), jnp.bfloat16)],
    )

    def attend(windows):
        return call(
            lambda *refs: attend_kernel(windows, *refs), [struct(len(windows) * WIN, width)],
            (filled, *projected), "attend",
        )

    windows = list(range(rows // WIN))
    half = len(windows) // 2
    mixed = attend(windows[:half])
    pieces_out, pieces_in, pieces_down, pieces_last = [], [], [], []
    if paired:
        y_in, mixed = after((y_in, mixed))
        z_in = swap(y_in, "gy", 1)
        projected, y_in = after((projected, y_in))
    mixed += attend(windows[half:])
    if paired:
        y_out, y_early, mixed = after((y_out, y_early, mixed))
        pieces_out = crossed(share_out, y_out)
        x_early = swap(y_early, "gx", 2)
    middle, second = call(
        lambda *refs: finish_kernel(len(mixed), plan(pieces_out), *refs),
        [struct(rows, width, jnp.float32), struct(rows, width)], (tokens, gain_two, out, *mixed, *arrays(pieces_out)),
        "finish", [pltpu.VMEM((width, width), jnp.bfloat16)],
    )

    def expand(own, pieces):
        (hidden,) = call(
            lambda *refs: hidden_kernel(plan(pieces), *refs), [struct(rows, into.shape[0])],
            (second, *(arrays(pieces) or [own])), "hidden",
        )
        return hidden

    if not paired:
        return call(
            lambda *refs: down_kernel([], *refs), [struct(rows, width)],
            (middle, expand(into, []), down), "down", result=None,
        )[0]
    (total,) = call(
        lambda *refs: down_kernel([], *refs), [struct(rows, width, jnp.float32)],
        (middle, expand(into, []), down), "down",
    )
    z_in, x_early, y_late, total = after((z_in, x_early, y_late, total))
    pieces = crossed(share_in, y_in) + crossed(share_in, z_in, 2)
    pieces_down = crossed(share_early, y_early) + crossed(share_early, x_early, 2) + crossed(share_late, y_late)
    hidden = expand(None, pieces)
    return call(
        lambda *refs: last_kernel(plan(pieces_down), *refs), [struct(rows, width)],
        (total, hidden, *arrays(pieces_down)), "down",
        [pltpu.VMEM((rows, width), jnp.bfloat16), pltpu.SemaphoreType.DMA((rows // WIN,))], result=HBM,
    )[0]


def solution(mesh):
    in_specs = (
        P(("gx", "gy", "fsdp"), None),
        P(),
        P(),
        P("fsdp", None),
        P("fsdp", None),
        P("fsdp", None),
        P("fsdp", None),
        P(("gx", "gy", "fsdp")),
        P(("gx", "gy", "fsdp")),
        P(("gx", "gy", "fsdp"), None),
        P(("gx", "gy", "fsdp")),
    )
    out_specs = P(("gx", "gy", "fsdp"), None)
    return jax.shard_map(body, mesh=mesh, in_specs=in_specs, out_specs=out_specs, check_vma=False)
```

time: 68.6 us -> 39.4 us (0.57)
  waiting for transfers between devices: 32 us -> 6.33 us
  local copies, waits for them, and re-layouts: 4.97 us -> 0.18 us
  starting transfers between devices: 13.9 us -> 16 us
  Pallas kernels: 17.2 us -> 16.5 us
    ppermute x10 -> x18, waiting for transfers between devices: 32 us -> 6.33 us  [the longest x16 3.7 us: swap(): lax.ppermute(value, axis, [(source, source ^ bit) for source in range(cou...]
    unnamed x26 -> x16, local copies, waits for them, and re-layouts: 2.93 us -> 0.18 us
    ppermute x10 -> x18, starting transfers between devices: 13.9 us -> 16 us  [the longest x16 14 us: swap(): lax.ppermute(value, axis, [(source, source ^ bit) for source in range(cou...]
    dynamic_slice x4 -> x0, local copies, waits for them, and re-layouts: 2.03 us -> none  [gather_pieces(): mine = lax.dynamic_slice_in_dim(weight, core * half, half, 0)]
    pallas_call x5 -> x11, Pallas kernels: 17.2 us -> 16.5 us  [call(): pl.pallas_call(kernel, out_shape=tuple(outs), in_specs=specs, out_specs=t...]
  transfers between devices with their start and end apart: 10 -> 18, of which waited for: 5 -> 4; matrix products, arithmetic and copies ran while one was open for 0% -> 0% of each run, Pallas kernels for 20% -> 34%
where the time goes in v2:
time: 39.4 us; the launch traced here: 39.2 us
  Pallas kernels  16.5 us (42%)
  starting transfers between devices  16 us (41%)
  waiting for transfers between devices  6.33 us (16%)
    pallas_call x11, Pallas kernels, call(): pl.pallas_call(kernel, out_shape=tuple(outs), in_specs=specs, out_specs=t...  16.5 us
    ppermute x16, starting transfers between devices, swap(): lax.ppermute(value, axis, [(source, source ^ bit) for source in range(cou...  14 us
    ppermute x16, waiting for transfers between devices, swap(): lax.ppermute(value, axis, [(source, source ^ bit) for source in range(cou...  3.7 us
    ppermute x2, waiting for transfers between devices, ring(): lax.ppermute(value, axis, [(source, (source + 1) % count) for source in r...  2.63 us
    ppermute x2, starting transfers between devices, ring(): lax.ppermute(value, axis, [(source, (source + 1) % count) for source in r...  2.01 us
  transfers between devices with their start and end apart: 18, of which 4 were waited for; matrix products, arithmetic and copies ran while one was open for 0% of the time, Pallas kernels for 34%

profile of v2, /device:TPU:0, one launch (start us, length us, event | category | flops | bytes accessed | tf_op | source)
XLA Modules:
  0.0 39.2 jit_solution(7779300368025023233)
XLA Ops:
  0.0 1.6 %prepare.1 = (bf16[512,512]{1,0:T(8,128)(2,1)S(1)}, bf16[128,512]{1,0:T(8,128)(2,1)S(1)}, bf16[128,512]{1,0:T(8,128)(2,1)S(1)}, bf16[512,512]{1,0:T(8,128)(2,1)S...) custom-call(bf16[512,512]{1,0:T(8,128)(2,1)} %refs_0_.1, f32[1,512]{1,0:T(1,128)} %bitcast.4, ...), custom_call_target="tpu_custom_call" | custom-call | flops 10000000 | tf_op jit(solution)/shard_map/prepare/pallas_call | solution.py:273
  1.6 3.0 %collective-permute-start.1 = (bf16[192,512]{1,0:T(8,128)(2,1)S(1)}, bf16[192,512]{1,0:T(8,128)(2,1)S(1)}, u32[]{:S(2)}, u32[]{:S(2)}) collective-permute-start(bf16[192,512]{1,0:T(8,128)(2,1)S(1)} %get-tuple-element.53), channel_id=1, source_target_pairs={{0,1},{1,0},{2,3},{3,2},{4,5},{5,4},{6,7},{7,6},{8,9},{9,8},{10,11... | collective-permute-start | bytes 589832 | tf_op jit(solution)/shard_map/ppermute | solution.py:30
  4.6 0.1 collective-permute-start.4
  4.7 0.0 collective-permute-start.2
  4.7 2.0 %collective-permute-start.3 = (bf16[128,512]{1,0:T(8,128)(2,1)S(1)}, bf16[128,512]{1,0:T(8,128)(2,1)S(1)}, u32[]{:S(2)}, u32[]{:S(2)}) collective-permute-start(bf16[128,512]{1,0:T(8,128)(2,1)S(1)} %get-tuple-element.55), channel_id=1, source_target_pairs={{0,2},{2,4},{4,6},{6,0},{1,3},{3,5},{5,7},{7,1},{8,10},{10,12},{12... | collective-permute-start | bytes 393224 | tf_op jit(solution)/shard_map/ppermute | solution.py:25
  6.7 0.0 copy-start.4
  6.7 0.0 copy-start.5
  6.7 0.0 copy-start.7
  6.7 1.2 %slices.1 = (bf16[256,512]{1,0:T(8,128)(2,1)S(1)}, bf16[128,512]{1,0:T(8,128)(2,1)S(1)}, bf16[128,512]{1,0:T(8,128)(2,1)S(1)}, bf16[256,512]{1,0:T(8,128)(2,1)S(1)}) custom-call(bf16[1024,512]{1,0:T(8,128)(2,1)} %refs_1_.2, bf16[256,512]{1,0:T(8,128)(2,1)} %refs_2_.5, bf16[1024,512]{1,0:T(8,128)(2,1)} %refs_2_.6, bf16[1024,512]{1,0:T(8,128)(2,1)} %refs_2_.6), custom_call_target="tpu_custom_call" | custom-call | flops 10000000 | tf_op jit(solution)/shard_map/slices/pallas_call | solution.py:273
  7.9 0.0 copy-start.1
  8.0 1.6 %collective-permute-start = (bf16[256,512]{1,0:T(8,128)(2,1)S(1)}, bf16[256,512]{1,0:T(8,128)(2,1)S(1)}, u32[]{:S(2)}, u32[]{:S(2)}) collective-permute-start(bf16[256,512]{1,0:T(8,128)(2,1)S(1)} %get-tuple-element.51), channel_id=1, source_target_pairs={{0,1},{1,0},{2,3},{3,2},{4,5},{5,4},{6,7},{7,6},{8,9},{9,8},{10,11... | collective-permute-start | bytes 786440 | tf_op jit(solution)/shard_map/ppermute | solution.py:30
  9.5 0.0 collective-permute-done.2.halo_x
  9.5 2.6 %collective-permute-done.3.halo_y = bf16[128,512]{1,0:T(8,128)(2,1)S(1)} collective-permute-done((bf16[128,512]{1,0:T(8,128)(2,1)S(1)}, bf16[128,512]{1,0:T(8,128)(2,1)S(1)}, u32[]{:S(2)}, u32[]{:S(2)}) %collective-permute-start.3) | collective-permute-done | bytes 131104 | tf_op jit(solution)/shard_map/ppermute | solution.py:25
  12.2 0.0 collective-permute-done.1.refs_5_
  12.2 0.7 %collective-permute-start.6 = (bf16[192,512]{1,0:T(8,128)(2,1)S(1)}, bf16[192,512]{1,0:T(8,128)(2,1)S(1)}, u32[]{:S(2)}, u32[]{:S(2)}) collective-permute-start(bf16[192,512]{1,0:T(8,128)(2,1)S(1)} %collective-permute-done.1.refs_5_), channel_id=1, source_target_pairs={{0,8},{8,0},{16,24},{24,16},{1,9},{9,1},{17,25},{25,17},{2,10},{10... | collective-permute-start | bytes 589832 | tf_op jit(solution)/shard_map/ppermute | solution.py:30
  12.9 1.7 %collective-permute-done.4.refs_3_ = bf16[192,512]{1,0:T(8,128)(2,1)S(1)} collective-permute-done((bf16[192,512]{1,0:T(8,128)(2,1)S(1)}, bf16[192,512]{1,0:T(8,128)(2,1)S(1)}, u32[]{:S(2)}, u32[]{:S(2)}) %collective-permute-start.4) | collective-permute-done | bytes 196640 | tf_op jit(solution)/shard_map/ppermute | solution.py:30
  14.6 0.0 collective-permute-start.5
  14.6 2.1 %collective-permute-start.8 = (bf16[128,512]{1,0:T(8,128)(2,1)S(1)}, bf16[128,512]{1,0:T(8,128)(2,1)S(1)}, u32[]{:S(2)}, u32[]{:S(2)}) collective-permute-start(bf16[128,512]{1,0:T(8,128)(2,1)S(1)} %get-tuple-element.68), channel_id=1, source_target_pairs={{0,1},{1,0},{2,3},{3,2},{4,5},{5,4},{6,7},{7,6},{8,9},{9,8},{10,11... | collective-permute-start | bytes 393224 | tf_op jit(solution)/shard_map/ppermute | solution.py:30
  16.6 0.0 collective-permute-start.9
  16.7 0.0 copy-done.4
  16.7 0.0 copy-done.5
  16.7 0.0 copy-done.7
  16.7 1.3 %context.2 = (bf16[512,512]{1,0:T(8,128)(2,1)S(1)}, s32[4,128]{1,0:T(4,128)S(1)}) custom-call(s32[4]{0:T(128)S(1)} %copy-done.7, bf16[512,512]{1,0:T(8,128)(2,1)S(1)} %get-tuple-element.52.normed.refs_0_, bf16[128,512]{1,0:T(8,128)(2,1)S(1)} %collective-permute-done.2.halo_x, bf16[128,512]{1,0:T(8,128)(2,1)S(1)} %collective-permute-done.3.halo_y, ...), custom_call_target="tpu_custom_call" | custom-call | flops 10000000 | tf_op jit(solution)/shard_map/context/pallas_call | solution.py:273
  18.0 0.0 collective-permute-done.6.refs_6_
  18.0 2.0 %collective-permute-start.11 = (bf16[256,512]{1,0:T(8,128)(2,1)S(1)}, bf16[256,512]{1,0:T(8,128)(2,1)S(1)}, u32[]{:S(2)}, u32[]{:S(2)}) collective-permute-start(bf16[256,512]{1,0:T(8,128)(2,1)S(1)} %get-tuple-element.77), channel_id=1, source_target_pairs={{0,1},{1,0},{2,3},{3,2},{4,5},{5,4},{6,7},{7,6},{8,9},{9,8},{10,11... | collective-permute-start | bytes 786440 | tf_op jit(solution)/shard_map/ppermute | solution.py:30
  20.1 0.0 collective-permute-done.5.refs_4_
  20.1 0.0 copy-done.1
  20.1 1.6 %project.1 = (bf16[512,512]{1,0:T(8,128)(2,1)S(1)}, bf16[512,512]{1,0:T(8,128)(2,1)S(1)}, bf16[512,512]{1,0:T(8,128)(2,1)S(1)}, bf16[512,512]{1,0:T(8,128)(2,1)S(1)}, bf16[512,512]{1,0:T(8,128)(2,1)S(1)}) custom-call(bf16[512,512]{1,0:T(8,128)(2,1)S(1)} %get-tuple-element.52.normed.refs_0_, bf16[512,512]{1,0:T(8,128)(2,1)S(1)} %get-tuple-element.59.refs_1_, ...), custom_call_target="tpu_custom_call" | custom-call | flops 10000000 | tf_op jit(solution)/shard_map/project/pallas_call | solution.py:273
  21.7 2.7 %attend.2.refs_3_ = bf16[256,512]{1,0:T(8,128)(2,1)S(1)} custom-call(s32[4,128]{1,0:T(4,128)S(1)} %get-tuple-element.58.refs_0_, bf16[512,512]{1,0:T(8,128)(2,1)S(1)} %get-tuple-element.71.refs_1_, bf16[512,512]{1,0:T(8,128)(2,1)S(1)} %get-tuple-element.72.refs_2_, bf16[512,512]{1,0:T(8,128)(2,1)S(1)} %get-tuple-element.73.refs_3_, ...), custom_call_target="tpu_custom_call" | custom-call | flops 10000000 | tf_op jit(solution)/shard_map/attend/pallas_call | solution.py:273
  24.4 0.0 copy-start.3
  24.4 0.0 collective-permute-done.refs_1_
  24.5 1.7 %collective-permute-start.7 = (bf16[256,512]{1,0:T(8,128)(2,1)S(1)}, bf16[256,512]{1,0:T(8,128)(2,1)S(1)}, u32[]{:S(2)}, u32[]{:S(2)}) collective-permute-start(bf16[256,512]{1,0:T(8,128)(2,1)S(1)} %collective-permute-done.refs_1_), channel_id=1, source_target_pairs={{0,2},{2,0},{4,6},{6,4},{1,3},{3,1},{5,7},{7,5},{8,10},{10,8},{12,... | collective-permute-start | bytes 786440 | tf_op jit(solution)/shard_map/ppermute | solution.py:30
  26.1 0.0 copy-start.6
  26.1 2.7 %attend.3.refs_4_ = bf16[256,512]{1,0:T(8,128)(2,1)S(1)} custom-call(s32[4,128]{1,0:T(4,128)S(1)} %get-tuple-element.58.refs_0_, bf16[512,512]{1,0:T(8,128)(2,1)S(1)} %get-tuple-element.71.refs_1_, bf16[512,512]{1,0:T(8,128)(2,1)S(1)} %get-tuple-element.72.refs_2_, bf16[512,512]{1,0:T(8,128)(2,1)S(1)} %get-tuple-element.73.refs_3_, ...), custom_call_target="tpu_custom_call" | custom-call | flops 10000000 | tf_op jit(solution)/shard_map/attend/pallas_call | solution.py:273
  28.8 0.0 copy-start.2
  28.8 0.0 collective-permute-done.8.refs_5_
  28.8 0.0 collective-permute-done.9.refs_2_
  28.8 0.1 collective-permute-start.12
  28.9 1.5 %collective-permute-start.10 = (bf16[128,512]{1,0:T(8,128)(2,1)S(1)}, bf16[128,512]{1,0:T(8,128)(2,1)S(1)}, u32[]{:S(2)}, u32[]{:S(2)}) collective-permute-start(bf16[128,512]{1,0:T(8,128)(2,1)S(1)} %collective-permute-done.9.refs_2_), channel_id=1, source_target_pairs={{0,16},{8,24},{16,0},{24,8},{1,17},{9,25},{17,1},{25,9},{2,18},{10... | collective-permute-start | bytes 393224 | tf_op jit(solution)/shard_map/ppermute | solution.py:30
  30.5 0.2 collective-permute-start.13
  30.6 0.0 collective-permute-done.12.refs_6_
  30.6 0.0 copy-done.3
  30.6 0.0 copy-done.6
  30.6 0.7 %finish.1 = (f32[512,512]{1,0:T(8,128)S(1)}, bf16[512,512]{1,0:T(8,128)(2,1)S(1)}) custom-call(bf16[512,512]{1,0:T(8,128)(2,1)S(1)} %get-tuple-element.78.refs_0_, f32[1,512]{1,0:T(1,128)S(1)} %bitcast.6, bf16[256,512]{1,0:T(8,128)(2,1)S(1)} %copy-done.3, bf16[256,512]{1,0:T(8,128)(2,1)S(1)} %attend.2.refs_3_, bf16[256,512]{1,0:T(8,128)(2,1)S(1)} %attend.3.refs_4_, ...), custom_call_target="tpu_custom_call" | custom-call | flops 10000000 | tf_op jit(solution)/shard_map/finish/pallas_call | solution.py:273
  31.4 0.0 copy-done.2
  31.4 0.0 copy-start
  31.4 1.1 %hidden.2.refs_1_ = bf16[512,1024]{1,0:T(8,128)(2,1)S(1)} custom-call(bf16[512,512]{1,0:T(8,128)(2,1)S(1)} %get-tuple-element.83.refs_0_, bf16[1024,512]{1,0:T(8,128)(2,1)S(1)} %copy-done.2), custom_call_target="tpu_custom_call" | custom-call | flops 10000000 | tf_op jit(solution)/shard_map/hidden/pallas_call | solution.py:273
  32.5 0.1 copy-done
  32.6 0.7 %down.2.refs_0_ = f32[512,512]{1,0:T(8,128)S(1)} custom-call(f32[512,512]{1,0:T(8,128)S(1)} %get-tuple-element.82.refs_0_, bf16[512,1024]{1,0:T(8,128)(2,1)S(1)} %hidden.2.refs_1_, bf16[1024,512]{1,0:T(8,128)(2,1)S(1)} %copy-done), custom_call_target="tpu_custom_call" | custom-call | flops 10000000 | tf_op jit(solution)/shard_map/down/pallas_call | solution.py:273
  33.3 0.0 collective-permute-done.11.refs_6_
  33.3 1.5 %collective-permute-done.10.refs_4_ = bf16[128,512]{1,0:T(8,128)(2,1)S(1)} collective-permute-done((bf16[128,512]{1,0:T(8,128)(2,1)S(1)}, bf16[128,512]{1,0:T(8,128)(2,1)S(1)}, u32[]{:S(2)}, u32[]{:S(2)}) %collective-permute-start.10) | collective-permute-done | bytes 131104 | tf_op jit(solution)/shard_map/ppermute | solution.py:30
  34.8 0.0 collective-permute-done.7.refs_3_
  34.8 0.0 collective-permute-start.14
  34.8 0.5 %collective-permute-start.17 = (bf16[256,512]{1,0:T(8,128)(2,1)S(1)}, bf16[256,512]{1,0:T(8,128)(2,1)S(1)}, u32[]{:S(2)}, u32[]{:S(2)}) collective-permute-start(bf16[256,512]{1,0:T(8,128)(2,1)S(1)} %collective-permute-done.11.refs_6_), channel_id=1, source_target_pairs={{0,8},{8,0},{16,24},{24,16},{1,9},{9,1},{17,25},{25,17},{2,10},{10... | collective-permute-start | bytes 786440 | tf_op jit(solution)/shard_map/ppermute | solution.py:30
  35.3 0.0 collective-permute-start.15
  35.4 0.5 %collective-permute-start.16 = (bf16[128,512]{1,0:T(8,128)(2,1)S(1)}, bf16[128,512]{1,0:T(8,128)(2,1)S(1)}, u32[]{:S(2)}, u32[]{:S(2)}) collective-permute-start(bf16[128,512]{1,0:T(8,128)(2,1)S(1)} %collective-permute-done.10.refs_4_), channel_id=1, source_target_pairs={{0,8},{8,0},{16,24},{24,16},{1,9},{9,1},{17,25},{25,17},{2,10},{10... | collective-permute-start | bytes 393224 | tf_op jit(solution)/shard_map/ppermute | solution.py:30
  35.9 0.0 collective-permute-done.13.refs_2_
  35.9 0.5 %collective-permute-done.14.refs_4_ = bf16[256,512]{1,0:T(8,128)(2,1)S(1)} collective-permute-done((bf16[256,512]{1,0:T(8,128)(2,1)S(1)}, bf16[256,512]{1,0:T(8,128)(2,1)S(1)}, u32[]{:S(2)}, u32[]{:S(2)}) %collective-permute-start.14) | collective-permute-done | bytes 262176 | tf_op jit(solution)/shard_map/ppermute | solution.py:30
  36.4 1.1 %hidden.3.refs_1_ = bf16[512,1024]{1,0:T(8,128)(2,1)S(1)} custom-call(bf16[512,512]{1,0:T(8,128)(2,1)S(1)} %get-tuple-element.83.refs_0_, bf16[256,512]{1,0:T(8,128)(2,1)S(1)} %collective-permute-done.refs_1_, bf16[256,512]{1,0:T(8,128)(2,1)S(1)} %collective-permute-done.13.refs_2_, bf16[256,512]{1,0:T(8,128)(2,1)S(1)} %collective-permute-done.7.refs_3_, ...), custom_call_target="tpu_custom_call" | custom-call | flops 10000000 | tf_op jit(solution)/shard_map/hidden/pallas_call | solution.py:273
  37.5 0.0 collective-permute-done.15.refs_3_
  37.5 0.0 collective-permute-done.16.refs_5_
  37.5 0.0 collective-permute-done.17.refs_7_
  37.5 1.7 %down.3 = bf16[512,512]{1,0:T(8,128)(2,1)} custom-call(f32[512,512]{1,0:T(8,128)S(1)} %down.2.refs_0_, bf16[512,1024]{1,0:T(8,128)(2,1)S(1)} %hidden.3.refs_1_, bf16[128,512]{1,0:T(8,128)(2,1)S(1)} %collective-permute-done.9.refs_2_, bf16[128,512]{1,0:T(8,128)(2,1)S(1)} %collective-permute-done.15.refs_3_, ...), custom_call_target="tpu_custom_call" | custom-call | flops 10000000 | tf_op jit(solution)/shard_map/down/pallas_call | solution.py:273
Async XLA Ops:
  1.6 10.6 %collective-permute-start.1 = (bf16[192,512]{1,0:T(8,128)(2,1)S(1)}, bf16[192,512]{1,0:T(8,128)(2,1)S(1)}, u32[]{:S(2)}, u32[]{:S(2)}) collective-permute-start(bf16[192,512]{1,0:T(8,128)(2,1)S(1)} %get-tuple-element.53), channel_id=1, source_target_pairs={{0,1},{1,0},{2,3},{3,2},{4,5},{5,4},{6,7},{7,6},{8,9},{9,8},{10,11... | collective-permute-start | bytes 589832 | tf_op jit(solution)/shard_map/ppermute | solution.py:30
  4.6 9.9 %collective-permute-start.4 = (bf16[192,512]{1,0:T(8,128)(2,1)S(1)}, bf16[192,512]{1,0:T(8,128)(2,1)S(1)}, u32[]{:S(2)}, u32[]{:S(2)}) collective-permute-start(bf16[192,512]{1,0:T(8,128)(2,1)S(1)} %get-tuple-element.60), channel_id=1, source_target_pairs={{0,1},{1,0},{2,3},{3,2},{4,5},{5,4},{6,7},{7,6},{8,9},{9,8},{10,11... | collective-permute-start | bytes 589832 | tf_op jit(solution)/shard_map/ppermute | solution.py:30
  4.7 4.9 %collective-permute-start.2 = (bf16[128,512]{1,0:T(8,128)(2,1)S(1)}, bf16[128,512]{1,0:T(8,128)(2,1)S(1)}, u32[]{:S(2)}, u32[]{:S(2)}) collective-permute-start(bf16[128,512]{1,0:T(8,128)(2,1)S(1)} %get-tuple-element.54), channel_id=1, source_target_pairs={{0,8},{8,16},{16,24},{24,0},{1,9},{9,17},{17,25},{25,1},{2,10},{10... | collective-permute-start | bytes 393224 | tf_op jit(solution)/shard_map/ppermute | solution.py:25
  4.7 7.5 %collective-permute-start.3 = (bf16[128,512]{1,0:T(8,128)(2,1)S(1)}, bf16[128,512]{1,0:T(8,128)(2,1)S(1)}, u32[]{:S(2)}, u32[]{:S(2)}) collective-permute-start(bf16[128,512]{1,0:T(8,128)(2,1)S(1)} %get-tuple-element.55), channel_id=1, source_target_pairs={{0,2},{2,4},{4,6},{6,0},{1,3},{3,5},{5,7},{7,1},{8,10},{10,12},{12... | collective-permute-start | bytes 393224 | tf_op jit(solution)/shard_map/ppermute | solution.py:25
  6.7 10.0 %copy-start.4 = (f32[512]{0:T(512)S(1)}, f32[512]{0:T(512)}, u32[]{:S(2)}) copy-start(f32[512]{0:T(512)} %param.12) | copy-start | bytes 6148
  6.7 10.0 %copy-start.5 = (s32[4,128]{1,0:T(4,128)S(1)}, s32[4,128]{1,0:T(4,128)}, u32[]{:S(2)}) copy-start(s32[4,128]{1,0:T(4,128)} %context.3) | copy-start | bytes 6148
  6.7 10.0 %copy-start.7 = (s32[4]{0:T(128)S(1)}, s32[4]{0:T(128)}, u32[]{:S(2)}) copy-start(s32[4]{0:T(128)} %lengths.1) | copy-start | bytes 52
  7.9 12.1 %copy-start.1 = (bf16[768,512]{1,0:T(8,128)(2,1)S(1)}, bf16[768,512]{1,0:T(8,128)(2,1)}, u32[]{:S(2)}) copy-start(bf16[768,512]{1,0:T(8,128)(2,1)} %refs_2_.4) | copy-start | bytes 2359300
  8.0 16.5 %collective-permute-start = (bf16[256,512]{1,0:T(8,128)(2,1)S(1)}, bf16[256,512]{1,0:T(8,128)(2,1)S(1)}, u32[]{:S(2)}, u32[]{:S(2)}) collective-permute-start(bf16[256,512]{1,0:T(8,128)(2,1)S(1)} %get-tuple-element.51), channel_id=1, source_target_pairs={{0,1},{1,0},{2,3},{3,2},{4,5},{5,4},{6,7},{7,6},{8,9},{9,8},{10,11... | collective-permute-start | bytes 786440 | tf_op jit(solution)/shard_map/ppermute | solution.py:30
  12.2 5.8 %collective-permute-start.6 = (bf16[192,512]{1,0:T(8,128)(2,1)S(1)}, bf16[192,512]{1,0:T(8,128)(2,1)S(1)}, u32[]{:S(2)}, u32[]{:S(2)}) collective-permute-start(bf16[192,512]{1,0:T(8,128)(2,1)S(1)} %collective-permute-done.1.refs_5_), channel_id=1, source_target_pairs={{0,8},{8,0},{16,24},{24,16},{1,9},{9,1},{17,25},{25,17},{2,10},{10... | collective-permute-start | bytes 589832 | tf_op jit(solution)/shard_map/ppermute | solution.py:30
  14.6 5.5 %collective-permute-start.5 = (bf16[192,512]{1,0:T(8,128)(2,1)S(1)}, bf16[192,512]{1,0:T(8,128)(2,1)S(1)}, u32[]{:S(2)}, u32[]{:S(2)}) collective-permute-start(bf16[192,512]{1,0:T(8,128)(2,1)S(1)} %collective-permute-done.4.refs_3_), channel_id=1, source_target_pairs={{0,8},{8,0},{16,24},{24,16},{1,9},{9,1},{17,25},{25,17},{2,10},{10... | collective-permute-start | bytes 589832 | tf_op jit(solution)/shard_map/ppermute | solution.py:30
  14.6 14.3 %collective-permute-start.8 = (bf16[128,512]{1,0:T(8,128)(2,1)S(1)}, bf16[128,512]{1,0:T(8,128)(2,1)S(1)}, u32[]{:S(2)}, u32[]{:S(2)}) collective-permute-start(bf16[128,512]{1,0:T(8,128)(2,1)S(1)} %get-tuple-element.68), channel_id=1, source_target_pairs={{0,1},{1,0},{2,3},{3,2},{4,5},{5,4},{6,7},{7,6},{8,9},{9,8},{10,11... | collective-permute-start | bytes 393224 | tf_op jit(solution)/shard_map/ppermute | solution.py:30
  16.6 12.2 %collective-permute-start.9 = (bf16[128,512]{1,0:T(8,128)(2,1)S(1)}, bf16[128,512]{1,0:T(8,128)(2,1)S(1)}, u32[]{:S(2)}, u32[]{:S(2)}) collective-permute-start(bf16[128,512]{1,0:T(8,128)(2,1)S(1)} %get-tuple-element.69), channel_id=1, source_target_pairs={{0,1},{1,0},{2,3},{3,2},{4,5},{5,4},{6,7},{7,6},{8,9},{9,8},{10,11... | collective-permute-start | bytes 393224 | tf_op jit(solution)/shard_map/ppermute | solution.py:30
  18.0 15.3 %collective-permute-start.11 = (bf16[256,512]{1,0:T(8,128)(2,1)S(1)}, bf16[256,512]{1,0:T(8,128)(2,1)S(1)}, u32[]{:S(2)}, u32[]{:S(2)}) collective-permute-start(bf16[256,512]{1,0:T(8,128)(2,1)S(1)} %get-tuple-element.77), channel_id=1, source_target_pairs={{0,1},{1,0},{2,3},{3,2},{4,5},{5,4},{6,7},{7,6},{8,9},{9,8},{10,11... | collective-permute-start | bytes 786440 | tf_op jit(solution)/shard_map/ppermute | solution.py:30
  24.4 6.2 %copy-start.3 = (bf16[256,512]{1,0:T(8,128)(2,1)S(1)}, bf16[256,512]{1,0:T(8,128)(2,1)}, u32[]{:S(2)}) copy-start(bf16[256,512]{1,0:T(8,128)(2,1)} %refs_2_.5) | copy-start | bytes 786436
  24.5 10.4 %collective-permute-start.7 = (bf16[256,512]{1,0:T(8,128)(2,1)S(1)}, bf16[256,512]{1,0:T(8,128)(2,1)S(1)}, u32[]{:S(2)}, u32[]{:S(2)}) collective-permute-start(bf16[256,512]{1,0:T(8,128)(2,1)S(1)} %collective-permute-done.refs_1_), channel_id=1, source_target_pairs={{0,2},{2,0},{4,6},{6,4},{1,3},{3,1},{5,7},{7,5},{8,10},{10,8},{12,... | collective-permute-start | bytes 786440 | tf_op jit(solution)/shard_map/ppermute | solution.py:30
  26.1 4.5 %copy-start.6 = (f32[512]{0:T(512)S(1)}, f32[512]{0:T(512)}, u32[]{:S(2)}) copy-start(f32[512]{0:T(512)} %param.13) | copy-start | bytes 6148
  28.8 2.6 %copy-start.2 = (bf16[1024,512]{1,0:T(8,128)(2,1)S(1)}, bf16[1024,512]{1,0:T(8,128)(2,1)}, u32[]{:S(2)}) copy-start(bf16[1024,512]{1,0:T(8,128)(2,1)} %refs_1_.2) | copy-start | bytes 3145732
  28.8 1.8 %collective-permute-start.12 = (bf16[128,512]{1,0:T(8,128)(2,1)S(1)}, bf16[128,512]{1,0:T(8,128)(2,1)S(1)}, u32[]{:S(2)}, u32[]{:S(2)}) collective-permute-start(bf16[128,512]{1,0:T(8,128)(2,1)S(1)} %collective-permute-done.8.refs_5_), channel_id=1, source_target_pairs={{0,8},{8,0},{16,24},{24,16},{1,9},{9,1},{17,25},{25,17},{2,10},{10... | collective-permute-start | bytes 393224 | tf_op jit(solution)/shard_map/ppermute | solution.py:30
  28.9 5.9 %collective-permute-start.10 = (bf16[128,512]{1,0:T(8,128)(2,1)S(1)}, bf16[128,512]{1,0:T(8,128)(2,1)S(1)}, u32[]{:S(2)}, u32[]{:S(2)}) collective-permute-start(bf16[128,512]{1,0:T(8,128)(2,1)S(1)} %collective-permute-done.9.refs_2_), channel_id=1, source_target_pairs={{0,16},{8,24},{16,0},{24,8},{1,17},{9,25},{17,1},{25,9},{2,18},{10... | collective-permute-start | bytes 393224 | tf_op jit(solution)/shard_map/ppermute | solution.py:30
  30.5 5.4 %collective-permute-start.13 = (bf16[256,512]{1,0:T(8,128)(2,1)S(1)}, bf16[256,512]{1,0:T(8,128)(2,1)S(1)}, u32[]{:S(2)}, u32[]{:S(2)}) collective-permute-start(bf16[256,512]{1,0:T(8,128)(2,1)S(1)} %collective-permute-done.refs_1_), channel_id=1, source_target_pairs={{0,8},{8,0},{16,24},{24,16},{1,9},{9,1},{17,25},{25,17},{2,10},{10... | collective-permute-start | bytes 786440 | tf_op jit(solution)/shard_map/ppermute | solution.py:30
  31.4 1.2 %copy-start = (bf16[1024,512]{1,0:T(8,128)(2,1)S(1)}, bf16[1024,512]{1,0:T(8,128)(2,1)}, u32[]{:S(2)}) copy-start(bf16[1024,512]{1,0:T(8,128)(2,1)} %refs_2_.6) | copy-start | bytes 3145732
  34.8 1.5 %collective-permute-start.14 = (bf16[256,512]{1,0:T(8,128)(2,1)S(1)}, bf16[256,512]{1,0:T(8,128)(2,1)S(1)}, u32[]{:S(2)}, u32[]{:S(2)}) collective-permute-start(bf16[256,512]{1,0:T(8,128)(2,1)S(1)} %collective-permute-done.7.refs_3_), channel_id=1, source_target_pairs={{0,8},{8,0},{16,24},{24,16},{1,9},{9,1},{17,25},{25,17},{2,10},{10... | collective-permute-start | bytes 786440 | tf_op jit(solution)/shard_map/ppermute | solution.py:30
  34.8 2.7 %collective-permute-start.17 = (bf16[256,512]{1,0:T(8,128)(2,1)S(1)}, bf16[256,512]{1,0:T(8,128)(2,1)S(1)}, u32[]{:S(2)}, u32[]{:S(2)}) collective-permute-start(bf16[256,512]{1,0:T(8,128)(2,1)S(1)} %collective-permute-done.11.refs_6_), channel_id=1, source_target_pairs={{0,8},{8,0},{16,24},{24,16},{1,9},{9,1},{17,25},{25,17},{2,10},{10... | collective-permute-start | bytes 786440 | tf_op jit(solution)/shard_map/ppermute | solution.py:30
  35.3 2.1 %collective-permute-start.15 = (bf16[128,512]{1,0:T(8,128)(2,1)S(1)}, bf16[128,512]{1,0:T(8,128)(2,1)S(1)}, u32[]{:S(2)}, u32[]{:S(2)}) collective-permute-start(bf16[128,512]{1,0:T(8,128)(2,1)S(1)} %collective-permute-done.9.refs_2_), channel_id=1, source_target_pairs={{0,8},{8,0},{16,24},{24,16},{1,9},{9,1},{17,25},{25,17},{2,10},{10... | collective-permute-start | bytes 393224 | tf_op jit(solution)/shard_map/ppermute | solution.py:30
  35.4 2.2 %collective-permute-start.16 = (bf16[128,512]{1,0:T(8,128)(2,1)S(1)}, bf16[128,512]{1,0:T(8,128)(2,1)S(1)}, u32[]{:S(2)}, u32[]{:S(2)}) collective-permute-start(bf16[128,512]{1,0:T(8,128)(2,1)S(1)} %collective-permute-done.10.refs_4_), channel_id=1, source_target_pairs={{0,8},{8,0},{16,24},{24,16},{1,9},{9,1},{17,25},{25,17},{2,10},{10... | collective-permute-start | bytes 393224 | tf_op jit(solution)/shard_map/ppermute | solution.py:30

commit v3 on v2

--- a/solution.py
+++ b/solution.py
@@ -67,13 +67,12 @@
     return jnp.where(lax.axis_index(axis) > 0, halo[...].astype(jnp.float32), 0.0)
 
 
-def context_kernel(lengths, normed, halo_x, halo_y, gain, context, chosen, filled):
+def context_kernel(normed, halo_x, halo_y, gain, context, chosen):
     parts = [layer_norm(present(halo_x, "gx"), gain[...]), layer_norm(present(halo_y, "gy"), gain[...])]
     pool = jnp.concatenate([normed[...]] + parts, axis=0)
     for window in range(context.shape[0]):
         picked = dot_nn(pick_rows(context[pl.ds(window, 1), :], pool.shape[0]), pool)
         chosen[pl.ds(window * CTX, CTX), :] = picked.astype(jnp.bfloat16)
-        filled[pl.ds(window, 1), :] = jnp.full((1, LANES), lengths[window], jnp.int32)
 
 
 class Share(typing.NamedTuple):
@@ -92,15 +91,16 @@
         return self.base + (index ^ flip) * self.stride
 
 
-def slice_kernel(shares, *refs):
-    count = len(shares)
-    shards, parts, sems = refs[:count], refs[count : 2 * count], refs[2 * count]
+def slice_kernel(groups, *refs):
+    parts, sems = refs[-1 - len(groups) : -1], refs[-1]
     copies = []
-    for number, share in enumerate(shares):
-        start = pl.multiple_of(share.start(0), 32)
-        copies.append(
-            pltpu.make_async_copy(shards[number].at[pl.ds(start, share.rows), :], parts[number], sems.at[number])
-        )
+    for part, group in zip(parts, groups):
+        low = 0
+        for share in group:
+            start = pl.multiple_of(share.start(0), 32)
+            source = refs[len(copies)].at[pl.ds(start, share.rows), :]
+            copies.append(pltpu.make_async_copy(source, part.at[pl.ds(low, share.rows), :], sems.at[len(copies)]))
+            low += share.rows
     for copy in copies:
         copy.start()
     for copy in copies:
@@ -109,23 +109,25 @@
 
 def prepare_kernel(shares, *refs):
     count = len(shares)
-    sources, shards, refs = refs[:4], refs[4 : 4 + count], refs[4 + count :]
-    (held, out_x, out_y, normed), parts, scratch, sems = refs[:4], refs[4 : 4 + count], refs[4 + count : -1], refs[-1]
-    copies = []
-    for source, target in zip(sources, (held, *scratch)):
-        copies.append(pltpu.make_async_copy(source, target, sems.at[len(copies)]))
+    (tokens, gain_one, gain_two, send_x, send_y, context, lengths), refs = refs[:7], refs[7:]
+    shards, refs = refs[:count], refs[count:]
+    (held, one, two, chosen, filled, out_x, out_y, normed), refs = refs[:8], refs[8:]
+    parts, (rows_x, rows_y, sizes, sems) = refs[:count], refs[count:]
+    pairs = [(tokens, held), (gain_one, one), (send_x, rows_x), (send_y, rows_y)]
     for number, share in enumerate(shares):
         start = pl.multiple_of(share.start(0), 32)
-        copies.append(
-            pltpu.make_async_copy(shards[number].at[pl.ds(start, share.rows), :], parts[number], sems.at[len(copies)])
-        )
+        pairs.append((shards[number].at[pl.ds(start, share.rows), :], parts[number]))
+    pairs += [(gain_two, two), (context, chosen), (lengths, sizes)]
+    copies = [pltpu.make_async_copy(*pair, sems.at[number]) for number, pair in enumerate(pairs)]
     for copy in copies:
         copy.start()
     for copy in copies[:4]:
         copy.wait()
-    norm_kernel(held, *scratch, out_x, out_y, normed)
+    norm_kernel(held, one, rows_x, rows_y, out_x, out_y, normed)
     for copy in copies[4:]:
         copy.wait()
+    for window in range(filled.shape[0]):
+        filled[pl.ds(window, 1), :] = jnp.full((1, LANES), sizes[window], jnp.int32)
 
 
 def assemble(whole, own, pieces):
@@ -159,53 +161,53 @@
     head_size = width // HEADS
     group = LANES // head_size
     scale = head_size ** (-0.5) * LOG2E
+    ready = []
     for window in windows:
-        low, high = window * WIN, (window + 1) * WIN
-        base = low - windows[0] * WIN
         length = filled[window : window + 1, :]
         row_full = lax.broadcasted_iota(jnp.int32, (WIN, LANES), 0) < length
-        row_full = jnp.concatenate([row_full] * (width // LANES), axis=1)
-        keys = jnp.concatenate(
-            [
-                jnp.where(row_full, own_keys[low:high, :], ctx_keys[low : low + 1, :]),
-                ctx_keys[low:high, :],
-            ],
-            axis=0,
+        slot_full = lax.broadcasted_iota(jnp.int32, (1, WIN), 1) < length
+        own_ones = lax.broadcasted_iota(jnp.int32, (16, WIN), 1) < length
+        ones = jnp.concatenate([jnp.where(own_ones, 1.0, 0.0), jnp.ones((16, CTX), jnp.float32)], axis=1)
+        ready.append((slice(window * WIN, (window + 1) * WIN), row_full, slot_full, ones.astype(jnp.bfloat16)))
+
+    def scores_of(number, first):
+        rows, row_full, _, _ = ready[number]
+        lanes = slice(first, first + LANES)
+        own = jnp.where(row_full, own_keys[rows, lanes], ctx_keys[rows.start : rows.start + 1, lanes])
+        keys = jnp.concatenate([own, ctx_keys[rows, lanes]], axis=0)
+        parts = []
+        for head in range(group):
+            pad = [jnp.zeros((head_size, WIN), jnp.bfloat16)] * group
+            pad[head] = queries[first + head * head_size : first + (head + 1) * head_size, rows]
+            parts.append(jnp.concatenate(pad, axis=0))
+        return dot_nn(keys, jnp.concatenate(parts, axis=1))
+
+    def mix(number, first, scores):
+        rows, _, slot_full, ones = ready[number]
+        largest = jnp.max(scores, axis=0, keepdims=True)
+        probs = jnp.exp2((scores - largest) * scale).astype(jnp.bfloat16)
+        outs = []
+        for head in range(0, group, 2):
+            features = slice(first + head * head_size, first + (head + 2) * head_size)
+            own = jnp.where(slot_full, own_values[features, rows], jnp.zeros((), jnp.bfloat16))
+            values = jnp.concatenate([own, ctx_values[features, rows]], axis=1)
+            sums = dot_nn(jnp.concatenate([values, ones], axis=0), probs[:, head * WIN : (head + 2) * WIN])
+            for part in range(2):
+                block = sums[:, part * WIN : (part + 1) * WIN]
+                weight = 1.0 / block[2 * head_size : 2 * head_size + 1]
+                outs.append(block[part * head_size : (part + 1) * head_size] * weight)
+        mixed[number * WIN : (number + 1) * WIN, first : first + LANES] = (
+            jnp.concatenate(outs, axis=0).T.astype(jnp.bfloat16)
         )
-        slot_full = lax.broadcasted_iota(jnp.int32, (1, WIN), 1) < length
-        values = jnp.concatenate(
-            [
-                jnp.where(slot_full, own_values[:, low:high], jnp.zeros((), jnp.bfloat16)),
-                ctx_values[:, low:high],
-            ],
-            axis=1,
-        )
-        slots = lax.broadcasted_iota(jnp.int32, (16, WIN), 1) < length
-        ones = jnp.concatenate([jnp.where(slots, 1.0, 0.0), jnp.ones((16, CTX), jnp.float32)], axis=1).astype(jnp.bfloat16)
-        for first in range(0, width, LANES):
-            group_queries = queries[first : first + LANES, low:high]
-            parts = []
-            for head in range(group):
-                pad = [jnp.zeros((head_size, WIN), jnp.bfloat16)] * group
-                pad[head] = group_queries[head * head_size : (head + 1) * head_size]
-                parts.append(jnp.concatenate(pad, axis=0))
-            scores = dot_nn(keys[:, first : first + LANES], jnp.concatenate(parts, axis=1))
-            largest = jnp.max(scores, axis=0, keepdims=True)
-            probs = jnp.exp2((scores - largest) * scale).astype(jnp.bfloat16)
-            outs = []
-            for head in range(0, group, 2):
-                top = first + head * head_size
-                weights = jnp.concatenate([values[top : top + 2 * head_size], ones], axis=0)
-                sums = dot_nn(weights, probs[:, head * WIN : (head + 2) * WIN])
-                for part in range(2):
-                    block = sums[:, part * WIN : (part + 1) * WIN]
-                    outs.append(
-                        block[part * head_size : (part + 1) * head_size]
-                        * (1.0 / block[2 * head_size : 2 * head_size + 1])
-                    )
-            mixed[base : base + WIN, first : first + LANES] = (
-                jnp.concatenate(outs, axis=0).T.astype(jnp.bfloat16)
-            )
+
+    waiting = []
+    for item in [(number, first) for number in range(len(windows)) for first in range(0, width, LANES)]:
+        waiting.append((item, scores_of(*item)))
+        if len(waiting) > 2:
+            done, scores = waiting.pop(0)
+            mix(*done, scores)
+    for done, scores in waiting:
+        mix(*done, scores)
 
 
 def finish_kernel(parts, plan, tokens, gain, shard, *refs):
@@ -235,12 +237,19 @@
         hidden[:, columns_of(plan, number, piece)] = units
 
 
-def down_kernel(plan, start, hidden, *refs):
-    output = refs[-1]
+def feed_kernel(start, second, into, down, output):
+    size = min(256, into.shape[0])
     total = start[...]
-    for number, piece in enumerate(refs[:-1]):
-        total = total + dot_nn(hidden[:, columns_of(plan, number, piece)], piece[...])
-    output[...] = total.astype(output.dtype)
+    waiting = []
+
+    def add(low, product):
+        return total + dot_nn(jax.nn.gelu(product).astype(jnp.bfloat16), down[low : low + size, :])
+
+    for low in range(0, into.shape[0], size):
+        waiting.append((low, dot_nt(second[...], into[low : low + size, :])))
+        if len(waiting) > 1:
+            total = add(*waiting.pop(0))
+    output[...] = add(*waiting.pop(0)).astype(output.dtype)
 
 
 def last_kernel(plan, start, hidden, *refs):
@@ -259,7 +268,7 @@
         copy.wait()
 
 
-COSTS = {"norm": 1, "slices": 1, "prepare": 1, "context": 1, "project": 1, "attend": 1, "finish": 1, "hidden": 1, "down": 1}
+COSTS = {"norm": 1, "slices": 1, "prepare": 1, "context": 1, "project": 1, "attend": 50, "finish": 1, "feed": 1, "hidden": 1, "last": 1}
 
 
 def call(kernel, outs, operands, name, scratch=(), specs=None, result=VMEM):
@@ -300,33 +309,39 @@
             lax.all_gather(weight, "fsdp", axis=0, tiled=True) for weight in (w_qkv, w_out, w_in, w_down)
         )
         out_x, out_y, normed = call(norm_kernel, edges, (tokens, gain_one, send_x, send_y), "norm")
+        filled = jnp.broadcast_to(lengths[:, None], context.shape)
     else:
         qkv, out, into, down = w_qkv, w_out, w_in, w_down
-        size = qkv.shape[0] // 4
-        share_qkv = [Share(chunk * size, "core", 2 * size, size) for chunk in range(2)]
+        size = qkv.shape[0] // 2
+        share_qkv = Share(0, "core", size, size)
         share_out = Share(0, "core", out.shape[0] // 2, out.shape[0] // 2)
         share_in = Share(0, "gy", into.shape[0] // 4, into.shape[0] // 4)
         size = down.shape[0] // 8
         share_early = Share(0, "gx", size, size)
         share_late = Share(4 * size, "core", 2 * size, 2 * size)
-        tokens, out_x, out_y, normed, *parts_qkv = call(
-            lambda *refs: prepare_kernel(share_qkv, *refs),
-            [struct(rows, width)] + edges + [struct(share.rows, width) for share in share_qkv],
-            (tokens, gain_one, send_x, send_y, qkv, qkv), "prepare",
+        tokens, gain_one, gain_two, context, filled, out_x, out_y, normed, part_qkv = call(
+            lambda *refs: prepare_kernel([share_qkv], *refs),
             [
-                pltpu.VMEM(gain_one.shape, gain_one.dtype), pltpu.VMEM(send_x.shape, send_x.dtype),
-                pltpu.VMEM(send_y.shape, send_y.dtype), pltpu.SemaphoreType.DMA((6,)),
+                struct(rows, width), struct(1, width, jnp.float32), struct(1, width, jnp.float32),
+                struct(*context.shape, jnp.int32), struct(*context.shape, jnp.int32),
+            ]
+            + edges + [struct(share_qkv.rows, width)],
+            (tokens, gain_one, gain_two, send_x, send_y, context, lengths, qkv), "prepare",
+            [
+                pltpu.VMEM(send_x.shape, jnp.int32), pltpu.VMEM(send_y.shape, jnp.int32),
+                pltpu.SMEM(lengths.shape, jnp.int32), pltpu.SemaphoreType.DMA((8,)),
             ],
-            [HBM] * 6,
+            [HBM] * 8,
         )
-        y_qkv = [swap(part, "fsdp", 1) for part in parts_qkv]
-        shares = [share_in, share_out, share_early, share_late]
+        y_qkv = swap(part_qkv, "fsdp", 1)
+        groups = [[share_in], [share_out, share_early], [share_late]]
         later, normed = after(((w_in, w_out, w_down), normed))
         parts = call(
-            lambda *refs: slice_kernel(shares, *refs), [struct(share.rows, width) for share in shares],
+            lambda *refs: slice_kernel(groups, *refs),
+            [struct(sum(share.rows for share in group), width) for group in groups],
             (later[0], later[1], later[2], later[2]), "slices", [pltpu.SemaphoreType.DMA((4,))], [HBM] * 4,
         )
-        y_in, y_out, y_early, y_late = (swap(part, "fsdp", 1) for part in parts)
+        y_in, y_middle, y_late = (swap(part, "fsdp", 1) for part in parts)
 
     def crossed(share, near, flip=0):
         return [(share, flip, near), (share, flip + 1, swap(near, "gx", 1))]
@@ -339,16 +354,16 @@
 
     halo_x = ring(out_x, "gx")
     halo_y = ring(out_y, "gy")
+    (chosen,) = call(context_kernel, [struct(rows, width)], (normed, halo_x, halo_y, gain_one, context), "context")
     if paired:
-        y_qkv[1], halo_x, halo_y = after((y_qkv[1], halo_x, halo_y))
-    chosen, filled = call(
-        context_kernel, [struct(rows, width), struct(*context.shape, jnp.int32)],
-        (lengths, normed, halo_x, halo_y, gain_one, context), "context", specs=[SMEM] + [VMEM] * 5,
-    )
+        y_qkv, chosen = after((y_qkv, chosen))
     pieces = []
     if paired:
-        for share, piece in zip(share_qkv, y_qkv):
-            pieces += crossed(share, piece)
+        pieces.append((share_qkv, 0, y_qkv))
+        size = share_qkv.rows // 2
+        for low in range(0, share_qkv.rows, size):
+            share = share_qkv._replace(base=low, rows=size)
+            pieces.append((share, 1, swap(y_qkv[low : low + size], "gx", 1)))
     projected = call(
         lambda *refs, plan=plan(pieces): project_kernel(plan, *refs), [struct(rows, width)] * 5,
         (normed, chosen, qkv, *arrays(pieces)), "project", [pltpu.VMEM((3 * width, width), jnp.bfloat16)],
@@ -370,7 +385,8 @@
         projected, y_in = after((projected, y_in))
     mixed += attend(windows[half:])
     if paired:
-        y_out, y_early, mixed = after((y_out, y_early, mixed))
+        y_middle, mixed = after((y_middle, mixed))
+        y_out, y_early = y_middle[: share_out.rows], y_middle[share_out.rows :]
         pieces_out = crossed(share_out, y_out)
         x_early = swap(y_early, "gx", 2)
     middle, second = call(
@@ -379,29 +395,29 @@
         "finish", [pltpu.VMEM((width, width), jnp.bfloat16)],
     )
 
-    def expand(own, pieces):
-        (hidden,) = call(
-            lambda *refs: hidden_kernel(plan(pieces), *refs), [struct(rows, into.shape[0])],
-            (second, *(arrays(pieces) or [own])), "hidden",
-        )
-        return hidden
-
+    (total,) = call(
+        feed_kernel, [struct(rows, width, jnp.float32 if paired else jnp.bfloat16)], (middle, second, into, down), "feed"
+    )
     if not paired:
-        return call(
-            lambda *refs: down_kernel([], *refs), [struct(rows, width)],
-            (middle, expand(into, []), down), "down", result=None,
-        )[0]
-    (total,) = call(
-        lambda *refs: down_kernel([], *refs), [struct(rows, width, jnp.float32)],
-        (middle, expand(into, []), down), "down",
+        return total
+    z_in, total = after((z_in, total))
+    pieces = crossed(share_in, y_in) + crossed(share_in, z_in, 2)
+    (hidden,) = call(
+        lambda *refs, plan=plan(pieces): hidden_kernel(plan, *refs), [struct(rows, into.shape[0])],
+        (second, *arrays(pieces)), "hidden",
     )
-    z_in, x_early, y_late, total = after((z_in, x_early, y_late, total))
-    pieces = crossed(share_in, y_in) + crossed(share_in, z_in, 2)
-    pieces_down = crossed(share_early, y_early) + crossed(share_early, x_early, 2) + crossed(share_late, y_late)
-    hidden = expand(None, pieces)
+    LATE = 0
+    if LATE == 0:
+        x_early, y_late, total = after((x_early, y_late, total))
+    elif LATE == 1:
+        x_early, y_late, hidden = after((x_early, y_late, hidden))
+    else:
+        y_late, total = after((y_late, total))
+        x_early, hidden = after((x_early, hidden))
+    pieces = crossed(share_early, y_early) + crossed(share_early, x_early, 2) + crossed(share_late, y_late)
     return call(
-        lambda *refs: last_kernel(plan(pieces_down), *refs), [struct(rows, width)],
-        (total, hidden, *arrays(pieces_down)), "down",
+        lambda *refs: last_kernel(plan(pieces), *refs), [struct(rows, width)],
+        (total, hidden, *arrays(pieces)), "last",
         [pltpu.VMEM((rows, width), jnp.bfloat16), pltpu.SemaphoreType.DMA((rows // WIN,))], result=HBM,
     )[0]
 

time: 39.4 us -> 35.9 us (0.911)
  Pallas kernels: 16.5 us -> 13.1 us
  waiting for transfers between devices: 6.33 us -> 9.18 us
  starting transfers between devices: 16 us -> 13.2 us
    pallas_call x11 -> x10, Pallas kernels: 16.5 us -> 13.1 us  [call(): pl.pallas_call(kernel, out_shape=tuple(outs), in_specs=specs, out_specs=t...]
    ppermute x16 -> x14, starting transfers between devices: 14 us -> 11.6 us  [swap(): lax.ppermute(value, axis, [(source, source ^ bit) for source in range(cou...]
    ppermute x2, waiting for transfers between devices: 2.63 us -> 4.16 us  [ring(): lax.ppermute(value, axis, [(source, (source + 1) % count) for source in r...]
    ppermute x16 -> x14, waiting for transfers between devices: 3.7 us -> 5.02 us  [swap(): lax.ppermute(value, axis, [(source, source ^ bit) for source in range(cou...]
    ppermute x2, starting transfers between devices: 2.01 us -> 1.58 us  [ring(): lax.ppermute(value, axis, [(source, (source + 1) % count) for source in r...]
  transfers between devices with their start and end apart: 18 -> 16, of which waited for: 4 -> 7; matrix products, arithmetic and copies ran while one was open for 0% -> 0% of each run, Pallas kernels for 34% -> 27%
where the time goes in v3:
time: 35.9 us; the launch traced here: 35.7 us
  starting transfers between devices  13.2 us (37%)
  Pallas kernels  13.1 us (36%)
  waiting for transfers between devices  9.18 us (26%)
    pallas_call x10, Pallas kernels, call(): pl.pallas_call(kernel, out_shape=tuple(outs), in_specs=specs, out_specs=t...  13.1 us
    ppermute x14, starting transfers between devices, swap(): lax.ppermute(value, axis, [(source, source ^ bit) for source in range(cou...  11.6 us
    ppermute x14, waiting for transfers between devices, swap(): lax.ppermute(value, axis, [(source, source ^ bit) for source in range(cou...  5.02 us
    ppermute x2, waiting for transfers between devices, ring(): lax.ppermute(value, axis, [(source, (source + 1) % count) for source in r...  4.16 us
    ppermute x2, starting transfers between devices, ring(): lax.ppermute(value, axis, [(source, (source + 1) % count) for source in r...  1.58 us
  transfers between devices with their start and end apart: 16, of which 7 were waited for; matrix products, arithmetic and copies ran while one was open for 0% of the time, Pallas kernels for 27%

profile of v3, /device:TPU:0, one launch (start us, length us, event | category | flops | bytes accessed | tf_op | source)
XLA Modules:
  0.0 35.7 jit_solution(1747360738228223770)
XLA Ops:
  0.0 1.6 %prepare.1 = (bf16[512,512]{1,0:T(8,128)(2,1)S(1)}, f32[1,512]{1,0:T(1,128)S(1)}, f32[1,512]{1,0:T(1,128)S(1)}, s32[4,128]{1,0:T(4,128)S(1)}, s32[4,128]{1,0:T(4...) custom-call(bf16[512,512]{1,0:T(8,128)(2,1)} %refs_0_.1, ...), custom_call_target="tpu_custom_call" | custom-call | flops 10000000 | tf_op jit(solution)/shard_map/prepare/pallas_call | solution.py:282
  1.6 3.0 %collective-permute-start.2 = (bf16[384,512]{1,0:T(8,128)(2,1)S(1)}, bf16[384,512]{1,0:T(8,128)(2,1)S(1)}, u32[]{:S(2)}, u32[]{:S(2)}) collective-permute-start(bf16[384,512]{1,0:T(8,128)(2,1)S(1)} %get-tuple-element.54), channel_id=1, source_target_pairs={{0,1},{1,0},{2,3},{3,2},{4,5},{5,4},{6,7},{7,6},{8,9},{9,8},{10,11... | collective-permute-start | bytes 1179656 | tf_op jit(solution)/shard_map/ppermute | solution.py:30
  4.6 0.0 collective-permute-start.3
  4.6 1.6 %collective-permute-start.4 = (bf16[128,512]{1,0:T(8,128)(2,1)S(1)}, bf16[128,512]{1,0:T(8,128)(2,1)S(1)}, u32[]{:S(2)}, u32[]{:S(2)}) collective-permute-start(bf16[128,512]{1,0:T(8,128)(2,1)S(1)} %get-tuple-element.56), channel_id=1, source_target_pairs={{0,2},{2,4},{4,6},{6,0},{1,3},{3,5},{5,7},{7,1},{8,10},{10,12},{12... | collective-permute-start | bytes 393224 | tf_op jit(solution)/shard_map/ppermute | solution.py:25
  6.2 1.2 %slices.1 = (bf16[256,512]{1,0:T(8,128)(2,1)S(1)}, bf16[256,512]{1,0:T(8,128)(2,1)S(1)}, bf16[256,512]{1,0:T(8,128)(2,1)S(1)}) custom-call(bf16[1024,512]{1,0:T(8,128)(2,1)} %into.1, bf16[256,512]{1,0:T(8,128)(2,1)} %refs_2_.4, bf16[1024,512]{1,0:T(8,128)(2,1)} %down.1, bf16[1024,512]{1,0:T(8,128)(2,1)} %down.1), custom_call_target="tpu_custom_call" | custom-call | flops 10000000 | tf_op jit(solution)/shard_map/slices/pallas_call | solution.py:282
  7.4 0.6 %collective-permute-start.1 = (bf16[256,512]{1,0:T(8,128)(2,1)S(1)}, bf16[256,512]{1,0:T(8,128)(2,1)S(1)}, u32[]{:S(2)}, u32[]{:S(2)}) collective-permute-start(bf16[256,512]{1,0:T(8,128)(2,1)S(1)} %get-tuple-element.51), channel_id=1, source_target_pairs={{0,1},{1,0},{2,3},{3,2},{4,5},{5,4},{6,7},{7,6},{8,9},{9,8},{10,11... | collective-permute-start | bytes 786440 | tf_op jit(solution)/shard_map/ppermute | solution.py:30
  8.0 1.0 %collective-permute-done.3.halo_x = bf16[128,512]{1,0:T(8,128)(2,1)S(1)} collective-permute-done((bf16[128,512]{1,0:T(8,128)(2,1)S(1)}, bf16[128,512]{1,0:T(8,128)(2,1)S(1)}, u32[]{:S(2)}, u32[]{:S(2)}) %collective-permute-start.3) | collective-permute-done | bytes 131104 | tf_op jit(solution)/shard_map/ppermute | solution.py:25
  9.0 3.1 %collective-permute-done.4.halo_y = bf16[128,512]{1,0:T(8,128)(2,1)S(1)} collective-permute-done((bf16[128,512]{1,0:T(8,128)(2,1)S(1)}, bf16[128,512]{1,0:T(8,128)(2,1)S(1)}, u32[]{:S(2)}, u32[]{:S(2)}) %collective-permute-start.4) | collective-permute-done | bytes 131104 | tf_op jit(solution)/shard_map/ppermute | solution.py:25
  12.2 0.0 copy-start.2
  12.2 0.8 %context.1.refs_1_ = bf16[512,512]{1,0:T(8,128)(2,1)S(1)} custom-call(bf16[512,512]{1,0:T(8,128)(2,1)S(1)} %get-tuple-element.53.normed.refs_0_, bf16[128,512]{1,0:T(8,128)(2,1)S(1)} %collective-permute-done.3.halo_x, bf16[128,512]{1,0:T(8,128)(2,1)S(1)} %collective-permute-done.4.halo_y, f32[1,512]{1,0:T(1,128)S(1)} %get-tuple-element.57.gain, ...), custom_call_target="tpu_custom_call" | custom-call | flops 10000000 | tf_op jit(solution)/shard_map/context/pallas_call | solution.py:282
  13.0 1.6 %collective-permute-done.2.refs_3_ = bf16[384,512]{1,0:T(8,128)(2,1)S(1)} collective-permute-done((bf16[384,512]{1,0:T(8,128)(2,1)S(1)}, bf16[384,512]{1,0:T(8,128)(2,1)S(1)}, u32[]{:S(2)}, u32[]{:S(2)}) %collective-permute-start.2) | collective-permute-done | bytes 393248 | tf_op jit(solution)/shard_map/ppermute | solution.py:30
  14.6 0.1 collective-permute-start.6
  14.7 0.5 %collective-permute-start.5 = (bf16[192,512]{1,0:T(8,128)(2,1)S(1)}, bf16[192,512]{1,0:T(8,128)(2,1)S(1)}, u32[]{:S(2)}, u32[]{:S(2)}) collective-permute-start(bf16[192,512]{1,0:T(8,128)(2,1)S(1)} %get-tuple-element.88), channel_id=1, source_target_pairs={{0,8},{8,0},{16,24},{24,16},{1,9},{9,1},{17,25},{25,17},{2,10},{10... | collective-permute-start | bytes 589832 | tf_op jit(solution)/shard_map/ppermute | solution.py:30
  15.2 2.1 %collective-permute-start = (bf16[256,512]{1,0:T(8,128)(2,1)S(1)}, bf16[256,512]{1,0:T(8,128)(2,1)S(1)}, u32[]{:S(2)}, u32[]{:S(2)}) collective-permute-start(bf16[256,512]{1,0:T(8,128)(2,1)S(1)} %get-tuple-element.50), channel_id=1, source_target_pairs={{0,1},{1,0},{2,3},{3,2},{4,5},{5,4},{6,7},{7,6},{8,9},{9,8},{10,11... | collective-permute-start | bytes 786440 | tf_op jit(solution)/shard_map/ppermute | solution.py:30
  17.3 0.0 collective-permute-start.8
  17.3 0.0 collective-permute-done.6.refs_5_
  17.3 0.0 collective-permute-done.5.refs_4_
  17.3 0.0 copy-done.2
  17.3 1.7 %project.1 = (bf16[512,512]{1,0:T(8,128)(2,1)S(1)}, bf16[512,512]{1,0:T(8,128)(2,1)S(1)}, bf16[512,512]{1,0:T(8,128)(2,1)S(1)}, bf16[512,512]{1,0:T(8,128)(2,1)S(1)}, bf16[512,512]{1,0:T(8,128)(2,1)S(1)}) custom-call(bf16[512,512]{1,0:T(8,128)(2,1)S(1)} %get-tuple-element.53.normed.refs_0_, bf16[512,512]{1,0:T(8,128)(2,1)S(1)} %context.1.refs_1_, ...), custom_call_target="tpu_custom_call" | custom-call | flops 10000000 | tf_op jit(solution)/shard_map/project/pallas_call | solution.py:282
  19.0 1.5 %attend.2.refs_3_ = bf16[256,512]{1,0:T(8,128)(2,1)S(1)} custom-call(s32[4,128]{1,0:T(4,128)S(1)} %get-tuple-element.52.refs_0_, bf16[512,512]{1,0:T(8,128)(2,1)S(1)} %get-tuple-element.68.refs_1_, bf16[512,512]{1,0:T(8,128)(2,1)S(1)} %get-tuple-element.69.refs_2_, bf16[512,512]{1,0:T(8,128)(2,1)S(1)} %get-tuple-element.70.refs_3_, ...), custom_call_target="tpu_custom_call" | custom-call | flops 500000000 | tf_op jit(solution)/shard_map/attend/pallas_call | solution.py:282
  20.4 0.0 collective-permute-done.1.refs_1_
  20.5 2.1 %collective-permute-start.9 = (bf16[256,512]{1,0:T(8,128)(2,1)S(1)}, bf16[256,512]{1,0:T(8,128)(2,1)S(1)}, u32[]{:S(2)}, u32[]{:S(2)}) collective-permute-start(bf16[256,512]{1,0:T(8,128)(2,1)S(1)} %collective-permute-done.1.refs_1_), channel_id=1, source_target_pairs={{0,2},{2,0},{4,6},{6,4},{1,3},{3,1},{5,7},{7,5},{8,10},{10,8},{12,... | collective-permute-start | bytes 786440 | tf_op jit(solution)/shard_map/ppermute | solution.py:30
  22.6 0.0 copy-start.3
  22.6 1.5 %attend.3.refs_4_ = bf16[256,512]{1,0:T(8,128)(2,1)S(1)} custom-call(s32[4,128]{1,0:T(4,128)S(1)} %get-tuple-element.52.refs_0_, bf16[512,512]{1,0:T(8,128)(2,1)S(1)} %get-tuple-element.68.refs_1_, bf16[512,512]{1,0:T(8,128)(2,1)S(1)} %get-tuple-element.69.refs_2_, bf16[512,512]{1,0:T(8,128)(2,1)S(1)} %get-tuple-element.70.refs_3_, ...), custom_call_target="tpu_custom_call" | custom-call | flops 500000000 | tf_op jit(solution)/shard_map/attend/pallas_call | solution.py:282
  24.1 0.0 copy-start
  24.1 0.0 copy-start.1
  24.1 1.7 %collective-permute-done = bf16[256,512]{1,0:T(8,128)(2,1)S(1)} collective-permute-done((bf16[256,512]{1,0:T(8,128)(2,1)S(1)}, bf16[256,512]{1,0:T(8,128)(2,1)S(1)}, u32[]{:S(2)}, u32[]{:S(2)}) %collective-permute-start) | collective-permute-done | bytes 262176 | tf_op jit(solution)/shard_map/ppermute | solution.py:30
  25.8 0.1 collective-permute-start.10
  25.9 2.1 %collective-permute-start.7 = (bf16[128,512]{1,0:T(8,128)(2,1)S(1)}, bf16[128,512]{1,0:T(8,128)(2,1)S(1)}, u32[]{:S(2)}, u32[]{:S(2)}) collective-permute-start(bf16[128,512]{1,0:T(8,128)(2,1)S(1)} %get-tuple-element.90.refs_2_), channel_id=1, source_target_pairs={{0,16},{8,24},{16,0},{24,8},{1,17},{9,25},{17,1},{25,9},{2,18},{10... | collective-permute-start | bytes 393224 | tf_op jit(solution)/shard_map/ppermute | solution.py:30
  28.0 0.2 collective-permute-start.11
  28.2 0.0 collective-permute-done.10.refs_6_
  28.2 0.0 copy-done.3
  28.2 0.7 %finish.1 = (f32[512,512]{1,0:T(8,128)S(1)}, bf16[512,512]{1,0:T(8,128)(2,1)S(1)}) custom-call(bf16[512,512]{1,0:T(8,128)(2,1)S(1)} %get-tuple-element.75.refs_0_, f32[1,512]{1,0:T(1,128)S(1)} %get-tuple-element.76.refs_1_, bf16[256,512]{1,0:T(8,128)(2,1)S(1)} %copy-done.3, bf16[256,512]{1,0:T(8,128)(2,1)S(1)} %attend.2.refs_3_, ...), custom_call_target="tpu_custom_call" | custom-call | flops 10000000 | tf_op jit(solution)/shard_map/finish/pallas_call | solution.py:282
  28.9 0.0 copy-done
  28.9 0.0 copy-done.1
  28.9 1.4 %feed.1.refs_0_ = f32[512,512]{1,0:T(8,128)S(1)} custom-call(f32[512,512]{1,0:T(8,128)S(1)} %get-tuple-element.79.start, bf16[512,512]{1,0:T(8,128)(2,1)S(1)} %get-tuple-element.80.second.refs_0_, bf16[1024,512]{1,0:T(8,128)(2,1)S(1)} %copy-done.1, bf16[1024,512]{1,0:T(8,128)(2,1)S(1)} %copy-done), custom_call_target="tpu_custom_call" | custom-call | flops 10000000 | tf_op jit(solution)/shard_map/feed/pallas_call | solution.py:282
  30.3 0.0 collective-permute-done.9.refs_3_
  30.3 0.4 %collective-permute-start.12 = (bf16[256,512]{1,0:T(8,128)(2,1)S(1)}, bf16[256,512]{1,0:T(8,128)(2,1)S(1)}, u32[]{:S(2)}, u32[]{:S(2)}) collective-permute-start(bf16[256,512]{1,0:T(8,128)(2,1)S(1)} %collective-permute-done.9.refs_3_), channel_id=1, source_target_pairs={{0,8},{8,0},{16,24},{24,16},{1,9},{9,1},{17,25},{25,17},{2,10},{10... | collective-permute-start | bytes 786440 | tf_op jit(solution)/shard_map/ppermute | solution.py:30
  30.7 0.0 collective-permute-done.8.refs_6_
  30.7 1.4 %collective-permute-done.7.refs_4_ = bf16[128,512]{1,0:T(8,128)(2,1)S(1)} collective-permute-done((bf16[128,512]{1,0:T(8,128)(2,1)S(1)}, bf16[128,512]{1,0:T(8,128)(2,1)S(1)}, u32[]{:S(2)}, u32[]{:S(2)}) %collective-permute-start.7) | collective-permute-done | bytes 131104 | tf_op jit(solution)/shard_map/ppermute | solution.py:30
  32.1 0.0 collective-permute-start.15
  32.1 0.5 %collective-permute-start.13 = (bf16[128,512]{1,0:T(8,128)(2,1)S(1)}, bf16[128,512]{1,0:T(8,128)(2,1)S(1)}, u32[]{:S(2)}, u32[]{:S(2)}) collective-permute-start(bf16[128,512]{1,0:T(8,128)(2,1)S(1)} %get-tuple-element.90.refs_2_), channel_id=1, source_target_pairs={{0,8},{8,0},{16,24},{24,16},{1,9},{9,1},{17,25},{25,17},{2,10},{10... | collective-permute-start | bytes 393224 | tf_op jit(solution)/shard_map/ppermute | solution.py:30
  32.6 0.0 collective-permute-start.14
  32.6 0.0 collective-permute-done.11.refs_2_
  32.6 0.0 collective-permute-done.12.refs_4_
  32.6 1.1 %hidden.1.refs_1_ = bf16[512,1024]{1,0:T(8,128)(2,1)S(1)} custom-call(bf16[512,512]{1,0:T(8,128)(2,1)S(1)} %get-tuple-element.80.second.refs_0_, bf16[256,512]{1,0:T(8,128)(2,1)S(1)} %collective-permute-done.1.refs_1_, bf16[256,512]{1,0:T(8,128)(2,1)S(1)} %collective-permute-done.11.refs_2_, bf16[256,512]{1,0:T(8,128)(2,1)S(1)} %collective-permute-done.9.refs_3_, ...), custom_call_target="tpu_custom_call" | custom-call | flops 10000000 | tf_op jit(solution)/shard_map/hidden/pallas_call | solution.py:282
  33.7 0.1 collective-permute-done.13.refs_3_
  33.8 0.2 collective-permute-done.14.refs_5_
  34.0 0.0 collective-permute-done.15.refs_7_
  34.0 1.7 %last.1 = bf16[512,512]{1,0:T(8,128)(2,1)} custom-call(f32[512,512]{1,0:T(8,128)S(1)} %feed.1.refs_0_, bf16[512,1024]{1,0:T(8,128)(2,1)S(1)} %hidden.1.refs_1_, bf16[128,512]{1,0:T(8,128)(2,1)S(1)} %get-tuple-element.90.refs_2_, bf16[128,512]{1,0:T(8,128)(2,1)S(1)} %collective-permute-done.13.refs_3_, bf16[128,512]{1,0:T(8,128)(2,1)S(1)} %collective-permute-done.7.refs_4_, ...), custom_call_target="tpu_custom_call" | custom-call | flops 10000000 | tf_op jit(solution)/shard_map/last/pallas_call | solution.py:282
  (2 shorter events, 0.0 us)
Async XLA Ops:
  1.6 13.0 %collective-permute-start.2 = (bf16[384,512]{1,0:T(8,128)(2,1)S(1)}, bf16[384,512]{1,0:T(8,128)(2,1)S(1)}, u32[]{:S(2)}, u32[]{:S(2)}) collective-permute-start(bf16[384,512]{1,0:T(8,128)(2,1)S(1)} %get-tuple-element.54), channel_id=1, source_target_pairs={{0,1},{1,0},{2,3},{3,2},{4,5},{5,4},{6,7},{7,6},{8,9},{9,8},{10,11... | collective-permute-start | bytes 1179656 | tf_op jit(solution)/shard_map/ppermute | solution.py:30
  4.6 4.4 %collective-permute-start.3 = (bf16[128,512]{1,0:T(8,128)(2,1)S(1)}, bf16[128,512]{1,0:T(8,128)(2,1)S(1)}, u32[]{:S(2)}, u32[]{:S(2)}) collective-permute-start(bf16[128,512]{1,0:T(8,128)(2,1)S(1)} %get-tuple-element.55), channel_id=1, source_target_pairs={{0,8},{8,16},{16,24},{24,0},{1,9},{9,17},{17,25},{25,1},{2,10},{10... | collective-permute-start | bytes 393224 | tf_op jit(solution)/shard_map/ppermute | solution.py:25
  4.6 7.5 %collective-permute-start.4 = (bf16[128,512]{1,0:T(8,128)(2,1)S(1)}, bf16[128,512]{1,0:T(8,128)(2,1)S(1)}, u32[]{:S(2)}, u32[]{:S(2)}) collective-permute-start(bf16[128,512]{1,0:T(8,128)(2,1)S(1)} %get-tuple-element.56), channel_id=1, source_target_pairs={{0,2},{2,4},{4,6},{6,0},{1,3},{3,5},{5,7},{7,1},{8,10},{10,12},{12... | collective-permute-start | bytes 393224 | tf_op jit(solution)/shard_map/ppermute | solution.py:25
  7.4 13.0 %collective-permute-start.1 = (bf16[256,512]{1,0:T(8,128)(2,1)S(1)}, bf16[256,512]{1,0:T(8,128)(2,1)S(1)}, u32[]{:S(2)}, u32[]{:S(2)}) collective-permute-start(bf16[256,512]{1,0:T(8,128)(2,1)S(1)} %get-tuple-element.51), channel_id=1, source_target_pairs={{0,1},{1,0},{2,3},{3,2},{4,5},{5,4},{6,7},{7,6},{8,9},{9,8},{10,11... | collective-permute-start | bytes 786440 | tf_op jit(solution)/shard_map/ppermute | solution.py:30
  12.2 5.1 %copy-start.2 = (bf16[768,512]{1,0:T(8,128)(2,1)S(1)}, bf16[768,512]{1,0:T(8,128)(2,1)}, u32[]{:S(2)}) copy-start(bf16[768,512]{1,0:T(8,128)(2,1)} %refs_2_.3) | copy-start | bytes 2359300
  14.6 2.7 %collective-permute-start.6 = (bf16[192,512]{1,0:T(8,128)(2,1)S(1)}, bf16[192,512]{1,0:T(8,128)(2,1)S(1)}, u32[]{:S(2)}, u32[]{:S(2)}) collective-permute-start(bf16[192,512]{1,0:T(8,128)(2,1)S(1)} %get-tuple-element.87), channel_id=1, source_target_pairs={{0,8},{8,0},{16,24},{24,16},{1,9},{9,1},{17,25},{25,17},{2,10},{10... | collective-permute-start | bytes 589832 | tf_op jit(solution)/shard_map/ppermute | solution.py:30
  14.7 2.6 %collective-permute-start.5 = (bf16[192,512]{1,0:T(8,128)(2,1)S(1)}, bf16[192,512]{1,0:T(8,128)(2,1)S(1)}, u32[]{:S(2)}, u32[]{:S(2)}) collective-permute-start(bf16[192,512]{1,0:T(8,128)(2,1)S(1)} %get-tuple-element.88), channel_id=1, source_target_pairs={{0,8},{8,0},{16,24},{24,16},{1,9},{9,1},{17,25},{25,17},{2,10},{10... | collective-permute-start | bytes 589832 | tf_op jit(solution)/shard_map/ppermute | solution.py:30
  15.2 10.6 %collective-permute-start = (bf16[256,512]{1,0:T(8,128)(2,1)S(1)}, bf16[256,512]{1,0:T(8,128)(2,1)S(1)}, u32[]{:S(2)}, u32[]{:S(2)}) collective-permute-start(bf16[256,512]{1,0:T(8,128)(2,1)S(1)} %get-tuple-element.50), channel_id=1, source_target_pairs={{0,1},{1,0},{2,3},{3,2},{4,5},{5,4},{6,7},{7,6},{8,9},{9,8},{10,11... | collective-permute-start | bytes 786440 | tf_op jit(solution)/shard_map/ppermute | solution.py:30
  17.3 13.5 %collective-permute-start.8 = (bf16[256,512]{1,0:T(8,128)(2,1)S(1)}, bf16[256,512]{1,0:T(8,128)(2,1)S(1)}, u32[]{:S(2)}, u32[]{:S(2)}) collective-permute-start(bf16[256,512]{1,0:T(8,128)(2,1)S(1)} %get-tuple-element.74), channel_id=1, source_target_pairs={{0,1},{1,0},{2,3},{3,2},{4,5},{5,4},{6,7},{7,6},{8,9},{9,8},{10,11... | collective-permute-start | bytes 786440 | tf_op jit(solution)/shard_map/ppermute | solution.py:30
  20.5 9.9 %collective-permute-start.9 = (bf16[256,512]{1,0:T(8,128)(2,1)S(1)}, bf16[256,512]{1,0:T(8,128)(2,1)S(1)}, u32[]{:S(2)}, u32[]{:S(2)}) collective-permute-start(bf16[256,512]{1,0:T(8,128)(2,1)S(1)} %collective-permute-done.1.refs_1_), channel_id=1, source_target_pairs={{0,2},{2,0},{4,6},{6,4},{1,3},{3,1},{5,7},{7,5},{8,10},{10,8},{12,... | collective-permute-start | bytes 786440 | tf_op jit(solution)/shard_map/ppermute | solution.py:30
  22.6 5.6 %copy-start.3 = (bf16[256,512]{1,0:T(8,128)(2,1)S(1)}, bf16[256,512]{1,0:T(8,128)(2,1)}, u32[]{:S(2)}) copy-start(bf16[256,512]{1,0:T(8,128)(2,1)} %refs_2_.4) | copy-start | bytes 786436
  24.1 4.9 %copy-start = (bf16[1024,512]{1,0:T(8,128)(2,1)S(1)}, bf16[1024,512]{1,0:T(8,128)(2,1)}, u32[]{:S(2)}) copy-start(bf16[1024,512]{1,0:T(8,128)(2,1)} %down.1) | copy-start | bytes 3145732
  24.1 4.9 %copy-start.1 = (bf16[1024,512]{1,0:T(8,128)(2,1)S(1)}, bf16[1024,512]{1,0:T(8,128)(2,1)}, u32[]{:S(2)}) copy-start(bf16[1024,512]{1,0:T(8,128)(2,1)} %into.1) | copy-start | bytes 3145732
  25.8 2.3 %collective-permute-start.10 = (bf16[128,512]{1,0:T(8,128)(2,1)S(1)}, bf16[128,512]{1,0:T(8,128)(2,1)S(1)}, u32[]{:S(2)}, u32[]{:S(2)}) collective-permute-start(bf16[128,512]{1,0:T(8,128)(2,1)S(1)} %get-tuple-element.89.refs_5_), channel_id=1, source_target_pairs={{0,8},{8,0},{16,24},{24,16},{1,9},{9,1},{17,25},{25,17},{2,10},{10... | collective-permute-start | bytes 393224 | tf_op jit(solution)/shard_map/ppermute | solution.py:30
  25.9 6.2 %collective-permute-start.7 = (bf16[128,512]{1,0:T(8,128)(2,1)S(1)}, bf16[128,512]{1,0:T(8,128)(2,1)S(1)}, u32[]{:S(2)}, u32[]{:S(2)}) collective-permute-start(bf16[128,512]{1,0:T(8,128)(2,1)S(1)} %get-tuple-element.90.refs_2_), channel_id=1, source_target_pairs={{0,16},{8,24},{16,0},{24,8},{1,17},{9,25},{17,1},{25,9},{2,18},{10... | collective-permute-start | bytes 393224 | tf_op jit(solution)/shard_map/ppermute | solution.py:30
  28.0 4.6 %collective-permute-start.11 = (bf16[256,512]{1,0:T(8,128)(2,1)S(1)}, bf16[256,512]{1,0:T(8,128)(2,1)S(1)}, u32[]{:S(2)}, u32[]{:S(2)}) collective-permute-start(bf16[256,512]{1,0:T(8,128)(2,1)S(1)} %collective-permute-done.1.refs_1_), channel_id=1, source_target_pairs={{0,8},{8,0},{16,24},{24,16},{1,9},{9,1},{17,25},{25,17},{2,10},{10... | collective-permute-start | bytes 786440 | tf_op jit(solution)/shard_map/ppermute | solution.py:30
  30.3 2.3 %collective-permute-start.12 = (bf16[256,512]{1,0:T(8,128)(2,1)S(1)}, bf16[256,512]{1,0:T(8,128)(2,1)S(1)}, u32[]{:S(2)}, u32[]{:S(2)}) collective-permute-start(bf16[256,512]{1,0:T(8,128)(2,1)S(1)} %collective-permute-done.9.refs_3_), channel_id=1, source_target_pairs={{0,8},{8,0},{16,24},{24,16},{1,9},{9,1},{17,25},{25,17},{2,10},{10... | collective-permute-start | bytes 786440 | tf_op jit(solution)/shard_map/ppermute | solution.py:30
  32.1 1.9 %collective-permute-start.15 = (bf16[256,512]{1,0:T(8,128)(2,1)S(1)}, bf16[256,512]{1,0:T(8,128)(2,1)S(1)}, u32[]{:S(2)}, u32[]{:S(2)}) collective-permute-start(bf16[256,512]{1,0:T(8,128)(2,1)S(1)} %collective-permute-done.8.refs_6_), channel_id=1, source_target_pairs={{0,8},{8,0},{16,24},{24,16},{1,9},{9,1},{17,25},{25,17},{2,10},{10... | collective-permute-start | bytes 786440 | tf_op jit(solution)/shard_map/ppermute | solution.py:30
  32.1 1.7 %collective-permute-start.13 = (bf16[128,512]{1,0:T(8,128)(2,1)S(1)}, bf16[128,512]{1,0:T(8,128)(2,1)S(1)}, u32[]{:S(2)}, u32[]{:S(2)}) collective-permute-start(bf16[128,512]{1,0:T(8,128)(2,1)S(1)} %get-tuple-element.90.refs_2_), channel_id=1, source_target_pairs={{0,8},{8,0},{16,24},{24,16},{1,9},{9,1},{17,25},{25,17},{2,10},{10... | collective-permute-start | bytes 393224 | tf_op jit(solution)/shard_map/ppermute | solution.py:30
  32.6 1.4 %collective-permute-start.14 = (bf16[128,512]{1,0:T(8,128)(2,1)S(1)}, bf16[128,512]{1,0:T(8,128)(2,1)S(1)}, u32[]{:S(2)}, u32[]{:S(2)}) collective-permute-start(bf16[128,512]{1,0:T(8,128)(2,1)S(1)} %collective-permute-done.7.refs_4_), channel_id=1, source_target_pairs={{0,8},{8,0},{16,24},{24,16},{1,9},{9,1},{17,25},{25,17},{2,10},{10... | collective-permute-start | bytes 393224 | tf_op jit(solution)/shard_map/ppermute | solution.py:30

commit v4 on v3

--- a/solution.py
+++ b/solution.py
@@ -67,12 +67,19 @@
     return jnp.where(lax.axis_index(axis) > 0, halo[...].astype(jnp.float32), 0.0)
 
 
-def context_kernel(normed, halo_x, halo_y, gain, context, chosen):
+def context_kernel(normed, halo_x, halo_y, gain, context, into, down, chosen, held_into, held_down, sems):
+    copies = [
+        pltpu.make_async_copy(into, held_into, sems.at[0]), pltpu.make_async_copy(down, held_down, sems.at[1])
+    ]
+    for copy in copies:
+        copy.start()
     parts = [layer_norm(present(halo_x, "gx"), gain[...]), layer_norm(present(halo_y, "gy"), gain[...])]
     pool = jnp.concatenate([normed[...]] + parts, axis=0)
     for window in range(context.shape[0]):
         picked = dot_nn(pick_rows(context[pl.ds(window, 1), :], pool.shape[0]), pool)
         chosen[pl.ds(window * CTX, CTX), :] = picked.astype(jnp.bfloat16)
+    for copy in copies:
+        copy.wait()
 
 
 class Share(typing.NamedTuple):
@@ -252,6 +259,10 @@
     output[...] = add(*waiting.pop(0)).astype(output.dtype)
 
 
+def add_kernel(plan, start, hidden, piece, output):
+    output[...] = start[...] + dot_nn(hidden[:, columns_of(plan, 0, piece)], piece[...])
+
+
 def last_kernel(plan, start, hidden, *refs):
     pieces, output, held, sems = refs[: len(plan)], refs[-3], refs[-2], refs[-1]
     blocks = start.shape[0] // WIN
@@ -268,7 +279,7 @@
         copy.wait()
 
 
-COSTS = {"norm": 1, "slices": 1, "prepare": 1, "context": 1, "project": 1, "attend": 50, "finish": 1, "feed": 1, "hidden": 1, "last": 1}
+COSTS = {"norm": 1, "slices": 1, "prepare": 1, "context": 1, "project": 20, "attend": 1, "finish": 1, "feed": 1, "hidden": 60, "add": 1, "last": 1}
 
 
 def call(kernel, outs, operands, name, scratch=(), specs=None, result=VMEM):
@@ -312,13 +323,11 @@
         filled = jnp.broadcast_to(lengths[:, None], context.shape)
     else:
         qkv, out, into, down = w_qkv, w_out, w_in, w_down
-        size = qkv.shape[0] // 2
-        share_qkv = Share(0, "core", size, size)
+        size = qkv.shape[0] // 4
+        share_qkv = Share(0, "gx", size, size)
         share_out = Share(0, "core", out.shape[0] // 2, out.shape[0] // 2)
         share_in = Share(0, "gy", into.shape[0] // 4, into.shape[0] // 4)
-        size = down.shape[0] // 8
-        share_early = Share(0, "gx", size, size)
-        share_late = Share(4 * size, "core", 2 * size, 2 * size)
+        share_down = Share(0, "core", down.shape[0] // 2, down.shape[0] // 2)
         tokens, gain_one, gain_two, context, filled, out_x, out_y, normed, part_qkv = call(
             lambda *refs: prepare_kernel([share_qkv], *refs),
             [
@@ -334,14 +343,14 @@
             [HBM] * 8,
         )
         y_qkv = swap(part_qkv, "fsdp", 1)
-        groups = [[share_in], [share_out, share_early], [share_late]]
+        groups = [[share_in, share_out], [share_down]]
         later, normed = after(((w_in, w_out, w_down), normed))
         parts = call(
             lambda *refs: slice_kernel(groups, *refs),
             [struct(sum(share.rows for share in group), width) for group in groups],
-            (later[0], later[1], later[2], later[2]), "slices", [pltpu.SemaphoreType.DMA((4,))], [HBM] * 4,
+            later, "slices", [pltpu.SemaphoreType.DMA((3,))], [HBM] * 3,
         )
-        y_in, y_middle, y_late = (swap(part, "fsdp", 1) for part in parts)
+        y_middle, y_down = (swap(part, "fsdp", 1) for part in parts)
 
     def crossed(share, near, flip=0):
         return [(share, flip, near), (share, flip + 1, swap(near, "gx", 1))]
@@ -354,20 +363,31 @@
 
     halo_x = ring(out_x, "gx")
     halo_y = ring(out_y, "gy")
-    (chosen,) = call(context_kernel, [struct(rows, width)], (normed, halo_x, halo_y, gain_one, context), "context")
+    chosen, into, down = call(
+        context_kernel, [struct(rows, width), struct(*into.shape), struct(*down.shape)],
+        (normed, halo_x, halo_y, gain_one, context, into, down), "context",
+        [pltpu.SemaphoreType.DMA((2,))], [VMEM] * 5 + [HBM] * 2,
+    )
     if paired:
-        y_qkv, chosen = after((y_qkv, chosen))
+        size = share_qkv.rows // 2
+        x_qkv = [swap(y_qkv[low : low + size], "gx", 2) for low in range(0, share_qkv.rows, size)]
+        x_qkv, chosen = after((x_qkv, chosen))
     pieces = []
     if paired:
-        pieces.append((share_qkv, 0, y_qkv))
-        size = share_qkv.rows // 2
-        for low in range(0, share_qkv.rows, size):
-            share = share_qkv._replace(base=low, rows=size)
-            pieces.append((share, 1, swap(y_qkv[low : low + size], "gx", 1)))
+        pieces = crossed(share_qkv, y_qkv)
+        for number, piece in enumerate(x_qkv):
+            pieces += crossed(share_qkv._replace(base=number * size, rows=size), piece, 2)
     projected = call(
         lambda *refs, plan=plan(pieces): project_kernel(plan, *refs), [struct(rows, width)] * 5,
         (normed, chosen, qkv, *arrays(pieces)), "project", [pltpu.VMEM((3 * width, width), jnp.bfloat16)],
     )
+
+    if paired:
+        y_middle, projected = after((y_middle, projected))
+        y_in, y_out = y_middle[: share_in.rows], y_middle[share_in.rows :]
+        size = share_in.rows // 2
+        z_in = [swap(y_in[low : low + size], "gy", 1) for low in range(0, share_in.rows, size)]
+        projected, y_in, y_out = after((projected, y_in, y_out))
 
     def attend(windows):
         return call(
@@ -379,16 +399,9 @@
     half = len(windows) // 2
     mixed = attend(windows[:half])
     pieces_out, pieces_in, pieces_down, pieces_last = [], [], [], []
-    if paired:
-        y_in, mixed = after((y_in, mixed))
-        z_in = swap(y_in, "gy", 1)
-        projected, y_in = after((projected, y_in))
     mixed += attend(windows[half:])
     if paired:
-        y_middle, mixed = after((y_middle, mixed))
-        y_out, y_early = y_middle[: share_out.rows], y_middle[share_out.rows :]
         pieces_out = crossed(share_out, y_out)
-        x_early = swap(y_early, "gx", 2)
     middle, second = call(
         lambda *refs: finish_kernel(len(mixed), plan(pieces_out), *refs),
         [struct(rows, width, jnp.float32), struct(rows, width)], (tokens, gain_two, out, *mixed, *arrays(pieces_out)),
@@ -401,23 +414,26 @@
     if not paired:
         return total
     z_in, total = after((z_in, total))
-    pieces = crossed(share_in, y_in) + crossed(share_in, z_in, 2)
+    pieces = crossed(share_in, y_in)
+    size = share_in.rows // 2
+    for number, piece in enumerate(z_in):
+        pieces += crossed(share_in._replace(base=number * size, rows=size), piece, 2)
+    held, y_down = after((arrays(pieces), y_down))
     (hidden,) = call(
-        lambda *refs, plan=plan(pieces): hidden_kernel(plan, *refs), [struct(rows, into.shape[0])],
-        (second, *arrays(pieces)), "hidden",
-    )
-    LATE = 0
-    if LATE == 0:
-        x_early, y_late, total = after((x_early, y_late, total))
-    elif LATE == 1:
-        x_early, y_late, hidden = after((x_early, y_late, hidden))
-    else:
-        y_late, total = after((y_late, total))
-        x_early, hidden = after((x_early, hidden))
-    pieces = crossed(share_early, y_early) + crossed(share_early, x_early, 2) + crossed(share_late, y_late)
+        lambda *refs, plan=plan(pieces): hidden_kernel(plan, *refs), [struct(rows, into.shape[0])], (second, *held), "hidden",
+    )
+    size = share_down.rows // 1
+    halves = [
+        (share_down._replace(base=low, rows=size), 1, swap(y_down[low : low + size], "gx", 1))
+        for low in range(0, share_down.rows, size)
+    ]
+    (total,) = call(
+        lambda *refs: add_kernel([(share_down, 0)], *refs), [struct(rows, width, jnp.float32)],
+        (total, hidden, y_down), "add",
+    )
     return call(
-        lambda *refs: last_kernel(plan(pieces), *refs), [struct(rows, width)],
-        (total, hidden, *arrays(pieces)), "last",
+        lambda *refs: last_kernel(plan(halves), *refs), [struct(rows, width)],
+        (total, hidden, *arrays(halves)), "last",
         [pltpu.VMEM((rows, width), jnp.bfloat16), pltpu.SemaphoreType.DMA((rows // WIN,))], result=HBM,
     )[0]
 

time: 35.9 us -> 34 us (0.947)
  waiting for transfers between devices: 9.18 us -> 6.98 us
  Pallas kernels: 13.1 us -> 14.4 us
  starting transfers between devices: 13.2 us -> 12.3 us
    ppermute x2, waiting for transfers between devices: 4.16 us -> 0.5 us  [ring(): lax.ppermute(value, axis, [(source, (source + 1) % count) for source in r...]
    ppermute x14 -> x15, waiting for transfers between devices: 5.02 us -> 6.48 us  [swap(): lax.ppermute(value, axis, [(source, source ^ bit) for source in range(cou...]
    pallas_call x10 -> x11, Pallas kernels: 13.1 us -> 14.4 us  [call(): pl.pallas_call(kernel, out_shape=tuple(outs), in_specs=specs, out_specs=t...]
    ppermute x14 -> x15, starting transfers between devices: 11.6 us -> 10.7 us  [swap(): lax.ppermute(value, axis, [(source, source ^ bit) for source in range(cou...]
  transfers between devices with their start and end apart: 16 -> 17, of which waited for: 7 -> 7; matrix products, arithmetic and copies ran while one was open for 0% -> 0% of each run, Pallas kernels for 27% -> 34%
where the time goes in v4:
time: 34 us; the launch traced here: 33.9 us
  Pallas kernels  14.4 us (42%)
  starting transfers between devices  12.3 us (36%)
  waiting for transfers between devices  6.98 us (21%)
    pallas_call x11, Pallas kernels, call(): pl.pallas_call(kernel, out_shape=tuple(outs), in_specs=specs, out_specs=t...  14.4 us
    ppermute x15, starting transfers between devices, swap(): lax.ppermute(value, axis, [(source, source ^ bit) for source in range(cou...  10.7 us
    ppermute x15, waiting for transfers between devices, swap(): lax.ppermute(value, axis, [(source, source ^ bit) for source in range(cou...  6.48 us
    ppermute x2, starting transfers between devices, ring(): lax.ppermute(value, axis, [(source, (source + 1) % count) for source in r...  1.58 us
  transfers between devices with their start and end apart: 17, of which 7 were waited for; matrix products, arithmetic and copies ran while one was open for 0% of the time, Pallas kernels for 34%

profile of v4, /device:TPU:0, one launch (start us, length us, event | category | flops | bytes accessed | tf_op | source)
XLA Modules:
  0.0 33.9 jit_solution(17238051326579016517)
XLA Ops:
  0.0 1.6 %prepare.1 = (bf16[512,512]{1,0:T(8,128)(2,1)S(1)}, f32[1,512]{1,0:T(1,128)S(1)}, f32[1,512]{1,0:T(1,128)S(1)}, s32[4,128]{1,0:T(4,128)S(1)}, s32[4,128]{1,0:T(4...) custom-call(bf16[512,512]{1,0:T(8,128)(2,1)} %refs_0_.1, ...), custom_call_target="tpu_custom_call" | custom-call | flops 10000000 | tf_op jit(solution)/shard_map/prepare/pallas_call | solution.py:293
  1.6 3.0 %collective-permute-start.1 = (bf16[192,512]{1,0:T(8,128)(2,1)S(1)}, bf16[192,512]{1,0:T(8,128)(2,1)S(1)}, u32[]{:S(2)}, u32[]{:S(2)}) collective-permute-start(bf16[192,512]{1,0:T(8,128)(2,1)S(1)} %get-tuple-element.62), channel_id=1, source_target_pairs={{0,1},{1,0},{2,3},{3,2},{4,5},{5,4},{6,7},{7,6},{8,9},{9,8},{10,11... | collective-permute-start | bytes 589832 | tf_op jit(solution)/shard_map/ppermute | solution.py:30
  4.6 0.0 collective-permute-start.4
  4.6 1.6 %collective-permute-start.5 = (bf16[128,512]{1,0:T(8,128)(2,1)S(1)}, bf16[128,512]{1,0:T(8,128)(2,1)S(1)}, u32[]{:S(2)}, u32[]{:S(2)}) collective-permute-start(bf16[128,512]{1,0:T(8,128)(2,1)S(1)} %get-tuple-element.64), channel_id=1, source_target_pairs={{0,2},{2,4},{4,6},{6,0},{1,3},{3,5},{5,7},{7,1},{8,10},{10,12},{12... | collective-permute-start | bytes 393224 | tf_op jit(solution)/shard_map/ppermute | solution.py:25
  6.2 1.2 %slices.1 = (bf16[384,512]{1,0:T(8,128)(2,1)S(1)}, bf16[512,512]{1,0:T(8,128)(2,1)S(1)}) custom-call(bf16[1024,512]{1,0:T(8,128)(2,1)} %into.1, bf16[256,512]{1,0:T(8,128)(2,1)} %refs_2_.4, bf16[1024,512]{1,0:T(8,128)(2,1)} %down.1), custom_call_target="tpu_custom_call" | custom-call | flops 10000000 | tf_op jit(solution)/shard_map/slices/pallas_call | solution.py:293
  7.4 0.6 %collective-permute-start = (bf16[384,512]{1,0:T(8,128)(2,1)S(1)}, bf16[384,512]{1,0:T(8,128)(2,1)S(1)}, u32[]{:S(2)}, u32[]{:S(2)}) collective-permute-start(bf16[384,512]{1,0:T(8,128)(2,1)S(1)} %get-tuple-element.60), channel_id=1, source_target_pairs={{0,1},{1,0},{2,3},{3,2},{4,5},{5,4},{6,7},{7,6},{8,9},{9,8},{10,11... | collective-permute-start | bytes 1179656 | tf_op jit(solution)/shard_map/ppermute | solution.py:30
  8.0 1.5 %collective-permute-done.1.refs_3_ = bf16[192,512]{1,0:T(8,128)(2,1)S(1)} collective-permute-done((bf16[192,512]{1,0:T(8,128)(2,1)S(1)}, bf16[192,512]{1,0:T(8,128)(2,1)S(1)}, u32[]{:S(2)}, u32[]{:S(2)}) %collective-permute-start.1) | collective-permute-done | bytes 196640 | tf_op jit(solution)/shard_map/ppermute | solution.py:30
  9.6 1.8 %collective-permute-start.2 = (bf16[96,512]{1,0:T(8,128)(2,1)S(1)}, bf16[96,512]{1,0:T(8,128)(2,1)S(1)}, u32[]{:S(2)}, u32[]{:S(2)}) collective-permute-start(bf16[96,512]{1,0:T(8,128)(2,1)S(1)} %get-tuple-element.111), channel_id=1, source_target_pairs={{0,16},{8,24},{16,0},{24,8},{1,17},{9,25},{17,1},{25,9},{2,18},{10... | collective-permute-start | bytes 294920 | tf_op jit(solution)/shard_map/ppermute | solution.py:30
  11.3 0.3 collective-permute-start.3
  11.7 0.0 collective-permute-done.4.halo_x
  11.7 0.0 collective-permute-start.6
  11.7 0.5 %collective-permute-done.5.halo_y = bf16[128,512]{1,0:T(8,128)(2,1)S(1)} collective-permute-done((bf16[128,512]{1,0:T(8,128)(2,1)S(1)}, bf16[128,512]{1,0:T(8,128)(2,1)S(1)}, u32[]{:S(2)}, u32[]{:S(2)}) %collective-permute-start.5) | collective-permute-done | bytes 131104 | tf_op jit(solution)/shard_map/ppermute | solution.py:25
  12.2 0.0 copy-start
  12.2 2.0 %context.1 = (bf16[512,512]{1,0:T(8,128)(2,1)S(1)}, bf16[1024,512]{1,0:T(8,128)(2,1)S(1)}, bf16[1024,512]{1,0:T(8,128)(2,1)S(1)}) custom-call(bf16[512,512]{1,0:T(8,128)(2,1)S(1)} %get-tuple-element.61.normed.refs_0_, bf16[128,512]{1,0:T(8,128)(2,1)S(1)} %collective-permute-done.4.halo_x, bf16[128,512]{1,0:T(8,128)(2,1)S(1)} %collective-permute-done.5.halo_y, ...), custom_call_target="tpu_custom_call" | custom-call | flops 10000000 | tf_op jit(solution)/shard_map/context/pallas_call | solution.py:293
  14.2 0.7 %collective-permute-done.2.refs_5_ = bf16[96,512]{1,0:T(8,128)(2,1)S(1)} collective-permute-done((bf16[96,512]{1,0:T(8,128)(2,1)S(1)}, bf16[96,512]{1,0:T(8,128)(2,1)S(1)}, u32[]{:S(2)}, u32[]{:S(2)}) %collective-permute-start.2) | collective-permute-done | bytes 98336 | tf_op jit(solution)/shard_map/ppermute | solution.py:30
  14.9 1.1 %collective-permute-done.3.refs_7_ = bf16[96,512]{1,0:T(8,128)(2,1)S(1)} collective-permute-done((bf16[96,512]{1,0:T(8,128)(2,1)S(1)}, bf16[96,512]{1,0:T(8,128)(2,1)S(1)}, u32[]{:S(2)}, u32[]{:S(2)}) %collective-permute-start.3) | collective-permute-done | bytes 98336 | tf_op jit(solution)/shard_map/ppermute | solution.py:30
  16.0 0.0 collective-permute-start.7
  16.0 0.5 %collective-permute-start.8 = (bf16[96,512]{1,0:T(8,128)(2,1)S(1)}, bf16[96,512]{1,0:T(8,128)(2,1)S(1)}, u32[]{:S(2)}, u32[]{:S(2)}) collective-permute-start(bf16[96,512]{1,0:T(8,128)(2,1)S(1)} %collective-permute-done.3.refs_7_), channel_id=1, source_target_pairs={{0,8},{8,0},{16,24},{24,16},{1,9},{9,1},{17,25},{25,17},{2,10},{10... | collective-permute-start | bytes 294920 | tf_op jit(solution)/shard_map/ppermute | solution.py:30
  16.5 1.8 %collective-permute-start.15 = (bf16[512,512]{1,0:T(8,128)(2,1)S(1)}, bf16[512,512]{1,0:T(8,128)(2,1)S(1)}, u32[]{:S(2)}, u32[]{:S(2)}) collective-permute-start(bf16[512,512]{1,0:T(8,128)(2,1)S(1)} %get-tuple-element.99), channel_id=1, source_target_pairs={{0,1},{1,0},{2,3},{3,2},{4,5},{5,4},{6,7},{7,6},{8,9},{9,8},{10,11... | collective-permute-start | bytes 1572872 | tf_op jit(solution)/shard_map/ppermute | solution.py:30
  18.2 0.0 collective-permute-done.7.refs_6_
  18.2 0.0 collective-permute-done.8.refs_8_
  18.2 0.0 collective-permute-done.6.refs_4_
  18.2 0.0 copy-done
  18.3 1.6 %project.1 = (bf16[512,512]{1,0:T(8,128)(2,1)S(1)}, bf16[512,512]{1,0:T(8,128)(2,1)S(1)}, bf16[512,512]{1,0:T(8,128)(2,1)S(1)}, bf16[512,512]{1,0:T(8,128)(2,1)S(1)}, bf16[512,512]{1,0:T(8,128)(2,1)S(1)}) custom-call(bf16[512,512]{1,0:T(8,128)(2,1)S(1)} %get-tuple-element.61.normed.refs_0_, bf16[512,512]{1,0:T(8,128)(2,1)S(1)} %get-tuple-element.68.refs_1_, ...), custom_call_target="tpu_custom_call" | custom-call | flops 200000000 | tf_op jit(solution)/shard_map/project/pallas_call | solution.py:293
  19.9 0.0 collective-permute-done
  20.0 0.1 collective-permute-start.11
  20.1 1.7 %collective-permute-start.10 = (bf16[128,512]{1,0:T(8,128)(2,1)S(1)}, bf16[128,512]{1,0:T(8,128)(2,1)S(1)}, u32[]{:S(2)}, u32[]{:S(2)}) collective-permute-start(bf16[128,512]{1,0:T(8,128)(2,1)S(1)} %get-tuple-element.108), channel_id=1, source_target_pairs={{0,2},{2,0},{4,6},{6,4},{1,3},{3,1},{5,7},{7,5},{8,10},{10,8},{12,... | collective-permute-start | bytes 393224 | tf_op jit(solution)/shard_map/ppermute | solution.py:30
  21.7 0.4 %collective-permute-start.9 = (bf16[128,512]{1,0:T(8,128)(2,1)S(1)}, bf16[128,512]{1,0:T(8,128)(2,1)S(1)}, u32[]{:S(2)}, u32[]{:S(2)}) collective-permute-start(bf16[128,512]{1,0:T(8,128)(2,1)S(1)} %get-tuple-element.109), channel_id=1, source_target_pairs={{0,2},{2,0},{4,6},{6,4},{1,3},{3,1},{5,7},{7,5},{8,10},{10,8},{12,... | collective-permute-start | bytes 393224 | tf_op jit(solution)/shard_map/ppermute | solution.py:30
  22.2 0.0 collective-permute-start.12
  22.2 1.5 %attend.3.refs_4_ = bf16[256,512]{1,0:T(8,128)(2,1)S(1)} custom-call(s32[4,128]{1,0:T(4,128)S(1)} %get-tuple-element.79.refs_0_, bf16[512,512]{1,0:T(8,128)(2,1)S(1)} %get-tuple-element.85.refs_1_, bf16[512,512]{1,0:T(8,128)(2,1)S(1)} %get-tuple-element.86.refs_2_, bf16[512,512]{1,0:T(8,128)(2,1)S(1)} %get-tuple-element.87.refs_3_, ...), custom_call_target="tpu_custom_call" | custom-call | flops 10000000 | tf_op jit(solution)/shard_map/attend/pallas_call | solution.py:293
  23.7 0.0 copy-start.1
  23.7 1.5 %attend.2.refs_3_ = bf16[256,512]{1,0:T(8,128)(2,1)S(1)} custom-call(s32[4,128]{1,0:T(4,128)S(1)} %get-tuple-element.79.refs_0_, bf16[512,512]{1,0:T(8,128)(2,1)S(1)} %get-tuple-element.85.refs_1_, bf16[512,512]{1,0:T(8,128)(2,1)S(1)} %get-tuple-element.86.refs_2_, bf16[512,512]{1,0:T(8,128)(2,1)S(1)} %get-tuple-element.87.refs_3_, ...), custom_call_target="tpu_custom_call" | custom-call | flops 10000000 | tf_op jit(solution)/shard_map/attend/pallas_call | solution.py:293
  25.1 0.0 collective-permute-done.11.refs_6_
  25.2 0.0 copy-done.1
  25.2 0.7 %finish.1 = (f32[512,512]{1,0:T(8,128)S(1)}, bf16[512,512]{1,0:T(8,128)(2,1)S(1)}) custom-call(bf16[512,512]{1,0:T(8,128)(2,1)S(1)} %get-tuple-element.77.refs_0_, f32[1,512]{1,0:T(1,128)S(1)} %get-tuple-element.78.refs_1_, bf16[256,512]{1,0:T(8,128)(2,1)S(1)} %copy-done.1, bf16[256,512]{1,0:T(8,128)(2,1)S(1)} %attend.2.refs_3_, ...), custom_call_target="tpu_custom_call" | custom-call | flops 10000000 | tf_op jit(solution)/shard_map/finish/pallas_call | solution.py:293
  25.9 1.4 %feed.1.refs_0_ = f32[512,512]{1,0:T(8,128)S(1)} custom-call(f32[512,512]{1,0:T(8,128)S(1)} %get-tuple-element.91.start, bf16[512,512]{1,0:T(8,128)(2,1)S(1)} %get-tuple-element.92.second.refs_0_, bf16[1024,512]{1,0:T(8,128)(2,1)S(1)} %get-tuple-element.93.into, bf16[1024,512]{1,0:T(8,128)(2,1)S(1)} %get-tuple-element.94.down), custom_call_target="tpu_custom_call" | custom-call | flops 10000000 | tf_op jit(solution)/shard_map/feed/pallas_call | solution.py:293
  27.3 0.0 collective-permute-done.10.refs_5_
  27.3 1.5 %collective-permute-done.9.refs_3_ = bf16[128,512]{1,0:T(8,128)(2,1)S(1)} collective-permute-done((bf16[128,512]{1,0:T(8,128)(2,1)S(1)}, bf16[128,512]{1,0:T(8,128)(2,1)S(1)}, u32[]{:S(2)}, u32[]{:S(2)}) %collective-permute-start.9) | collective-permute-done | bytes 131104 | tf_op jit(solution)/shard_map/ppermute | solution.py:30
  28.8 0.0 collective-permute-start.13
  28.8 0.5 %collective-permute-start.14 = (bf16[128,512]{1,0:T(8,128)(2,1)S(1)}, bf16[128,512]{1,0:T(8,128)(2,1)S(1)}, u32[]{:S(2)}, u32[]{:S(2)}) collective-permute-start(bf16[128,512]{1,0:T(8,128)(2,1)S(1)} %collective-permute-done.10.refs_5_), channel_id=1, source_target_pairs={{0,8},{8,0},{16,24},{24,16},{1,9},{9,1},{17,25},{25,17},{2,10},{10... | collective-permute-start | bytes 393224 | tf_op jit(solution)/shard_map/ppermute | solution.py:30
  29.3 1.4 %collective-permute-done.15.refs_2_ = bf16[512,512]{1,0:T(8,128)(2,1)S(1)} collective-permute-done((bf16[512,512]{1,0:T(8,128)(2,1)S(1)}, bf16[512,512]{1,0:T(8,128)(2,1)S(1)}, u32[]{:S(2)}, u32[]{:S(2)}) %collective-permute-start.15) | collective-permute-done | bytes 524320 | tf_op jit(solution)/shard_map/ppermute | solution.py:30
  30.7 0.0 collective-permute-done.13.refs_4_
  30.7 0.0 collective-permute-done.14.refs_6_
  30.7 0.0 collective-permute-done.12.refs_2_
  30.8 0.1 collective-permute-start.16
  30.8 1.3 %hidden.1.refs_1_ = bf16[512,1024]{1,0:T(8,128)(2,1)S(1)} custom-call(bf16[512,512]{1,0:T(8,128)(2,1)S(1)} %get-tuple-element.92.second.refs_0_, bf16[256,512]{1,0:T(8,128)(2,1)S(1)} %slice.24.refs_1_, bf16[256,512]{1,0:T(8,128)(2,1)S(1)} %collective-permute-done.12.refs_2_, bf16[128,512]{1,0:T(8,128)(2,1)S(1)} %collective-permute-done.9.refs_3_, ...), custom_call_target="tpu_custom_call" | custom-call | flops 600000000 | tf_op jit(solution)/shard_map/hidden/pallas_call | solution.py:293
  32.1 0.4 %add.1.refs_0_ = f32[512,512]{1,0:T(8,128)S(1)} custom-call(f32[512,512]{1,0:T(8,128)S(1)} %feed.1.refs_0_, bf16[512,1024]{1,0:T(8,128)(2,1)S(1)} %hidden.1.refs_1_, bf16[512,512]{1,0:T(8,128)(2,1)S(1)} %collective-permute-done.15.refs_2_), custom_call_target="tpu_custom_call" | custom-call | flops 10000000 | tf_op jit(solution)/shard_map/add/pallas_call | solution.py:293
  32.5 0.2 collective-permute-done.16.refs_2_
  32.7 1.1 %last.1 = bf16[512,512]{1,0:T(8,128)(2,1)} custom-call(f32[512,512]{1,0:T(8,128)S(1)} %add.1.refs_0_, bf16[512,1024]{1,0:T(8,128)(2,1)S(1)} %hidden.1.refs_1_, bf16[512,512]{1,0:T(8,128)(2,1)S(1)} %collective-permute-done.16.refs_2_), custom_call_target="tpu_custom_call" | custom-call | flops 10000000 | tf_op jit(solution)/shard_map/last/pallas_call | solution.py:293
  (3 shorter events, 0.1 us)
Async XLA Ops:
  1.6 7.9 %collective-permute-start.1 = (bf16[192,512]{1,0:T(8,128)(2,1)S(1)}, bf16[192,512]{1,0:T(8,128)(2,1)S(1)}, u32[]{:S(2)}, u32[]{:S(2)}) collective-permute-start(bf16[192,512]{1,0:T(8,128)(2,1)S(1)} %get-tuple-element.62), channel_id=1, source_target_pairs={{0,1},{1,0},{2,3},{3,2},{4,5},{5,4},{6,7},{7,6},{8,9},{9,8},{10,11... | collective-permute-start | bytes 589832 | tf_op jit(solution)/shard_map/ppermute | solution.py:30
  4.6 7.0 %collective-permute-start.4 = (bf16[128,512]{1,0:T(8,128)(2,1)S(1)}, bf16[128,512]{1,0:T(8,128)(2,1)S(1)}, u32[]{:S(2)}, u32[]{:S(2)}) collective-permute-start(bf16[128,512]{1,0:T(8,128)(2,1)S(1)} %get-tuple-element.63), channel_id=1, source_target_pairs={{0,8},{8,16},{16,24},{24,0},{1,9},{9,17},{17,25},{25,1},{2,10},{10... | collective-permute-start | bytes 393224 | tf_op jit(solution)/shard_map/ppermute | solution.py:25
  4.6 7.5 %collective-permute-start.5 = (bf16[128,512]{1,0:T(8,128)(2,1)S(1)}, bf16[128,512]{1,0:T(8,128)(2,1)S(1)}, u32[]{:S(2)}, u32[]{:S(2)}) collective-permute-start(bf16[128,512]{1,0:T(8,128)(2,1)S(1)} %get-tuple-element.64), channel_id=1, source_target_pairs={{0,2},{2,4},{4,6},{6,0},{1,3},{3,5},{5,7},{7,1},{8,10},{10,12},{12... | collective-permute-start | bytes 393224 | tf_op jit(solution)/shard_map/ppermute | solution.py:25
  7.4 12.5 %collective-permute-start = (bf16[384,512]{1,0:T(8,128)(2,1)S(1)}, bf16[384,512]{1,0:T(8,128)(2,1)S(1)}, u32[]{:S(2)}, u32[]{:S(2)}) collective-permute-start(bf16[384,512]{1,0:T(8,128)(2,1)S(1)} %get-tuple-element.60), channel_id=1, source_target_pairs={{0,1},{1,0},{2,3},{3,2},{4,5},{5,4},{6,7},{7,6},{8,9},{9,8},{10,11... | collective-permute-start | bytes 1179656 | tf_op jit(solution)/shard_map/ppermute | solution.py:30
  9.6 5.3 %collective-permute-start.2 = (bf16[96,512]{1,0:T(8,128)(2,1)S(1)}, bf16[96,512]{1,0:T(8,128)(2,1)S(1)}, u32[]{:S(2)}, u32[]{:S(2)}) collective-permute-start(bf16[96,512]{1,0:T(8,128)(2,1)S(1)} %get-tuple-element.111), channel_id=1, source_target_pairs={{0,16},{8,24},{16,0},{24,8},{1,17},{9,25},{17,1},{25,9},{2,18},{10... | collective-permute-start | bytes 294920 | tf_op jit(solution)/shard_map/ppermute | solution.py:30
  11.3 4.6 %collective-permute-start.3 = (bf16[96,512]{1,0:T(8,128)(2,1)S(1)}, bf16[96,512]{1,0:T(8,128)(2,1)S(1)}, u32[]{:S(2)}, u32[]{:S(2)}) collective-permute-start(bf16[96,512]{1,0:T(8,128)(2,1)S(1)} %get-tuple-element.110), channel_id=1, source_target_pairs={{0,16},{8,24},{16,0},{24,8},{1,17},{9,25},{17,1},{25,9},{2,18},{10... | collective-permute-start | bytes 294920 | tf_op jit(solution)/shard_map/ppermute | solution.py:30
  11.7 6.6 %collective-permute-start.6 = (bf16[192,512]{1,0:T(8,128)(2,1)S(1)}, bf16[192,512]{1,0:T(8,128)(2,1)S(1)}, u32[]{:S(2)}, u32[]{:S(2)}) collective-permute-start(bf16[192,512]{1,0:T(8,128)(2,1)S(1)} %collective-permute-done.1.refs_3_), channel_id=1, source_target_pairs={{0,8},{8,0},{16,24},{24,16},{1,9},{9,1},{17,25},{25,17},{2,10},{10... | collective-permute-start | bytes 589832 | tf_op jit(solution)/shard_map/ppermute | solution.py:30
  12.2 6.1 %copy-start = (bf16[768,512]{1,0:T(8,128)(2,1)S(1)}, bf16[768,512]{1,0:T(8,128)(2,1)}, u32[]{:S(2)}) copy-start(bf16[768,512]{1,0:T(8,128)(2,1)} %refs_2_.3) | copy-start | bytes 2359300
  16.0 2.3 %collective-permute-start.7 = (bf16[96,512]{1,0:T(8,128)(2,1)S(1)}, bf16[96,512]{1,0:T(8,128)(2,1)S(1)}, u32[]{:S(2)}, u32[]{:S(2)}) collective-permute-start(bf16[96,512]{1,0:T(8,128)(2,1)S(1)} %collective-permute-done.2.refs_5_), channel_id=1, source_target_pairs={{0,8},{8,0},{16,24},{24,16},{1,9},{9,1},{17,25},{25,17},{2,10},{10... | collective-permute-start | bytes 294920 | tf_op jit(solution)/shard_map/ppermute | solution.py:30
  16.0 2.3 %collective-permute-start.8 = (bf16[96,512]{1,0:T(8,128)(2,1)S(1)}, bf16[96,512]{1,0:T(8,128)(2,1)S(1)}, u32[]{:S(2)}, u32[]{:S(2)}) collective-permute-start(bf16[96,512]{1,0:T(8,128)(2,1)S(1)} %collective-permute-done.3.refs_7_), channel_id=1, source_target_pairs={{0,8},{8,0},{16,24},{24,16},{1,9},{9,1},{17,25},{25,17},{2,10},{10... | collective-permute-start | bytes 294920 | tf_op jit(solution)/shard_map/ppermute | solution.py:30
  16.5 14.3 %collective-permute-start.15 = (bf16[512,512]{1,0:T(8,128)(2,1)S(1)}, bf16[512,512]{1,0:T(8,128)(2,1)S(1)}, u32[]{:S(2)}, u32[]{:S(2)}) collective-permute-start(bf16[512,512]{1,0:T(8,128)(2,1)S(1)} %get-tuple-element.99), channel_id=1, source_target_pairs={{0,1},{1,0},{2,3},{3,2},{4,5},{5,4},{6,7},{7,6},{8,9},{9,8},{10,11... | collective-permute-start | bytes 1572872 | tf_op jit(solution)/shard_map/ppermute | solution.py:30
  20.0 5.2 %collective-permute-start.11 = (bf16[128,512]{1,0:T(8,128)(2,1)S(1)}, bf16[128,512]{1,0:T(8,128)(2,1)S(1)}, u32[]{:S(2)}, u32[]{:S(2)}) collective-permute-start(bf16[128,512]{1,0:T(8,128)(2,1)S(1)} %get-tuple-element.90.refs_5_), channel_id=1, source_target_pairs={{0,8},{8,0},{16,24},{24,16},{1,9},{9,1},{17,25},{25,17},{2,10},{10... | collective-permute-start | bytes 393224 | tf_op jit(solution)/shard_map/ppermute | solution.py:30
  20.1 7.2 %collective-permute-start.10 = (bf16[128,512]{1,0:T(8,128)(2,1)S(1)}, bf16[128,512]{1,0:T(8,128)(2,1)S(1)}, u32[]{:S(2)}, u32[]{:S(2)}) collective-permute-start(bf16[128,512]{1,0:T(8,128)(2,1)S(1)} %get-tuple-element.108), channel_id=1, source_target_pairs={{0,2},{2,0},{4,6},{6,4},{1,3},{3,1},{5,7},{7,5},{8,10},{10,8},{12,... | collective-permute-start | bytes 393224 | tf_op jit(solution)/shard_map/ppermute | solution.py:30
  21.7 7.1 %collective-permute-start.9 = (bf16[128,512]{1,0:T(8,128)(2,1)S(1)}, bf16[128,512]{1,0:T(8,128)(2,1)S(1)}, u32[]{:S(2)}, u32[]{:S(2)}) collective-permute-start(bf16[128,512]{1,0:T(8,128)(2,1)S(1)} %get-tuple-element.109), channel_id=1, source_target_pairs={{0,2},{2,0},{4,6},{6,4},{1,3},{3,1},{5,7},{7,5},{8,10},{10,8},{12,... | collective-permute-start | bytes 393224 | tf_op jit(solution)/shard_map/ppermute | solution.py:30
  22.2 8.6 %collective-permute-start.12 = (bf16[256,512]{1,0:T(8,128)(2,1)S(1)}, bf16[256,512]{1,0:T(8,128)(2,1)S(1)}, u32[]{:S(2)}, u32[]{:S(2)}) collective-permute-start(bf16[256,512]{1,0:T(8,128)(2,1)S(1)} %slice.24.refs_1_), channel_id=1, source_target_pairs={{0,8},{8,0},{16,24},{24,16},{1,9},{9,1},{17,25},{25,17},{2,10},{10... | collective-permute-start | bytes 786440 | tf_op jit(solution)/shard_map/ppermute | solution.py:30
  23.7 1.5 %copy-start.1 = (bf16[256,512]{1,0:T(8,128)(2,1)S(1)}, bf16[256,512]{1,0:T(8,128)(2,1)}, u32[]{:S(2)}) copy-start(bf16[256,512]{1,0:T(8,128)(2,1)} %refs_2_.4) | copy-start | bytes 786436
  28.8 2.0 %collective-permute-start.13 = (bf16[128,512]{1,0:T(8,128)(2,1)S(1)}, bf16[128,512]{1,0:T(8,128)(2,1)S(1)}, u32[]{:S(2)}, u32[]{:S(2)}) collective-permute-start(bf16[128,512]{1,0:T(8,128)(2,1)S(1)} %collective-permute-done.9.refs_3_), channel_id=1, source_target_pairs={{0,8},{8,0},{16,24},{24,16},{1,9},{9,1},{17,25},{25,17},{2,10},{10... | collective-permute-start | bytes 393224 | tf_op jit(solution)/shard_map/ppermute | solution.py:30
  28.8 2.0 %collective-permute-start.14 = (bf16[128,512]{1,0:T(8,128)(2,1)S(1)}, bf16[128,512]{1,0:T(8,128)(2,1)S(1)}, u32[]{:S(2)}, u32[]{:S(2)}) collective-permute-start(bf16[128,512]{1,0:T(8,128)(2,1)S(1)} %collective-permute-done.10.refs_5_), channel_id=1, source_target_pairs={{0,8},{8,0},{16,24},{24,16},{1,9},{9,1},{17,25},{25,17},{2,10},{10... | collective-permute-start | bytes 393224 | tf_op jit(solution)/shard_map/ppermute | solution.py:30
  30.8 2.0 %collective-permute-start.16 = (bf16[512,512]{1,0:T(8,128)(2,1)S(1)}, bf16[512,512]{1,0:T(8,128)(2,1)S(1)}, u32[]{:S(2)}, u32[]{:S(2)}) collective-permute-start(bf16[512,512]{1,0:T(8,128)(2,1)S(1)} %collective-permute-done.15.refs_2_), channel_id=1, source_target_pairs={{0,8},{8,0},{16,24},{24,16},{1,9},{9,1},{17,25},{25,17},{2,10},{10... | collective-permute-start | bytes 1572872 | tf_op jit(solution)/shard_map/ppermute | solution.py:30

commit v5 on v4

--- a/solution.py
+++ b/solution.py
@@ -259,8 +259,11 @@
     output[...] = add(*waiting.pop(0)).astype(output.dtype)
 
 
-def add_kernel(plan, start, hidden, piece, output):
-    output[...] = start[...] + dot_nn(hidden[:, columns_of(plan, 0, piece)], piece[...])
+def add_kernel(plan, start, hidden, *refs):
+    total = start[...]
+    for number, piece in enumerate(refs[:-1]):
+        total = total + dot_nn(hidden[:, columns_of(plan, number, piece)], piece[...])
+    refs[-1][...] = total
 
 
 def last_kernel(plan, start, hidden, *refs):
@@ -279,7 +282,7 @@
         copy.wait()
 
 
-COSTS = {"norm": 1, "slices": 1, "prepare": 1, "context": 1, "project": 20, "attend": 1, "finish": 1, "feed": 1, "hidden": 60, "add": 1, "last": 1}
+COSTS = {"norm": 1, "slices": 1, "prepare": 1, "context": 160, "project": 20, "attend": 20, "finish": 1, "feed": 1, "hidden": 1, "add": 1, "last": 1}
 
 
 def call(kernel, outs, operands, name, scratch=(), specs=None, result=VMEM):
@@ -327,7 +330,9 @@
         share_qkv = Share(0, "gx", size, size)
         share_out = Share(0, "core", out.shape[0] // 2, out.shape[0] // 2)
         share_in = Share(0, "gy", into.shape[0] // 4, into.shape[0] // 4)
-        share_down = Share(0, "core", down.shape[0] // 2, down.shape[0] // 2)
+        size = down.shape[0] // 8
+        share_early = Share(0, "gx", size, size)
+        share_late = Share(4 * size, "core", 2 * size, 2 * size)
         tokens, gain_one, gain_two, context, filled, out_x, out_y, normed, part_qkv = call(
             lambda *refs: prepare_kernel([share_qkv], *refs),
             [
@@ -343,14 +348,14 @@
             [HBM] * 8,
         )
         y_qkv = swap(part_qkv, "fsdp", 1)
-        groups = [[share_in, share_out], [share_down]]
+        groups = [[share_in], [share_out, share_early], [share_late]]
         later, normed = after(((w_in, w_out, w_down), normed))
         parts = call(
             lambda *refs: slice_kernel(groups, *refs),
             [struct(sum(share.rows for share in group), width) for group in groups],
-            later, "slices", [pltpu.SemaphoreType.DMA((3,))], [HBM] * 3,
+            (*later, later[2]), "slices", [pltpu.SemaphoreType.DMA((4,))], [HBM] * 4,
         )
-        y_middle, y_down = (swap(part, "fsdp", 1) for part in parts)
+        y_in, y_middle, y_late = (swap(part, "fsdp", 1) for part in parts)
 
     def crossed(share, near, flip=0):
         return [(share, flip, near), (share, flip + 1, swap(near, "gx", 1))]
@@ -369,25 +374,21 @@
         [pltpu.SemaphoreType.DMA((2,))], [VMEM] * 5 + [HBM] * 2,
     )
     if paired:
-        size = share_qkv.rows // 2
-        x_qkv = [swap(y_qkv[low : low + size], "gx", 2) for low in range(0, share_qkv.rows, size)]
-        x_qkv, chosen = after((x_qkv, chosen))
+        x_qkv = swap(y_qkv, "gx", 2)
+        x_qkv, y_in, chosen = after((x_qkv, y_in, chosen))
+        z_in = swap(y_in, "gy", 1)
+        if 1:
+            chosen, y_in = after((chosen, y_in))
     pieces = []
     if paired:
-        pieces = crossed(share_qkv, y_qkv)
-        for number, piece in enumerate(x_qkv):
-            pieces += crossed(share_qkv._replace(base=number * size, rows=size), piece, 2)
+        pieces = crossed(share_qkv, y_qkv) + [(share_qkv, 2, x_qkv)]
+        size = share_qkv.rows // 1
+        for low in range(0, share_qkv.rows, size):
+            pieces.append((share_qkv._replace(base=low, rows=size), 3, swap(x_qkv[low : low + size], "gx", 1)))
     projected = call(
         lambda *refs, plan=plan(pieces): project_kernel(plan, *refs), [struct(rows, width)] * 5,
         (normed, chosen, qkv, *arrays(pieces)), "project", [pltpu.VMEM((3 * width, width), jnp.bfloat16)],
     )
-
-    if paired:
-        y_middle, projected = after((y_middle, projected))
-        y_in, y_out = y_middle[: share_in.rows], y_middle[share_in.rows :]
-        size = share_in.rows // 2
-        z_in = [swap(y_in[low : low + size], "gy", 1) for low in range(0, share_in.rows, size)]
-        projected, y_in, y_out = after((projected, y_in, y_out))
 
     def attend(windows):
         return call(
@@ -399,9 +400,15 @@
     half = len(windows) // 2
     mixed = attend(windows[:half])
     pieces_out, pieces_in, pieces_down, pieces_last = [], [], [], []
+    if paired:
+        y_middle, mixed = after((y_middle, mixed))
+        y_out, y_early = y_middle[: share_out.rows], y_middle[share_out.rows :]
+        x_early = swap(y_early, "gx", 2)
+        projected, y_out, y_early = after((projected, y_out, y_early))
     mixed += attend(windows[half:])
     if paired:
         pieces_out = crossed(share_out, y_out)
+        z_in, mixed = after((z_in, mixed))
     middle, second = call(
         lambda *refs: finish_kernel(len(mixed), plan(pieces_out), *refs),
         [struct(rows, width, jnp.float32), struct(rows, width)], (tokens, gain_two, out, *mixed, *arrays(pieces_out)),
@@ -413,27 +420,22 @@
     )
     if not paired:
         return total
-    z_in, total = after((z_in, total))
     pieces = crossed(share_in, y_in)
-    size = share_in.rows // 2
-    for number, piece in enumerate(z_in):
-        pieces += crossed(share_in._replace(base=number * size, rows=size), piece, 2)
-    held, y_down = after((arrays(pieces), y_down))
+    pieces += crossed(share_in, z_in, 2)
+    held = arrays(pieces)
+    x_early, y_late, total = after((x_early, y_late, total))
     (hidden,) = call(
         lambda *refs, plan=plan(pieces): hidden_kernel(plan, *refs), [struct(rows, into.shape[0])], (second, *held), "hidden",
     )
-    size = share_down.rows // 1
-    halves = [
-        (share_down._replace(base=low, rows=size), 1, swap(y_down[low : low + size], "gx", 1))
-        for low in range(0, share_down.rows, size)
-    ]
+    first = crossed(share_early, y_early) + [(share_late, 0, y_late)]
+    rest = crossed(share_early, x_early, 2) + [(share_late, 1, swap(y_late, "gx", 1))]
     (total,) = call(
-        lambda *refs: add_kernel([(share_down, 0)], *refs), [struct(rows, width, jnp.float32)],
-        (total, hidden, y_down), "add",
+        lambda *refs: add_kernel(plan(first), *refs), [struct(rows, width, jnp.float32)],
+        (total, hidden, *arrays(first)), "add",
     )
     return call(
-        lambda *refs: last_kernel(plan(halves), *refs), [struct(rows, width)],
-        (total, hidden, *arrays(halves)), "last",
+        lambda *refs: last_kernel(plan(rest), *refs), [struct(rows, width)],
+        (total, hidden, *arrays(rest)), "last",
         [pltpu.VMEM((rows, width), jnp.bfloat16), pltpu.SemaphoreType.DMA((rows // WIN,))], result=HBM,
     )[0]
 

time: 34 us -> 32.2 us (0.947)
  waiting for transfers between devices: 6.98 us -> 3.3 us
  starting transfers between devices: 12.3 us -> 14.1 us
    ppermute x15, waiting for transfers between devices: 6.48 us -> 3.29 us  [swap(): lax.ppermute(value, axis, [(source, source ^ bit) for source in range(cou...]
    ppermute x15, starting transfers between devices: 10.7 us -> 12.5 us  [swap(): lax.ppermute(value, axis, [(source, source ^ bit) for source in range(cou...]
    ppermute x2, waiting for transfers between devices: 0.5 us -> 0.01 us  [ring(): lax.ppermute(value, axis, [(source, (source + 1) % count) for source in r...]
  transfers between devices with their start and end apart: 17 -> 17, of which waited for: 7 -> 4; matrix products, arithmetic and copies ran while one was open for 0% -> 0% of each run, Pallas kernels for 34% -> 36%
where the time goes in v5:
time: 32.2 us; the launch traced here: 32 us
  Pallas kernels  14.4 us (45%)
  starting transfers between devices  14.1 us (44%)
  waiting for transfers between devices  3.3 us (10%)
    pallas_call x11, Pallas kernels, call(): pl.pallas_call(kernel, out_shape=tuple(outs), in_specs=specs, out_specs=t...  14.4 us
    ppermute x15, starting transfers between devices, swap(): lax.ppermute(value, axis, [(source, source ^ bit) for source in range(cou...  12.5 us
    ppermute x15, waiting for transfers between devices, swap(): lax.ppermute(value, axis, [(source, source ^ bit) for source in range(cou...  3.29 us
    ppermute x2, starting transfers between devices, ring(): lax.ppermute(value, axis, [(source, (source + 1) % count) for source in r...  1.58 us
  transfers between devices with their start and end apart: 17, of which 4 were waited for; matrix products, arithmetic and copies ran while one was open for 0% of the time, Pallas kernels for 36%

profile of v5, /device:TPU:0, one launch (start us, length us, event | category | flops | bytes accessed | tf_op | source)
XLA Modules:
  0.0 32.0 jit_solution(735525020707182395)
XLA Ops:
  0.0 1.6 %prepare.1 = (bf16[512,512]{1,0:T(8,128)(2,1)S(1)}, f32[1,512]{1,0:T(1,128)S(1)}, f32[1,512]{1,0:T(1,128)S(1)}, s32[4,128]{1,0:T(4,128)S(1)}, s32[4,128]{1,0:T(4...) custom-call(bf16[512,512]{1,0:T(8,128)(2,1)} %refs_0_.1, ...), custom_call_target="tpu_custom_call" | custom-call | flops 10000000 | tf_op jit(solution)/shard_map/prepare/pallas_call | solution.py:296
  1.6 3.0 %collective-permute-start.1 = (bf16[192,512]{1,0:T(8,128)(2,1)S(1)}, bf16[192,512]{1,0:T(8,128)(2,1)S(1)}, u32[]{:S(2)}, u32[]{:S(2)}) collective-permute-start(bf16[192,512]{1,0:T(8,128)(2,1)S(1)} %get-tuple-element.58), channel_id=1, source_target_pairs={{0,1},{1,0},{2,3},{3,2},{4,5},{5,4},{6,7},{7,6},{8,9},{9,8},{10,11... | collective-permute-start | bytes 589832 | tf_op jit(solution)/shard_map/ppermute | solution.py:30
  4.6 0.0 collective-permute-start.4
  4.6 1.6 %collective-permute-start.5 = (bf16[128,512]{1,0:T(8,128)(2,1)S(1)}, bf16[128,512]{1,0:T(8,128)(2,1)S(1)}, u32[]{:S(2)}, u32[]{:S(2)}) collective-permute-start(bf16[128,512]{1,0:T(8,128)(2,1)S(1)} %get-tuple-element.61), channel_id=1, source_target_pairs={{0,2},{2,4},{4,6},{6,0},{1,3},{3,5},{5,7},{7,1},{8,10},{10,12},{12... | collective-permute-start | bytes 393224 | tf_op jit(solution)/shard_map/ppermute | solution.py:25
  6.2 1.2 %slices.1 = (bf16[256,512]{1,0:T(8,128)(2,1)S(1)}, bf16[256,512]{1,0:T(8,128)(2,1)S(1)}, bf16[256,512]{1,0:T(8,128)(2,1)S(1)}) custom-call(bf16[1024,512]{1,0:T(8,128)(2,1)} %into.1, bf16[256,512]{1,0:T(8,128)(2,1)} %refs_2_.4, bf16[1024,512]{1,0:T(8,128)(2,1)} %down.1, bf16[1024,512]{1,0:T(8,128)(2,1)} %down.1), custom_call_target="tpu_custom_call" | custom-call | flops 10000000 | tf_op jit(solution)/shard_map/slices/pallas_call | solution.py:296
  7.4 0.6 %collective-permute-start.3 = (bf16[256,512]{1,0:T(8,128)(2,1)S(1)}, bf16[256,512]{1,0:T(8,128)(2,1)S(1)}, u32[]{:S(2)}, u32[]{:S(2)}) collective-permute-start(bf16[256,512]{1,0:T(8,128)(2,1)S(1)} %get-tuple-element.59), channel_id=1, source_target_pairs={{0,1},{1,0},{2,3},{3,2},{4,5},{5,4},{6,7},{7,6},{8,9},{9,8},{10,11... | collective-permute-start | bytes 786440 | tf_op jit(solution)/shard_map/ppermute | solution.py:30
  8.0 1.6 %collective-permute-done.1.refs_3_ = bf16[192,512]{1,0:T(8,128)(2,1)S(1)} collective-permute-done((bf16[192,512]{1,0:T(8,128)(2,1)S(1)}, bf16[192,512]{1,0:T(8,128)(2,1)S(1)}, u32[]{:S(2)}, u32[]{:S(2)}) %collective-permute-start.1) | collective-permute-done | bytes 196640 | tf_op jit(solution)/shard_map/ppermute | solution.py:30
  9.5 1.7 %collective-permute-start.2 = (bf16[192,512]{1,0:T(8,128)(2,1)S(1)}, bf16[192,512]{1,0:T(8,128)(2,1)S(1)}, u32[]{:S(2)}, u32[]{:S(2)}) collective-permute-start(bf16[192,512]{1,0:T(8,128)(2,1)S(1)} %collective-permute-done.1.refs_3_), channel_id=1, source_target_pairs={{0,16},{8,24},{16,0},{24,8},{1,17},{9,25},{17,1},{25,9},{2,18},{10... | collective-permute-start | bytes 589832 | tf_op jit(solution)/shard_map/ppermute | solution.py:30
  11.3 1.8 %collective-permute-start = (bf16[256,512]{1,0:T(8,128)(2,1)S(1)}, bf16[256,512]{1,0:T(8,128)(2,1)S(1)}, u32[]{:S(2)}, u32[]{:S(2)}) collective-permute-start(bf16[256,512]{1,0:T(8,128)(2,1)S(1)} %get-tuple-element.55), channel_id=1, source_target_pairs={{0,1},{1,0},{2,3},{3,2},{4,5},{5,4},{6,7},{7,6},{8,9},{9,8},{10,11... | collective-permute-start | bytes 786440 | tf_op jit(solution)/shard_map/ppermute | solution.py:30
  13.0 0.0 collective-permute-done.4.halo_x
  13.0 0.0 collective-permute-done.5.halo_y
  13.0 0.0 copy-start
  13.1 2.0 %context.1 = (bf16[512,512]{1,0:T(8,128)(2,1)S(1)}, bf16[1024,512]{1,0:T(8,128)(2,1)S(1)}, bf16[1024,512]{1,0:T(8,128)(2,1)S(1)}) custom-call(bf16[512,512]{1,0:T(8,128)(2,1)S(1)} %get-tuple-element.57.normed.refs_0_, bf16[128,512]{1,0:T(8,128)(2,1)S(1)} %collective-permute-done.4.halo_x, bf16[128,512]{1,0:T(8,128)(2,1)S(1)} %collective-permute-done.5.halo_y, ...), custom_call_target="tpu_custom_call" | custom-call | flops 1600000000 | tf_op jit(solution)/shard_map/context/pallas_call | solution.py:296
  15.1 0.1 collective-permute-start.6
  15.1 1.3 %collective-permute-done.3.refs_1_ = bf16[256,512]{1,0:T(8,128)(2,1)S(1)} collective-permute-done((bf16[256,512]{1,0:T(8,128)(2,1)S(1)}, bf16[256,512]{1,0:T(8,128)(2,1)S(1)}, u32[]{:S(2)}, u32[]{:S(2)}) %collective-permute-start.3) | collective-permute-done | bytes 262176 | tf_op jit(solution)/shard_map/ppermute | solution.py:30
  16.4 0.0 collective-permute-done.2.refs_5_
  16.4 0.6 %collective-permute-start.7 = (bf16[192,512]{1,0:T(8,128)(2,1)S(1)}, bf16[192,512]{1,0:T(8,128)(2,1)S(1)}, u32[]{:S(2)}, u32[]{:S(2)}) collective-permute-start(bf16[192,512]{1,0:T(8,128)(2,1)S(1)} %collective-permute-done.2.refs_5_), channel_id=1, source_target_pairs={{0,8},{8,0},{16,24},{24,16},{1,9},{9,1},{17,25},{25,17},{2,10},{10... | collective-permute-start | bytes 589832 | tf_op jit(solution)/shard_map/ppermute | solution.py:30
  17.0 0.5 %collective-permute-start.9 = (bf16[256,512]{1,0:T(8,128)(2,1)S(1)}, bf16[256,512]{1,0:T(8,128)(2,1)S(1)}, u32[]{:S(2)}, u32[]{:S(2)}) collective-permute-start(bf16[256,512]{1,0:T(8,128)(2,1)S(1)} %get-tuple-element.75), channel_id=1, source_target_pairs={{0,1},{1,0},{2,3},{3,2},{4,5},{5,4},{6,7},{7,6},{8,9},{9,8},{10,11... | collective-permute-start | bytes 786440 | tf_op jit(solution)/shard_map/ppermute | solution.py:30
  17.6 1.6 %collective-permute-start.10 = (bf16[256,512]{1,0:T(8,128)(2,1)S(1)}, bf16[256,512]{1,0:T(8,128)(2,1)S(1)}, u32[]{:S(2)}, u32[]{:S(2)}) collective-permute-start(bf16[256,512]{1,0:T(8,128)(2,1)S(1)} %collective-permute-done.3.refs_1_), channel_id=1, source_target_pairs={{0,2},{2,0},{4,6},{6,4},{1,3},{3,1},{5,7},{7,5},{8,10},{10,8},{12,... | collective-permute-start | bytes 786440 | tf_op jit(solution)/shard_map/ppermute | solution.py:30
  19.1 0.0 collective-permute-done.6.refs_4_
  19.1 0.0 collective-permute-done.7.refs_6_
  19.1 0.0 copy-done
  19.1 1.6 %project.1 = (bf16[512,512]{1,0:T(8,128)(2,1)S(1)}, bf16[512,512]{1,0:T(8,128)(2,1)S(1)}, bf16[512,512]{1,0:T(8,128)(2,1)S(1)}, bf16[512,512]{1,0:T(8,128)(2,1)S(1)}, bf16[512,512]{1,0:T(8,128)(2,1)S(1)}) custom-call(bf16[512,512]{1,0:T(8,128)(2,1)S(1)} %get-tuple-element.57.normed.refs_0_, bf16[512,512]{1,0:T(8,128)(2,1)S(1)} %get-tuple-element.67.refs_1_, ...), custom_call_target="tpu_custom_call" | custom-call | flops 200000000 | tf_op jit(solution)/shard_map/project/pallas_call | solution.py:296
  20.8 1.5 %attend.2.refs_3_ = bf16[256,512]{1,0:T(8,128)(2,1)S(1)} custom-call(s32[4,128]{1,0:T(4,128)S(1)} %get-tuple-element.56.refs_0_, bf16[512,512]{1,0:T(8,128)(2,1)S(1)} %get-tuple-element.79.refs_1_, bf16[512,512]{1,0:T(8,128)(2,1)S(1)} %get-tuple-element.80.refs_2_, bf16[512,512]{1,0:T(8,128)(2,1)S(1)} %get-tuple-element.81.refs_3_, ...), custom_call_target="tpu_custom_call" | custom-call | flops 200000000 | tf_op jit(solution)/shard_map/attend/pallas_call | solution.py:296
  22.3 0.0 collective-permute-done
  22.3 0.0 copy-start.1
  22.3 0.4 %collective-permute-start.11 = (bf16[128,512]{1,0:T(8,128)(2,1)S(1)}, bf16[128,512]{1,0:T(8,128)(2,1)S(1)}, u32[]{:S(2)}, u32[]{:S(2)}) collective-permute-start(bf16[128,512]{1,0:T(8,128)(2,1)S(1)} %get-tuple-element.86.refs_5_), channel_id=1, source_target_pairs={{0,8},{8,0},{16,24},{24,16},{1,9},{9,1},{17,25},{25,17},{2,10},{10... | collective-permute-start | bytes 393224 | tf_op jit(solution)/shard_map/ppermute | solution.py:30
  22.8 1.2 %collective-permute-start.8 = (bf16[128,512]{1,0:T(8,128)(2,1)S(1)}, bf16[128,512]{1,0:T(8,128)(2,1)S(1)}, u32[]{:S(2)}, u32[]{:S(2)}) collective-permute-start(bf16[128,512]{1,0:T(8,128)(2,1)S(1)} %get-tuple-element.94.refs_2_), channel_id=1, source_target_pairs={{0,16},{8,24},{16,0},{24,8},{1,17},{9,25},{17,1},{25,9},{2,18},{10... | collective-permute-start | bytes 393224 | tf_op jit(solution)/shard_map/ppermute | solution.py:30
  23.9 0.2 collective-permute-start.12
  24.1 1.5 %attend.3.refs_4_ = bf16[256,512]{1,0:T(8,128)(2,1)S(1)} custom-call(s32[4,128]{1,0:T(4,128)S(1)} %get-tuple-element.56.refs_0_, bf16[512,512]{1,0:T(8,128)(2,1)S(1)} %get-tuple-element.79.refs_1_, bf16[512,512]{1,0:T(8,128)(2,1)S(1)} %get-tuple-element.80.refs_2_, bf16[512,512]{1,0:T(8,128)(2,1)S(1)} %get-tuple-element.81.refs_3_, ...), custom_call_target="tpu_custom_call" | custom-call | flops 200000000 | tf_op jit(solution)/shard_map/attend/pallas_call | solution.py:296
  25.6 0.2 collective-permute-done.10.refs_3_
  25.8 0.2 collective-permute-start.13
  26.0 0.0 collective-permute-done.11.refs_6_
  26.0 0.0 copy-done.1
  26.0 0.7 %finish.1 = (f32[512,512]{1,0:T(8,128)S(1)}, bf16[512,512]{1,0:T(8,128)(2,1)S(1)}) custom-call(bf16[512,512]{1,0:T(8,128)(2,1)S(1)} %get-tuple-element.76.refs_0_, f32[1,512]{1,0:T(1,128)S(1)} %get-tuple-element.77.refs_1_, bf16[256,512]{1,0:T(8,128)(2,1)S(1)} %copy-done.1, bf16[256,512]{1,0:T(8,128)(2,1)S(1)} %attend.2.refs_3_, ...), custom_call_target="tpu_custom_call" | custom-call | flops 10000000 | tf_op jit(solution)/shard_map/finish/pallas_call | solution.py:296
  26.7 1.4 %feed.1.refs_0_ = f32[512,512]{1,0:T(8,128)S(1)} custom-call(f32[512,512]{1,0:T(8,128)S(1)} %get-tuple-element.87.start, bf16[512,512]{1,0:T(8,128)(2,1)S(1)} %get-tuple-element.88.second.refs_0_, bf16[1024,512]{1,0:T(8,128)(2,1)S(1)} %get-tuple-element.89.into, bf16[1024,512]{1,0:T(8,128)(2,1)S(1)} %get-tuple-element.90.down), custom_call_target="tpu_custom_call" | custom-call | flops 10000000 | tf_op jit(solution)/shard_map/feed/pallas_call | solution.py:296
  28.1 0.0 collective-permute-done.9.refs_4_
  28.1 0.2 collective-permute-done.8.refs_2_
  28.3 0.2 collective-permute-start.16
  28.5 0.3 collective-permute-start.14
  28.8 0.2 collective-permute-start.15
  29.0 0.0 collective-permute-done.12.refs_2_
  29.0 0.0 collective-permute-done.13.refs_4_
  29.0 1.1 %hidden.1.refs_1_ = bf16[512,1024]{1,0:T(8,128)(2,1)S(1)} custom-call(bf16[512,512]{1,0:T(8,128)(2,1)S(1)} %get-tuple-element.88.second.refs_0_, bf16[256,512]{1,0:T(8,128)(2,1)S(1)} %collective-permute-done.3.refs_1_, bf16[256,512]{1,0:T(8,128)(2,1)S(1)} %collective-permute-done.12.refs_2_, bf16[256,512]{1,0:T(8,128)(2,1)S(1)} %collective-permute-done.10.refs_3_, ...), custom_call_target="tpu_custom_call" | custom-call | flops 10000000 | tf_op jit(solution)/shard_map/hidden/pallas_call | solution.py:296
  30.2 0.0 collective-permute-done.14.refs_3_
  30.2 0.6 %add.1.refs_0_ = f32[512,512]{1,0:T(8,128)S(1)} custom-call(f32[512,512]{1,0:T(8,128)S(1)} %feed.1.refs_0_, bf16[512,1024]{1,0:T(8,128)(2,1)S(1)} %hidden.1.refs_1_, bf16[128,512]{1,0:T(8,128)(2,1)S(1)} %get-tuple-element.94.refs_2_, bf16[128,512]{1,0:T(8,128)(2,1)S(1)} %collective-permute-done.14.refs_3_, bf16[256,512]{1,0:T(8,128)(2,1)S(1)} %collective-permute-done.9.refs_4_), custom_call_target="tpu_custom_call" | custom-call | flops 10000000 | tf_op jit(solution)/shard_map/add/pallas_call | solution.py:296
  30.7 0.0 collective-permute-done.15.refs_3_
  30.7 0.0 collective-permute-done.16.refs_4_
  30.8 1.3 %last.1 = bf16[512,512]{1,0:T(8,128)(2,1)} custom-call(f32[512,512]{1,0:T(8,128)S(1)} %add.1.refs_0_, bf16[512,1024]{1,0:T(8,128)(2,1)S(1)} %hidden.1.refs_1_, bf16[128,512]{1,0:T(8,128)(2,1)S(1)} %collective-permute-done.8.refs_2_, bf16[128,512]{1,0:T(8,128)(2,1)S(1)} %collective-permute-done.15.refs_3_, bf16[256,512]{1,0:T(8,128)(2,1)S(1)} %collective-permute-done.16.refs_4_), custom_call_target="tpu_custom_call" | custom-call | flops 10000000 | tf_op jit(solution)/shard_map/last/pallas_call | solution.py:296
  (1 shorter events, 0.0 us)
Async XLA Ops:
  1.6 7.9 %collective-permute-start.1 = (bf16[192,512]{1,0:T(8,128)(2,1)S(1)}, bf16[192,512]{1,0:T(8,128)(2,1)S(1)}, u32[]{:S(2)}, u32[]{:S(2)}) collective-permute-start(bf16[192,512]{1,0:T(8,128)(2,1)S(1)} %get-tuple-element.58), channel_id=1, source_target_pairs={{0,1},{1,0},{2,3},{3,2},{4,5},{5,4},{6,7},{7,6},{8,9},{9,8},{10,11... | collective-permute-start | bytes 589832 | tf_op jit(solution)/shard_map/ppermute | solution.py:30
  4.6 8.4 %collective-permute-start.4 = (bf16[128,512]{1,0:T(8,128)(2,1)S(1)}, bf16[128,512]{1,0:T(8,128)(2,1)S(1)}, u32[]{:S(2)}, u32[]{:S(2)}) collective-permute-start(bf16[128,512]{1,0:T(8,128)(2,1)S(1)} %get-tuple-element.60), channel_id=1, source_target_pairs={{0,8},{8,16},{16,24},{24,0},{1,9},{9,17},{17,25},{25,1},{2,10},{10... | collective-permute-start | bytes 393224 | tf_op jit(solution)/shard_map/ppermute | solution.py:25
  4.6 8.4 %collective-permute-start.5 = (bf16[128,512]{1,0:T(8,128)(2,1)S(1)}, bf16[128,512]{1,0:T(8,128)(2,1)S(1)}, u32[]{:S(2)}, u32[]{:S(2)}) collective-permute-start(bf16[128,512]{1,0:T(8,128)(2,1)S(1)} %get-tuple-element.61), channel_id=1, source_target_pairs={{0,2},{2,4},{4,6},{6,0},{1,3},{3,5},{5,7},{7,1},{8,10},{10,12},{12... | collective-permute-start | bytes 393224 | tf_op jit(solution)/shard_map/ppermute | solution.py:25
  7.4 9.0 %collective-permute-start.3 = (bf16[256,512]{1,0:T(8,128)(2,1)S(1)}, bf16[256,512]{1,0:T(8,128)(2,1)S(1)}, u32[]{:S(2)}, u32[]{:S(2)}) collective-permute-start(bf16[256,512]{1,0:T(8,128)(2,1)S(1)} %get-tuple-element.59), channel_id=1, source_target_pairs={{0,1},{1,0},{2,3},{3,2},{4,5},{5,4},{6,7},{7,6},{8,9},{9,8},{10,11... | collective-permute-start | bytes 786440 | tf_op jit(solution)/shard_map/ppermute | solution.py:30
  9.5 6.9 %collective-permute-start.2 = (bf16[192,512]{1,0:T(8,128)(2,1)S(1)}, bf16[192,512]{1,0:T(8,128)(2,1)S(1)}, u32[]{:S(2)}, u32[]{:S(2)}) collective-permute-start(bf16[192,512]{1,0:T(8,128)(2,1)S(1)} %collective-permute-done.1.refs_3_), channel_id=1, source_target_pairs={{0,16},{8,24},{16,0},{24,8},{1,17},{9,25},{17,1},{25,9},{2,18},{10... | collective-permute-start | bytes 589832 | tf_op jit(solution)/shard_map/ppermute | solution.py:30
  11.3 11.0 %collective-permute-start = (bf16[256,512]{1,0:T(8,128)(2,1)S(1)}, bf16[256,512]{1,0:T(8,128)(2,1)S(1)}, u32[]{:S(2)}, u32[]{:S(2)}) collective-permute-start(bf16[256,512]{1,0:T(8,128)(2,1)S(1)} %get-tuple-element.55), channel_id=1, source_target_pairs={{0,1},{1,0},{2,3},{3,2},{4,5},{5,4},{6,7},{7,6},{8,9},{9,8},{10,11... | collective-permute-start | bytes 786440 | tf_op jit(solution)/shard_map/ppermute | solution.py:30
  13.0 6.1 %copy-start = (bf16[768,512]{1,0:T(8,128)(2,1)S(1)}, bf16[768,512]{1,0:T(8,128)(2,1)}, u32[]{:S(2)}) copy-start(bf16[768,512]{1,0:T(8,128)(2,1)} %refs_2_.3) | copy-start | bytes 2359300
  15.1 4.1 %collective-permute-start.6 = (bf16[192,512]{1,0:T(8,128)(2,1)S(1)}, bf16[192,512]{1,0:T(8,128)(2,1)S(1)}, u32[]{:S(2)}, u32[]{:S(2)}) collective-permute-start(bf16[192,512]{1,0:T(8,128)(2,1)S(1)} %collective-permute-done.1.refs_3_), channel_id=1, source_target_pairs={{0,8},{8,0},{16,24},{24,16},{1,9},{9,1},{17,25},{25,17},{2,10},{10... | collective-permute-start | bytes 589832 | tf_op jit(solution)/shard_map/ppermute | solution.py:30
  16.4 2.7 %collective-permute-start.7 = (bf16[192,512]{1,0:T(8,128)(2,1)S(1)}, bf16[192,512]{1,0:T(8,128)(2,1)S(1)}, u32[]{:S(2)}, u32[]{:S(2)}) collective-permute-start(bf16[192,512]{1,0:T(8,128)(2,1)S(1)} %collective-permute-done.2.refs_5_), channel_id=1, source_target_pairs={{0,8},{8,0},{16,24},{24,16},{1,9},{9,1},{17,25},{25,17},{2,10},{10... | collective-permute-start | bytes 589832 | tf_op jit(solution)/shard_map/ppermute | solution.py:30
  17.0 11.1 %collective-permute-start.9 = (bf16[256,512]{1,0:T(8,128)(2,1)S(1)}, bf16[256,512]{1,0:T(8,128)(2,1)S(1)}, u32[]{:S(2)}, u32[]{:S(2)}) collective-permute-start(bf16[256,512]{1,0:T(8,128)(2,1)S(1)} %get-tuple-element.75), channel_id=1, source_target_pairs={{0,1},{1,0},{2,3},{3,2},{4,5},{5,4},{6,7},{7,6},{8,9},{9,8},{10,11... | collective-permute-start | bytes 786440 | tf_op jit(solution)/shard_map/ppermute | solution.py:30
  17.6 8.3 %collective-permute-start.10 = (bf16[256,512]{1,0:T(8,128)(2,1)S(1)}, bf16[256,512]{1,0:T(8,128)(2,1)S(1)}, u32[]{:S(2)}, u32[]{:S(2)}) collective-permute-start(bf16[256,512]{1,0:T(8,128)(2,1)S(1)} %collective-permute-done.3.refs_1_), channel_id=1, source_target_pairs={{0,2},{2,0},{4,6},{6,4},{1,3},{3,1},{5,7},{7,5},{8,10},{10,8},{12,... | collective-permute-start | bytes 786440 | tf_op jit(solution)/shard_map/ppermute | solution.py:30
  22.3 3.7 %copy-start.1 = (bf16[256,512]{1,0:T(8,128)(2,1)S(1)}, bf16[256,512]{1,0:T(8,128)(2,1)}, u32[]{:S(2)}) copy-start(bf16[256,512]{1,0:T(8,128)(2,1)} %refs_2_.4) | copy-start | bytes 786436
  22.3 3.7 %collective-permute-start.11 = (bf16[128,512]{1,0:T(8,128)(2,1)S(1)}, bf16[128,512]{1,0:T(8,128)(2,1)S(1)}, u32[]{:S(2)}, u32[]{:S(2)}) collective-permute-start(bf16[128,512]{1,0:T(8,128)(2,1)S(1)} %get-tuple-element.86.refs_5_), channel_id=1, source_target_pairs={{0,8},{8,0},{16,24},{24,16},{1,9},{9,1},{17,25},{25,17},{2,10},{10... | collective-permute-start | bytes 393224 | tf_op jit(solution)/shard_map/ppermute | solution.py:30
  22.8 5.5 %collective-permute-start.8 = (bf16[128,512]{1,0:T(8,128)(2,1)S(1)}, bf16[128,512]{1,0:T(8,128)(2,1)S(1)}, u32[]{:S(2)}, u32[]{:S(2)}) collective-permute-start(bf16[128,512]{1,0:T(8,128)(2,1)S(1)} %get-tuple-element.94.refs_2_), channel_id=1, source_target_pairs={{0,16},{8,24},{16,0},{24,8},{1,17},{9,25},{17,1},{25,9},{2,18},{10... | collective-permute-start | bytes 393224 | tf_op jit(solution)/shard_map/ppermute | solution.py:30
  23.9 5.1 %collective-permute-start.12 = (bf16[256,512]{1,0:T(8,128)(2,1)S(1)}, bf16[256,512]{1,0:T(8,128)(2,1)S(1)}, u32[]{:S(2)}, u32[]{:S(2)}) collective-permute-start(bf16[256,512]{1,0:T(8,128)(2,1)S(1)} %collective-permute-done.3.refs_1_), channel_id=1, source_target_pairs={{0,8},{8,0},{16,24},{24,16},{1,9},{9,1},{17,25},{25,17},{2,10},{10... | collective-permute-start | bytes 786440 | tf_op jit(solution)/shard_map/ppermute | solution.py:30
  25.8 3.2 %collective-permute-start.13 = (bf16[256,512]{1,0:T(8,128)(2,1)S(1)}, bf16[256,512]{1,0:T(8,128)(2,1)S(1)}, u32[]{:S(2)}, u32[]{:S(2)}) collective-permute-start(bf16[256,512]{1,0:T(8,128)(2,1)S(1)} %collective-permute-done.10.refs_3_), channel_id=1, source_target_pairs={{0,8},{8,0},{16,24},{24,16},{1,9},{9,1},{17,25},{25,17},{2,10},{10... | collective-permute-start | bytes 786440 | tf_op jit(solution)/shard_map/ppermute | solution.py:30
  28.3 2.4 %collective-permute-start.16 = (bf16[256,512]{1,0:T(8,128)(2,1)S(1)}, bf16[256,512]{1,0:T(8,128)(2,1)S(1)}, u32[]{:S(2)}, u32[]{:S(2)}) collective-permute-start(bf16[256,512]{1,0:T(8,128)(2,1)S(1)} %collective-permute-done.9.refs_4_), channel_id=1, source_target_pairs={{0,8},{8,0},{16,24},{24,16},{1,9},{9,1},{17,25},{25,17},{2,10},{10... | collective-permute-start | bytes 786440 | tf_op jit(solution)/shard_map/ppermute | solution.py:30
  28.5 1.6 %collective-permute-start.14 = (bf16[128,512]{1,0:T(8,128)(2,1)S(1)}, bf16[128,512]{1,0:T(8,128)(2,1)S(1)}, u32[]{:S(2)}, u32[]{:S(2)}) collective-permute-start(bf16[128,512]{1,0:T(8,128)(2,1)S(1)} %get-tuple-element.94.refs_2_), channel_id=1, source_target_pairs={{0,8},{8,0},{16,24},{24,16},{1,9},{9,1},{17,25},{25,17},{2,10},{10... | collective-permute-start | bytes 393224 | tf_op jit(solution)/shard_map/ppermute | solution.py:30
  28.8 1.9 %collective-permute-start.15 = (bf16[128,512]{1,0:T(8,128)(2,1)S(1)}, bf16[128,512]{1,0:T(8,128)(2,1)S(1)}, u32[]{:S(2)}, u32[]{:S(2)}) collective-permute-start(bf16[128,512]{1,0:T(8,128)(2,1)S(1)} %collective-permute-done.8.refs_2_), channel_id=1, source_target_pairs={{0,8},{8,0},{16,24},{24,16},{1,9},{9,1},{17,25},{25,17},{2,10},{10... | collective-permute-start | bytes 393224 | tf_op jit(solution)/shard_map/ppermute | solution.py:30

commit v6 on v5

--- a/solution.py
+++ b/solution.py
@@ -55,31 +55,69 @@
     return jnp.concatenate(blocks, axis=1)
 
 
-def norm_kernel(tokens, gain, send_x, send_y, out_x, out_y, normed):
+def pick_kernel(tokens, send_x, send_y, out_x, out_y):
     rows = tokens.shape[0]
     block = tokens[...]
     out_x[...] = dot_nn(pick_rows(send_x[...], rows), block).astype(jnp.bfloat16)
     out_y[...] = dot_nn(pick_rows(send_y[...], rows), block).astype(jnp.bfloat16)
-    normed[...] = layer_norm(block, gain[...])
 
 
 def present(halo, axis):
     return jnp.where(lax.axis_index(axis) > 0, halo[...].astype(jnp.float32), 0.0)
 
 
-def context_kernel(normed, halo_x, halo_y, gain, context, into, down, chosen, held_into, held_down, sems):
-    copies = [
-        pltpu.make_async_copy(into, held_into, sems.at[0]), pltpu.make_async_copy(down, held_down, sems.at[1])
-    ]
-    for copy in copies:
-        copy.start()
+def context_rows(tokens, halo_x, halo_y, gain, context, normed, chosen):
+    normed[...] = layer_norm(tokens[...], gain[...])
     parts = [layer_norm(present(halo_x, "gx"), gain[...]), layer_norm(present(halo_y, "gy"), gain[...])]
     pool = jnp.concatenate([normed[...]] + parts, axis=0)
     for window in range(context.shape[0]):
         picked = dot_nn(pick_rows(context[pl.ds(window, 1), :], pool.shape[0]), pool)
         chosen[pl.ds(window * CTX, CTX), :] = picked.astype(jnp.bfloat16)
+
+
+def project_half(second, weights, own, ctx, queries, own_keys, ctx_keys, own_values, ctx_values):
+    width = own.shape[1]
+    half = width // 2
+    rows, others = own[...], ctx[...]
+    if second:
+        columns, w_k = slice(half, width), weights[:half, :]
+        own_values[...] = dot_nt(weights[half:, :], rows).astype(jnp.bfloat16)
+        ctx_values[...] = dot_nt(weights[half:, :], others).astype(jnp.bfloat16)
+    else:
+        columns, w_k = slice(0, half), weights[width:, :]
+        queries[...] = dot_nt(weights[:width, :], rows).astype(jnp.bfloat16)
+    own_keys[:, columns] = dot_nt(rows, w_k).astype(jnp.bfloat16)
+    ctx_keys[:, columns] = dot_nt(others, w_k).astype(jnp.bfloat16)
+
+
+def context_kernel(tokens, halo_x, halo_y, gain, context, qkv, into, down, normed, chosen, *refs):
+    projected, (held_into, held_down, held_qkv, sems) = refs[:5], refs[5:]
+    copies = [
+        pltpu.make_async_copy(source, target, sems.at[number])
+        for number, (source, target) in enumerate([(qkv, held_qkv), (into, held_into), (down, held_down)])
+    ]
     for copy in copies:
+        copy.start()
+    context_rows(tokens, halo_x, halo_y, gain, context, normed, chosen)
+    copies[0].wait()
+    for rank in range(2):
+        @pl.when(lax.axis_index("fsdp") == rank)
+        def _(rank=rank):
+            project_half(rank == 1, held_qkv, normed, chosen, *projected)
+    for copy in copies[1:]:
         copy.wait()
+
+
+def project_rest_kernel(plan, normed, chosen, *refs):
+    pieces, refs = refs[: len(plan)], refs[len(plan) + 5 :]
+    projected, whole = refs[:5], refs[5]
+    for (share, flip), piece in zip(plan, pieces):
+        start = pl.multiple_of(share.start(flip), 32)
+        whole[pl.ds(start, share.rows), :] = piece[...]
+    for rank in range(2):
+        @pl.when(lax.axis_index("fsdp") == rank)
+        def _(rank=rank):
+            project_half(rank == 0, whole, normed, chosen, *projected)
 
 
 class Share(typing.NamedTuple):
@@ -118,20 +156,20 @@
     count = len(shares)
     (tokens, gain_one, gain_two, send_x, send_y, context, lengths), refs = refs[:7], refs[7:]
     shards, refs = refs[:count], refs[count:]
-    (held, one, two, chosen, filled, out_x, out_y, normed), refs = refs[:8], refs[8:]
+    (held, one, two, chosen, filled, out_x, out_y), refs = refs[:7], refs[7:]
     parts, (rows_x, rows_y, sizes, sems) = refs[:count], refs[count:]
-    pairs = [(tokens, held), (gain_one, one), (send_x, rows_x), (send_y, rows_y)]
+    pairs = [(tokens, held), (send_x, rows_x), (send_y, rows_y)]
     for number, share in enumerate(shares):
         start = pl.multiple_of(share.start(0), 32)
         pairs.append((shards[number].at[pl.ds(start, share.rows), :], parts[number]))
-    pairs += [(gain_two, two), (context, chosen), (lengths, sizes)]
+    pairs += [(gain_one, one), (gain_two, two), (context, chosen), (lengths, sizes)]
     copies = [pltpu.make_async_copy(*pair, sems.at[number]) for number, pair in enumerate(pairs)]
     for copy in copies:
         copy.start()
-    for copy in copies[:4]:
+    for copy in copies[:3]:
         copy.wait()
-    norm_kernel(held, one, rows_x, rows_y, out_x, out_y, normed)
-    for copy in copies[4:]:
+    pick_kernel(held, rows_x, rows_y, out_x, out_y)
+    for copy in copies[3:]:
         copy.wait()
     for window in range(filled.shape[0]):
         filled[pl.ds(window, 1), :] = jnp.full((1, LANES), sizes[window], jnp.int32)
@@ -149,11 +187,8 @@
         whole[pl.ds(start, share.rows), :] = value[...]
 
 
-def project_kernel(plan, normed, chosen, shard, *refs):
-    pieces = refs[: len(plan)]
-    queries, own_keys, ctx_keys, own_values, ctx_values, w_qkv = refs[len(plan) :]
+def project_kernel(normed, chosen, w_qkv, queries, own_keys, ctx_keys, own_values, ctx_values):
     width = normed.shape[1]
-    assemble(w_qkv, shard, [(*where, piece) for where, piece in zip(plan, pieces)])
     own, ctx = normed[...], chosen[...]
     w_q, w_k, w_v = (w_qkv[pl.ds(part * width, width), :] for part in range(3))
     queries[...] = dot_nt(w_q, own).astype(jnp.bfloat16)
@@ -237,11 +272,21 @@
     return pl.ds(pl.multiple_of(share.start(flip), LANES), share.rows)
 
 
-def hidden_kernel(plan, second, *refs):
-    hidden = refs[-1]
-    for number, piece in enumerate(refs[:-1]):
-        units = jax.nn.gelu(dot_nt(second[...], piece[...])).astype(jnp.bfloat16)
-        hidden[:, columns_of(plan, number, piece)] = units
+def hidden_kernel(plan_in, plan_down, start, second, *refs):
+    into, down, (hidden, total) = refs[: len(plan_in)], refs[len(plan_in) : -2], refs[-2:]
+    waiting = []
+
+    def keep(number, product):
+        hidden[:, columns_of(plan_in, number, into[number])] = jax.nn.gelu(product).astype(jnp.bfloat16)
+
+    for number, piece in enumerate(into):
+        waiting.append((number, dot_nt(second[...], piece[...])))
+        if len(waiting) > 1:
+            keep(*waiting.pop(0))
+    keep(*waiting.pop(0))
+    units = [hidden[:, columns_of(plan_down, number, piece)] for number, piece in enumerate(down)]
+    weights = jnp.concatenate([piece[...] for piece in down], axis=0)
+    total[...] = start[...] + dot_nn(jnp.concatenate(units, axis=1), weights)
 
 
 def feed_kernel(start, second, into, down, output):
@@ -259,22 +304,16 @@
     output[...] = add(*waiting.pop(0)).astype(output.dtype)
 
 
-def add_kernel(plan, start, hidden, *refs):
-    total = start[...]
-    for number, piece in enumerate(refs[:-1]):
-        total = total + dot_nn(hidden[:, columns_of(plan, number, piece)], piece[...])
-    refs[-1][...] = total
-
-
 def last_kernel(plan, start, hidden, *refs):
     pieces, output, held, sems = refs[: len(plan)], refs[-3], refs[-2], refs[-1]
-    blocks = start.shape[0] // WIN
+    weights = jnp.concatenate([piece[...] for piece in pieces], axis=0)
+    blocks = sems.shape[0]
+    size = start.shape[0] // blocks
     copies = []
     for block in range(blocks):
-        rows = slice(block * WIN, (block + 1) * WIN)
-        total = start[rows, :]
-        for number, piece in enumerate(pieces):
-            total = total + dot_nn(hidden[rows, columns_of(plan, number, piece)], piece[...])
+        rows = slice(block * size, (block + 1) * size)
+        units = [hidden[rows, columns_of(plan, number, piece)] for number, piece in enumerate(pieces)]
+        total = start[rows, :] + dot_nn(jnp.concatenate(units, axis=1), weights)
         held[rows, :] = total.astype(output.dtype)
         copies.append(pltpu.make_async_copy(held.at[rows, :], output.at[rows, :], sems.at[block]))
         copies[-1].start()
@@ -282,10 +321,10 @@
         copy.wait()
 
 
-COSTS = {"norm": 1, "slices": 1, "prepare": 1, "context": 160, "project": 20, "attend": 20, "finish": 1, "feed": 1, "hidden": 1, "add": 1, "last": 1}
-
-
-def call(kernel, outs, operands, name, scratch=(), specs=None, result=VMEM):
+COSTS = {"pick": 1, "slices": 1, "prepare": 1, "context": 160, "project": 20, "attend": 20, "finish": 1, "feed": 1, "hidden": 1, "last": 1}
+
+
+def call(kernel, outs, operands, name, scratch=(), specs=None, result=VMEM, aliases={}):
     specs = specs or [VMEM] * len(operands)
     placed = [
         pltpu.with_memory_space_constraint(operand, pltpu.HBM) if spec is HBM else operand
@@ -301,6 +340,7 @@
         scratch_shapes=list(scratch),
         compiler_params=PARAMS,
         name=name,
+        input_output_aliases=aliases,
         cost_estimate=pl.CostEstimate(flops=COSTS[name] * 10**7, bytes_accessed=0, transcendentals=0),
     )(*placed)
 
@@ -316,13 +356,13 @@
     send_x, send_y = send_x[None, :], send_y[None, :]
     after = lax.optimization_barrier
     paired = lax.axis_size("fsdp") == 2 and lax.axis_size("gx") == 4 and lax.axis_size("gy") % 2 == 0
-    edges = [struct(halo, width), struct(halo, width), struct(rows, width)]
+    edges = [struct(halo, width), struct(halo, width)]
 
     if not paired:
         qkv, out, into, down = (
             lax.all_gather(weight, "fsdp", axis=0, tiled=True) for weight in (w_qkv, w_out, w_in, w_down)
         )
-        out_x, out_y, normed = call(norm_kernel, edges, (tokens, gain_one, send_x, send_y), "norm")
+        out_x, out_y = call(pick_kernel, edges, (tokens, send_x, send_y), "pick")
         filled = jnp.broadcast_to(lengths[:, None], context.shape)
     else:
         qkv, out, into, down = w_qkv, w_out, w_in, w_down
@@ -333,7 +373,7 @@
         size = down.shape[0] // 8
         share_early = Share(0, "gx", size, size)
         share_late = Share(4 * size, "core", 2 * size, 2 * size)
-        tokens, gain_one, gain_two, context, filled, out_x, out_y, normed, part_qkv = call(
+        tokens, gain_one, gain_two, context, filled, out_x, out_y, part_qkv = call(
             lambda *refs: prepare_kernel([share_qkv], *refs),
             [
                 struct(rows, width), struct(1, width, jnp.float32), struct(1, width, jnp.float32),
@@ -349,7 +389,7 @@
         )
         y_qkv = swap(part_qkv, "fsdp", 1)
         groups = [[share_in], [share_out, share_early], [share_late]]
-        later, normed = after(((w_in, w_out, w_down), normed))
+        later, out_x = after(((w_in, w_out, w_down), out_x))
         parts = call(
             lambda *refs: slice_kernel(groups, *refs),
             [struct(sum(share.rows for share in group), width) for group in groups],
@@ -368,27 +408,35 @@
 
     halo_x = ring(out_x, "gx")
     halo_y = ring(out_y, "gy")
-    chosen, into, down = call(
-        context_kernel, [struct(rows, width), struct(*into.shape), struct(*down.shape)],
-        (normed, halo_x, halo_y, gain_one, context, into, down), "context",
-        [pltpu.SemaphoreType.DMA((2,))], [VMEM] * 5 + [HBM] * 2,
-    )
+    if paired:
+        normed, chosen, *projected, into, down = call(
+            context_kernel, [struct(rows, width)] * 7 + [struct(*into.shape), struct(*down.shape)],
+            (tokens, halo_x, halo_y, gain_one, context, qkv, into, down), "context",
+            [pltpu.VMEM(qkv.shape, jnp.bfloat16), pltpu.SemaphoreType.DMA((3,))], [VMEM] * 5 + [HBM] * 3,
+        )
+    else:
+        normed, chosen = call(
+            context_rows, [struct(rows, width)] * 2, (tokens, halo_x, halo_y, gain_one, context), "context"
+        )
     if paired:
         x_qkv = swap(y_qkv, "gx", 2)
         x_qkv, y_in, chosen = after((x_qkv, y_in, chosen))
         z_in = swap(y_in, "gy", 1)
         if 1:
             chosen, y_in = after((chosen, y_in))
-    pieces = []
     if paired:
         pieces = crossed(share_qkv, y_qkv) + [(share_qkv, 2, x_qkv)]
         size = share_qkv.rows // 1
         for low in range(0, share_qkv.rows, size):
             pieces.append((share_qkv._replace(base=low, rows=size), 3, swap(x_qkv[low : low + size], "gx", 1)))
-    projected = call(
-        lambda *refs, plan=plan(pieces): project_kernel(plan, *refs), [struct(rows, width)] * 5,
-        (normed, chosen, qkv, *arrays(pieces)), "project", [pltpu.VMEM((3 * width, width), jnp.bfloat16)],
-    )
+        count = 2 + len(pieces)
+        projected = call(
+            lambda *refs, plan=plan(pieces): project_rest_kernel(plan, *refs), [struct(rows, width)] * 5,
+            (normed, chosen, *arrays(pieces), *projected), "project", [pltpu.VMEM(qkv.shape, jnp.bfloat16)],
+            aliases={count + number: number for number in range(5)},
+        )
+    else:
+        projected = call(project_kernel, [struct(rows, width)] * 5, (normed, chosen, qkv), "project")
 
     def attend(windows):
         return call(
@@ -400,43 +448,54 @@
     half = len(windows) // 2
     mixed = attend(windows[:half])
     pieces_out, pieces_in, pieces_down, pieces_last = [], [], [], []
+    if 0:
+        mixed += attend(windows[half:])
     if paired:
         y_middle, mixed = after((y_middle, mixed))
         y_out, y_early = y_middle[: share_out.rows], y_middle[share_out.rows :]
         x_early = swap(y_early, "gx", 2)
         projected, y_out, y_early = after((projected, y_out, y_early))
-    mixed += attend(windows[half:])
+    if not 0:
+        mixed += attend(windows[half:])
     if paired:
         pieces_out = crossed(share_out, y_out)
-        z_in, mixed = after((z_in, mixed))
+        if 1 == 0:
+            z_in, mixed = after((z_in, mixed))
     middle, second = call(
         lambda *refs: finish_kernel(len(mixed), plan(pieces_out), *refs),
         [struct(rows, width, jnp.float32), struct(rows, width)], (tokens, gain_two, out, *mixed, *arrays(pieces_out)),
         "finish", [pltpu.VMEM((width, width), jnp.bfloat16)],
     )
 
+    if paired and 1:
+        z_in, second = after((z_in, second))
+        pieces = crossed(share_in, y_in) + crossed(share_in, z_in, 2)
+        z_in, second = after((z_in, second))
     (total,) = call(
         feed_kernel, [struct(rows, width, jnp.float32 if paired else jnp.bfloat16)], (middle, second, into, down), "feed"
     )
     if not paired:
         return total
-    pieces = crossed(share_in, y_in)
-    pieces += crossed(share_in, z_in, 2)
-    held = arrays(pieces)
-    x_early, y_late, total = after((x_early, y_late, total))
-    (hidden,) = call(
-        lambda *refs, plan=plan(pieces): hidden_kernel(plan, *refs), [struct(rows, into.shape[0])], (second, *held), "hidden",
+    if 1 == 0:
+        pieces = crossed(share_in, y_in) + crossed(share_in, z_in, 2)
+    if 0:
+        y_late, total = after((y_late, total))
+    else:
+        x_early, y_late, total = after((x_early, y_late, total))
+    late = swap(y_late, "gx", 1)
+    here = [(share_early, 0, y_early), (share_late, 0, y_late)]
+    hidden, total = call(
+        lambda *refs, plan=plan(pieces): hidden_kernel(plan, [piece[:2] for piece in here], *refs),
+        [struct(rows, into.shape[0]), struct(rows, width, jnp.float32)],
+        (total, second, *arrays(pieces), *arrays(here)), "hidden",
     )
-    first = crossed(share_early, y_early) + [(share_late, 0, y_late)]
-    rest = crossed(share_early, x_early, 2) + [(share_late, 1, swap(y_late, "gx", 1))]
-    (total,) = call(
-        lambda *refs: add_kernel(plan(first), *refs), [struct(rows, width, jnp.float32)],
-        (total, hidden, *arrays(first)), "add",
-    )
+    if 0:
+        x_early, hidden = after((x_early, hidden))
+    rest = [(share_early, 1, swap(y_early, "gx", 1))] + crossed(share_early, x_early, 2) + [(share_late, 1, late)]
     return call(
         lambda *refs: last_kernel(plan(rest), *refs), [struct(rows, width)],
         (total, hidden, *arrays(rest)), "last",
-        [pltpu.VMEM((rows, width), jnp.bfloat16), pltpu.SemaphoreType.DMA((rows // WIN,))], result=HBM,
+        [pltpu.VMEM((rows, width), jnp.bfloat16), pltpu.SemaphoreType.DMA((4,))], result=HBM,
     )[0]
 
 

time: 32.2 us -> 31.8 us (0.988)
  Pallas kernels: 14.4 us -> 13.6 us
  starting transfers between devices: 14.1 us -> 14.5 us
    pallas_call x11 -> x10, Pallas kernels: 14.4 us -> 13.6 us  [call(): pl.pallas_call(kernel, out_shape=tuple(outs), in_specs=specs, out_specs=t...]
    ppermute x15, starting transfers between devices: 12.5 us -> 12.9 us  [swap(): lax.ppermute(value, axis, [(source, source ^ bit) for source in range(cou...]
  transfers between devices with their start and end apart: 17 -> 17, of which waited for: 4 -> 4; matrix products, arithmetic and copies ran while one was open for 0% -> 0% of each run, Pallas kernels for 36% -> 34%
where the time goes in v6:
time: 31.8 us; the launch traced here: 31.6 us
  starting transfers between devices  14.5 us (46%)
  Pallas kernels  13.6 us (43%)
  waiting for transfers between devices  3.38 us (11%)
    pallas_call x10, Pallas kernels, call(): pl.pallas_call(kernel, out_shape=tuple(outs), in_specs=specs, out_specs=t...  13.6 us
    ppermute x15, starting transfers between devices, swap(): lax.ppermute(value, axis, [(source, source ^ bit) for source in range(cou...  12.9 us
    ppermute x15, waiting for transfers between devices, swap(): lax.ppermute(value, axis, [(source, source ^ bit) for source in range(cou...  3.38 us
    ppermute x2, starting transfers between devices, ring(): lax.ppermute(value, axis, [(source, (source + 1) % count) for source in r...  1.58 us
  transfers between devices with their start and end apart: 17, of which 4 were waited for; matrix products, arithmetic and copies ran while one was open for 0% of the time, Pallas kernels for 34%

profile of v6, /device:TPU:0, one launch (start us, length us, event | category | flops | bytes accessed | tf_op | source)
XLA Modules:
  0.0 31.6 jit_solution(14710933278637593963)
XLA Ops:
  0.0 1.5 %prepare.1 = (bf16[512,512]{1,0:T(8,128)(2,1)S(1)}, f32[1,512]{1,0:T(1,128)S(1)}, f32[1,512]{1,0:T(1,128)S(1)}, s32[4,128]{1,0:T(4,128)S(1)}, s32[4,128]{1,0:T(4...) custom-call(bf16[512,512]{1,0:T(8,128)(2,1)} %refs_0_.1, ...), custom_call_target="tpu_custom_call" | custom-call | flops 10000000 | tf_op jit(solution)/shard_map/prepare/pallas_call | solution.py:335
  1.5 3.0 %collective-permute-start.3 = (bf16[192,512]{1,0:T(8,128)(2,1)S(1)}, bf16[192,512]{1,0:T(8,128)(2,1)S(1)}, u32[]{:S(2)}, u32[]{:S(2)}) collective-permute-start(bf16[192,512]{1,0:T(8,128)(2,1)S(1)} %get-tuple-element.70), channel_id=1, source_target_pairs={{0,1},{1,0},{2,3},{3,2},{4,5},{5,4},{6,7},{7,6},{8,9},{9,8},{10,11... | collective-permute-start | bytes 589832 | tf_op jit(solution)/shard_map/ppermute | solution.py:30
  4.5 0.0 collective-permute-start.1
  4.5 1.6 %collective-permute-start.2 = (bf16[128,512]{1,0:T(8,128)(2,1)S(1)}, bf16[128,512]{1,0:T(8,128)(2,1)S(1)}, u32[]{:S(2)}, u32[]{:S(2)}) collective-permute-start(bf16[128,512]{1,0:T(8,128)(2,1)S(1)} %get-tuple-element.66), channel_id=1, source_target_pairs={{0,2},{2,4},{4,6},{6,0},{1,3},{3,5},{5,7},{7,1},{8,10},{10,12},{12... | collective-permute-start | bytes 393224 | tf_op jit(solution)/shard_map/ppermute | solution.py:25
  6.1 1.2 %slices.1 = (bf16[256,512]{1,0:T(8,128)(2,1)S(1)}, bf16[256,512]{1,0:T(8,128)(2,1)S(1)}, bf16[256,512]{1,0:T(8,128)(2,1)S(1)}) custom-call(bf16[1024,512]{1,0:T(8,128)(2,1)} %into.1, bf16[256,512]{1,0:T(8,128)(2,1)} %refs_2_.2, bf16[1024,512]{1,0:T(8,128)(2,1)} %down.1, bf16[1024,512]{1,0:T(8,128)(2,1)} %down.1), custom_call_target="tpu_custom_call" | custom-call | flops 10000000 | tf_op jit(solution)/shard_map/slices/pallas_call | solution.py:335
  7.3 0.6 %collective-permute-start.5 = (bf16[256,512]{1,0:T(8,128)(2,1)S(1)}, bf16[256,512]{1,0:T(8,128)(2,1)S(1)}, u32[]{:S(2)}, u32[]{:S(2)}) collective-permute-start(bf16[256,512]{1,0:T(8,128)(2,1)S(1)} %get-tuple-element.71), channel_id=1, source_target_pairs={{0,1},{1,0},{2,3},{3,2},{4,5},{5,4},{6,7},{7,6},{8,9},{9,8},{10,11... | collective-permute-start | bytes 786440 | tf_op jit(solution)/shard_map/ppermute | solution.py:30
  7.9 1.6 %collective-permute-done.3.refs_2_ = bf16[192,512]{1,0:T(8,128)(2,1)S(1)} collective-permute-done((bf16[192,512]{1,0:T(8,128)(2,1)S(1)}, bf16[192,512]{1,0:T(8,128)(2,1)S(1)}, u32[]{:S(2)}, u32[]{:S(2)}) %collective-permute-start.3) | collective-permute-done | bytes 196640 | tf_op jit(solution)/shard_map/ppermute | solution.py:30
  9.4 1.7 %collective-permute-start.4 = (bf16[192,512]{1,0:T(8,128)(2,1)S(1)}, bf16[192,512]{1,0:T(8,128)(2,1)S(1)}, u32[]{:S(2)}, u32[]{:S(2)}) collective-permute-start(bf16[192,512]{1,0:T(8,128)(2,1)S(1)} %collective-permute-done.3.refs_2_), channel_id=1, source_target_pairs={{0,16},{8,24},{16,0},{24,8},{1,17},{9,25},{17,1},{25,9},{2,18},{10... | collective-permute-start | bytes 589832 | tf_op jit(solution)/shard_map/ppermute | solution.py:30
  11.1 1.8 %collective-permute-start = (bf16[256,512]{1,0:T(8,128)(2,1)S(1)}, bf16[256,512]{1,0:T(8,128)(2,1)S(1)}, u32[]{:S(2)}, u32[]{:S(2)}) collective-permute-start(bf16[256,512]{1,0:T(8,128)(2,1)S(1)} %get-tuple-element.62), channel_id=1, source_target_pairs={{0,1},{1,0},{2,3},{3,2},{4,5},{5,4},{6,7},{7,6},{8,9},{9,8},{10,11... | collective-permute-start | bytes 786440 | tf_op jit(solution)/shard_map/ppermute | solution.py:30
  12.9 0.0 collective-permute-done.1.halo_x
  12.9 0.0 collective-permute-done.2.halo_y
  12.9 2.0 %context.1 = (bf16[512,512]{1,0:T(8,128)(2,1)S(1)}, bf16[512,512]{1,0:T(8,128)(2,1)S(1)}, bf16[512,512]{1,0:T(8,128)(2,1)S(1)}, bf16[512,512]{1,0:T(8,128)(2,1)S...) custom-call(bf16[512,512]{1,0:T(8,128)(2,1)S(1)} %get-tuple-element., ...), custom_call_target="tpu_custom_call" | custom-call | flops 1600000000 | tf_op jit(solution)/shard_map/context/pallas_call | solution.py:335
  14.9 0.1 collective-permute-start.6
  15.0 1.3 %collective-permute-done.5.refs_2_ = bf16[256,512]{1,0:T(8,128)(2,1)S(1)} collective-permute-done((bf16[256,512]{1,0:T(8,128)(2,1)S(1)}, bf16[256,512]{1,0:T(8,128)(2,1)S(1)}, u32[]{:S(2)}, u32[]{:S(2)}) %collective-permute-start.5) | collective-permute-done | bytes 262176 | tf_op jit(solution)/shard_map/ppermute | solution.py:30
  16.3 0.0 collective-permute-done.4.refs_4_
  16.3 0.6 %collective-permute-start.7 = (bf16[192,512]{1,0:T(8,128)(2,1)S(1)}, bf16[192,512]{1,0:T(8,128)(2,1)S(1)}, u32[]{:S(2)}, u32[]{:S(2)}) collective-permute-start(bf16[192,512]{1,0:T(8,128)(2,1)S(1)} %collective-permute-done.4.refs_4_), channel_id=1, source_target_pairs={{0,8},{8,0},{16,24},{24,16},{1,9},{9,1},{17,25},{25,17},{2,10},{10... | collective-permute-start | bytes 589832 | tf_op jit(solution)/shard_map/ppermute | solution.py:30
  16.9 0.5 %collective-permute-start.9 = (bf16[256,512]{1,0:T(8,128)(2,1)S(1)}, bf16[256,512]{1,0:T(8,128)(2,1)S(1)}, u32[]{:S(2)}, u32[]{:S(2)}) collective-permute-start(bf16[256,512]{1,0:T(8,128)(2,1)S(1)} %get-tuple-element.88), channel_id=1, source_target_pairs={{0,1},{1,0},{2,3},{3,2},{4,5},{5,4},{6,7},{7,6},{8,9},{9,8},{10,11... | collective-permute-start | bytes 786440 | tf_op jit(solution)/shard_map/ppermute | solution.py:30
  17.4 1.6 %collective-permute-start.11 = (bf16[256,512]{1,0:T(8,128)(2,1)S(1)}, bf16[256,512]{1,0:T(8,128)(2,1)S(1)}, u32[]{:S(2)}, u32[]{:S(2)}) collective-permute-start(bf16[256,512]{1,0:T(8,128)(2,1)S(1)} %collective-permute-done.5.refs_2_), channel_id=1, source_target_pairs={{0,2},{2,0},{4,6},{6,4},{1,3},{3,1},{5,7},{7,5},{8,10},{10,8},{12,... | collective-permute-start | bytes 786440 | tf_op jit(solution)/shard_map/ppermute | solution.py:30
  19.0 0.0 collective-permute-done.6.refs_3_
  19.0 0.0 collective-permute-done.7.refs_5_
  19.0 1.1 %project.1 = (bf16[512,512]{1,0:T(8,128)(2,1)S(1)}, bf16[512,512]{1,0:T(8,128)(2,1)S(1)}, bf16[512,512]{1,0:T(8,128)(2,1)S(1)}, bf16[512,512]{1,0:T(8,128)(2,1)S(1)}, bf16[512,512]{1,0:T(8,128)(2,1)S(1)}) custom-call(bf16[512,512]{1,0:T(8,128)(2,1)S(1)} %get-tuple-element.69.refs_0_, ...), custom_call_target="tpu_custom_call", output_to_operand_aliasing={{0}: (6, {}), {1}: (7, {}), {2}: (8, {}), {3}: (9, {}), {4}... | custom-call | flops 200000000 | tf_op jit(solution)/shard_map/project/pallas_call | solution.py:335
  20.1 1.5 %attend.2.refs_3_ = bf16[256,512]{1,0:T(8,128)(2,1)S(1)} custom-call(s32[4,128]{1,0:T(4,128)S(1)} %get-tuple-element.63.refs_0_, bf16[512,512]{1,0:T(8,128)(2,1)S(1)} %get-tuple-element.91.refs_1_, bf16[512,512]{1,0:T(8,128)(2,1)S(1)} %get-tuple-element.92.refs_2_, bf16[512,512]{1,0:T(8,128)(2,1)S(1)} %get-tuple-element.93.refs_3_, ...), custom_call_target="tpu_custom_call" | custom-call | flops 200000000 | tf_op jit(solution)/shard_map/attend/pallas_call | solution.py:335
  21.6 0.3 %collective-permute-done = bf16[256,512]{1,0:T(8,128)(2,1)S(1)} collective-permute-done((bf16[256,512]{1,0:T(8,128)(2,1)S(1)}, bf16[256,512]{1,0:T(8,128)(2,1)S(1)}, u32[]{:S(2)}, u32[]{:S(2)}) %collective-permute-start) | collective-permute-done | bytes 262176 | tf_op jit(solution)/shard_map/ppermute | solution.py:30
  21.9 0.0 copy-start
  21.9 0.7 %collective-permute-start.10 = (bf16[128,512]{1,0:T(8,128)(2,1)S(1)}, bf16[128,512]{1,0:T(8,128)(2,1)S(1)}, u32[]{:S(2)}, u32[]{:S(2)}) collective-permute-start(bf16[128,512]{1,0:T(8,128)(2,1)S(1)} %get-tuple-element.96.refs_5_), channel_id=1, source_target_pairs={{0,8},{8,0},{16,24},{24,16},{1,9},{9,1},{17,25},{25,17},{2,10},{10... | collective-permute-start | bytes 393224 | tf_op jit(solution)/shard_map/ppermute | solution.py:30
  22.6 1.1 %collective-permute-start.8 = (bf16[128,512]{1,0:T(8,128)(2,1)S(1)}, bf16[128,512]{1,0:T(8,128)(2,1)S(1)}, u32[]{:S(2)}, u32[]{:S(2)}) collective-permute-start(bf16[128,512]{1,0:T(8,128)(2,1)S(1)} %get-tuple-element.105.refs_6_), channel_id=1, source_target_pairs={{0,16},{8,24},{16,0},{24,8},{1,17},{9,25},{17,1},{25,9},{2,18},{10... | collective-permute-start | bytes 393224 | tf_op jit(solution)/shard_map/ppermute | solution.py:30
  23.8 0.2 collective-permute-start.12
  24.0 1.5 %attend.3.refs_4_ = bf16[256,512]{1,0:T(8,128)(2,1)S(1)} custom-call(s32[4,128]{1,0:T(4,128)S(1)} %get-tuple-element.63.refs_0_, bf16[512,512]{1,0:T(8,128)(2,1)S(1)} %get-tuple-element.91.refs_1_, bf16[512,512]{1,0:T(8,128)(2,1)S(1)} %get-tuple-element.92.refs_2_, bf16[512,512]{1,0:T(8,128)(2,1)S(1)} %get-tuple-element.93.refs_3_, ...), custom_call_target="tpu_custom_call" | custom-call | flops 200000000 | tf_op jit(solution)/shard_map/attend/pallas_call | solution.py:335
  25.4 0.0 collective-permute-done.10.refs_6_
  25.4 0.0 copy-done
  25.4 0.7 %finish.1 = (f32[512,512]{1,0:T(8,128)S(1)}, bf16[512,512]{1,0:T(8,128)(2,1)S(1)}) custom-call(bf16[512,512]{1,0:T(8,128)(2,1)S(1)} %get-tuple-element.64.tokens.refs_0_, f32[1,512]{1,0:T(1,128)S(1)} %get-tuple-element.89.refs_1_, bf16[256,512]{1,0:T(8,128)(2,1)S(1)} %copy-done, bf16[256,512]{1,0:T(8,128)(2,1)S(1)} %attend.2.refs_3_, ...), custom_call_target="tpu_custom_call" | custom-call | flops 10000000 | tf_op jit(solution)/shard_map/finish/pallas_call | solution.py:335
  26.2 0.0 collective-permute-done.11.refs_4_
  26.2 0.4 %collective-permute-start.13 = (bf16[256,512]{1,0:T(8,128)(2,1)S(1)}, bf16[256,512]{1,0:T(8,128)(2,1)S(1)}, u32[]{:S(2)}, u32[]{:S(2)}) collective-permute-start(bf16[256,512]{1,0:T(8,128)(2,1)S(1)} %collective-permute-done.11.refs_4_), channel_id=1, source_target_pairs={{0,8},{8,0},{16,24},{24,16},{1,9},{9,1},{17,25},{25,17},{2,10},{10... | collective-permute-start | bytes 786440 | tf_op jit(solution)/shard_map/ppermute | solution.py:30
  26.6 1.4 %feed.1.refs_0_ = f32[512,512]{1,0:T(8,128)S(1)} custom-call(f32[512,512]{1,0:T(8,128)S(1)} %get-tuple-element.97.start, bf16[512,512]{1,0:T(8,128)(2,1)S(1)} %get-tuple-element.99.second.refs_1_, bf16[1024,512]{1,0:T(8,128)(2,1)S(1)} %get-tuple-element.100.into, bf16[1024,512]{1,0:T(8,128)(2,1)S(1)} %get-tuple-element.101.down), custom_call_target="tpu_custom_call" | custom-call | flops 10000000 | tf_op jit(solution)/shard_map/feed/pallas_call | solution.py:335
  28.0 0.0 collective-permute-done.9.refs_7_
  28.0 0.1 collective-permute-done.8.refs_3_
  28.1 0.1 collective-permute-start.16
  28.2 0.4 %collective-permute-start.14 = (bf16[128,512]{1,0:T(8,128)(2,1)S(1)}, bf16[128,512]{1,0:T(8,128)(2,1)S(1)}, u32[]{:S(2)}, u32[]{:S(2)}) collective-permute-start(bf16[128,512]{1,0:T(8,128)(2,1)S(1)} %get-tuple-element.105.refs_6_), channel_id=1, source_target_pairs={{0,8},{8,0},{16,24},{24,16},{1,9},{9,1},{17,25},{25,17},{2,10},{10... | collective-permute-start | bytes 393224 | tf_op jit(solution)/shard_map/ppermute | solution.py:30
  28.6 0.1 collective-permute-start.15
  28.7 0.0 collective-permute-done.12.refs_3_
  28.7 0.0 collective-permute-done.13.refs_5_
  28.7 1.5 %hidden.1 = (bf16[512,1024]{1,0:T(8,128)(2,1)S(1)}, f32[512,512]{1,0:T(8,128)S(1)}) custom-call(f32[512,512]{1,0:T(8,128)S(1)} %feed.1.refs_0_, bf16[512,512]{1,0:T(8,128)(2,1)S(1)} %get-tuple-element.99.second.refs_1_, bf16[256,512]{1,0:T(8,128)(2,1)S(1)} %collective-permute-done.5.refs_2_, bf16[256,512]{1,0:T(8,128)(2,1)S(1)} %collective-permute-done.12.refs_3_, ...), custom_call_target="tpu_custom_call" | custom-call | flops 10000000 | tf_op jit(solution)/shard_map/hidden/pallas_call | solution.py:335
  30.3 0.0 collective-permute-done.14.refs_2_
  30.3 0.0 collective-permute-done.15.refs_4_
  30.3 0.0 collective-permute-done.16.refs_5_
  30.3 1.3 %last.1 = bf16[512,512]{1,0:T(8,128)(2,1)} custom-call(f32[512,512]{1,0:T(8,128)S(1)} %get-tuple-element.107.refs_0_, bf16[512,1024]{1,0:T(8,128)(2,1)S(1)} %get-tuple-element.108.refs_1_, bf16[128,512]{1,0:T(8,128)(2,1)S(1)} %collective-permute-done.14.refs_2_, bf16[128,512]{1,0:T(8,128)(2,1)S(1)} %collective-permute-done.8.refs_3_, ...), custom_call_target="tpu_custom_call" | custom-call | flops 10000000 | tf_op jit(solution)/shard_map/last/pallas_call | solution.py:335
  (1 shorter events, 0.0 us)
Async XLA Ops:
  1.5 7.9 %collective-permute-start.3 = (bf16[192,512]{1,0:T(8,128)(2,1)S(1)}, bf16[192,512]{1,0:T(8,128)(2,1)S(1)}, u32[]{:S(2)}, u32[]{:S(2)}) collective-permute-start(bf16[192,512]{1,0:T(8,128)(2,1)S(1)} %get-tuple-element.70), channel_id=1, source_target_pairs={{0,1},{1,0},{2,3},{3,2},{4,5},{5,4},{6,7},{7,6},{8,9},{9,8},{10,11... | collective-permute-start | bytes 589832 | tf_op jit(solution)/shard_map/ppermute | solution.py:30
  4.5 8.4 %collective-permute-start.1 = (bf16[128,512]{1,0:T(8,128)(2,1)S(1)}, bf16[128,512]{1,0:T(8,128)(2,1)S(1)}, u32[]{:S(2)}, u32[]{:S(2)}) collective-permute-start(bf16[128,512]{1,0:T(8,128)(2,1)S(1)} %get-tuple-element.65), channel_id=1, source_target_pairs={{0,8},{8,16},{16,24},{24,0},{1,9},{9,17},{17,25},{25,1},{2,10},{10... | collective-permute-start | bytes 393224 | tf_op jit(solution)/shard_map/ppermute | solution.py:25
  4.5 8.4 %collective-permute-start.2 = (bf16[128,512]{1,0:T(8,128)(2,1)S(1)}, bf16[128,512]{1,0:T(8,128)(2,1)S(1)}, u32[]{:S(2)}, u32[]{:S(2)}) collective-permute-start(bf16[128,512]{1,0:T(8,128)(2,1)S(1)} %get-tuple-element.66), channel_id=1, source_target_pairs={{0,2},{2,4},{4,6},{6,0},{1,3},{3,5},{5,7},{7,1},{8,10},{10,12},{12... | collective-permute-start | bytes 393224 | tf_op jit(solution)/shard_map/ppermute | solution.py:25
  7.3 9.0 %collective-permute-start.5 = (bf16[256,512]{1,0:T(8,128)(2,1)S(1)}, bf16[256,512]{1,0:T(8,128)(2,1)S(1)}, u32[]{:S(2)}, u32[]{:S(2)}) collective-permute-start(bf16[256,512]{1,0:T(8,128)(2,1)S(1)} %get-tuple-element.71), channel_id=1, source_target_pairs={{0,1},{1,0},{2,3},{3,2},{4,5},{5,4},{6,7},{7,6},{8,9},{9,8},{10,11... | collective-permute-start | bytes 786440 | tf_op jit(solution)/shard_map/ppermute | solution.py:30
  9.4 6.9 %collective-permute-start.4 = (bf16[192,512]{1,0:T(8,128)(2,1)S(1)}, bf16[192,512]{1,0:T(8,128)(2,1)S(1)}, u32[]{:S(2)}, u32[]{:S(2)}) collective-permute-start(bf16[192,512]{1,0:T(8,128)(2,1)S(1)} %collective-permute-done.3.refs_2_), channel_id=1, source_target_pairs={{0,16},{8,24},{16,0},{24,8},{1,17},{9,25},{17,1},{25,9},{2,18},{10... | collective-permute-start | bytes 589832 | tf_op jit(solution)/shard_map/ppermute | solution.py:30
  11.1 10.8 %collective-permute-start = (bf16[256,512]{1,0:T(8,128)(2,1)S(1)}, bf16[256,512]{1,0:T(8,128)(2,1)S(1)}, u32[]{:S(2)}, u32[]{:S(2)}) collective-permute-start(bf16[256,512]{1,0:T(8,128)(2,1)S(1)} %get-tuple-element.62), channel_id=1, source_target_pairs={{0,1},{1,0},{2,3},{3,2},{4,5},{5,4},{6,7},{7,6},{8,9},{9,8},{10,11... | collective-permute-start | bytes 786440 | tf_op jit(solution)/shard_map/ppermute | solution.py:30
  14.9 4.1 %collective-permute-start.6 = (bf16[192,512]{1,0:T(8,128)(2,1)S(1)}, bf16[192,512]{1,0:T(8,128)(2,1)S(1)}, u32[]{:S(2)}, u32[]{:S(2)}) collective-permute-start(bf16[192,512]{1,0:T(8,128)(2,1)S(1)} %collective-permute-done.3.refs_2_), channel_id=1, source_target_pairs={{0,8},{8,0},{16,24},{24,16},{1,9},{9,1},{17,25},{25,17},{2,10},{10... | collective-permute-start | bytes 589832 | tf_op jit(solution)/shard_map/ppermute | solution.py:30
  16.3 2.7 %collective-permute-start.7 = (bf16[192,512]{1,0:T(8,128)(2,1)S(1)}, bf16[192,512]{1,0:T(8,128)(2,1)S(1)}, u32[]{:S(2)}, u32[]{:S(2)}) collective-permute-start(bf16[192,512]{1,0:T(8,128)(2,1)S(1)} %collective-permute-done.4.refs_4_), channel_id=1, source_target_pairs={{0,8},{8,0},{16,24},{24,16},{1,9},{9,1},{17,25},{25,17},{2,10},{10... | collective-permute-start | bytes 589832 | tf_op jit(solution)/shard_map/ppermute | solution.py:30
  16.9 11.1 %collective-permute-start.9 = (bf16[256,512]{1,0:T(8,128)(2,1)S(1)}, bf16[256,512]{1,0:T(8,128)(2,1)S(1)}, u32[]{:S(2)}, u32[]{:S(2)}) collective-permute-start(bf16[256,512]{1,0:T(8,128)(2,1)S(1)} %get-tuple-element.88), channel_id=1, source_target_pairs={{0,1},{1,0},{2,3},{3,2},{4,5},{5,4},{6,7},{7,6},{8,9},{9,8},{10,11... | collective-permute-start | bytes 786440 | tf_op jit(solution)/shard_map/ppermute | solution.py:30
  17.4 8.7 %collective-permute-start.11 = (bf16[256,512]{1,0:T(8,128)(2,1)S(1)}, bf16[256,512]{1,0:T(8,128)(2,1)S(1)}, u32[]{:S(2)}, u32[]{:S(2)}) collective-permute-start(bf16[256,512]{1,0:T(8,128)(2,1)S(1)} %collective-permute-done.5.refs_2_), channel_id=1, source_target_pairs={{0,2},{2,0},{4,6},{6,4},{1,3},{3,1},{5,7},{7,5},{8,10},{10,8},{12,... | collective-permute-start | bytes 786440 | tf_op jit(solution)/shard_map/ppermute | solution.py:30
  21.9 3.5 %copy-start = (bf16[256,512]{1,0:T(8,128)(2,1)S(1)}, bf16[256,512]{1,0:T(8,128)(2,1)}, u32[]{:S(2)}) copy-start(bf16[256,512]{1,0:T(8,128)(2,1)} %refs_2_.2) | copy-start | bytes 786436
  21.9 3.5 %collective-permute-start.10 = (bf16[128,512]{1,0:T(8,128)(2,1)S(1)}, bf16[128,512]{1,0:T(8,128)(2,1)S(1)}, u32[]{:S(2)}, u32[]{:S(2)}) collective-permute-start(bf16[128,512]{1,0:T(8,128)(2,1)S(1)} %get-tuple-element.96.refs_5_), channel_id=1, source_target_pairs={{0,8},{8,0},{16,24},{24,16},{1,9},{9,1},{17,25},{25,17},{2,10},{10... | collective-permute-start | bytes 393224 | tf_op jit(solution)/shard_map/ppermute | solution.py:30
  22.6 5.5 %collective-permute-start.8 = (bf16[128,512]{1,0:T(8,128)(2,1)S(1)}, bf16[128,512]{1,0:T(8,128)(2,1)S(1)}, u32[]{:S(2)}, u32[]{:S(2)}) collective-permute-start(bf16[128,512]{1,0:T(8,128)(2,1)S(1)} %get-tuple-element.105.refs_6_), channel_id=1, source_target_pairs={{0,16},{8,24},{16,0},{24,8},{1,17},{9,25},{17,1},{25,9},{2,18},{10... | collective-permute-start | bytes 393224 | tf_op jit(solution)/shard_map/ppermute | solution.py:30
  23.8 5.0 %collective-permute-start.12 = (bf16[256,512]{1,0:T(8,128)(2,1)S(1)}, bf16[256,512]{1,0:T(8,128)(2,1)S(1)}, u32[]{:S(2)}, u32[]{:S(2)}) collective-permute-start(bf16[256,512]{1,0:T(8,128)(2,1)S(1)} %collective-permute-done.5.refs_2_), channel_id=1, source_target_pairs={{0,8},{8,0},{16,24},{24,16},{1,9},{9,1},{17,25},{25,17},{2,10},{10... | collective-permute-start | bytes 786440 | tf_op jit(solution)/shard_map/ppermute | solution.py:30
  26.2 2.6 %collective-permute-start.13 = (bf16[256,512]{1,0:T(8,128)(2,1)S(1)}, bf16[256,512]{1,0:T(8,128)(2,1)S(1)}, u32[]{:S(2)}, u32[]{:S(2)}) collective-permute-start(bf16[256,512]{1,0:T(8,128)(2,1)S(1)} %collective-permute-done.11.refs_4_), channel_id=1, source_target_pairs={{0,8},{8,0},{16,24},{24,16},{1,9},{9,1},{17,25},{25,17},{2,10},{10... | collective-permute-start | bytes 786440 | tf_op jit(solution)/shard_map/ppermute | solution.py:30
  28.1 2.2 %collective-permute-start.16 = (bf16[256,512]{1,0:T(8,128)(2,1)S(1)}, bf16[256,512]{1,0:T(8,128)(2,1)S(1)}, u32[]{:S(2)}, u32[]{:S(2)}) collective-permute-start(bf16[256,512]{1,0:T(8,128)(2,1)S(1)} %collective-permute-done.9.refs_7_), channel_id=1, source_target_pairs={{0,8},{8,0},{16,24},{24,16},{1,9},{9,1},{17,25},{25,17},{2,10},{10... | collective-permute-start | bytes 786440 | tf_op jit(solution)/shard_map/ppermute | solution.py:30
  28.2 2.0 %collective-permute-start.14 = (bf16[128,512]{1,0:T(8,128)(2,1)S(1)}, bf16[128,512]{1,0:T(8,128)(2,1)S(1)}, u32[]{:S(2)}, u32[]{:S(2)}) collective-permute-start(bf16[128,512]{1,0:T(8,128)(2,1)S(1)} %get-tuple-element.105.refs_6_), channel_id=1, source_target_pairs={{0,8},{8,0},{16,24},{24,16},{1,9},{9,1},{17,25},{25,17},{2,10},{10... | collective-permute-start | bytes 393224 | tf_op jit(solution)/shard_map/ppermute | solution.py:30
  28.6 1.7 %collective-permute-start.15 = (bf16[128,512]{1,0:T(8,128)(2,1)S(1)}, bf16[128,512]{1,0:T(8,128)(2,1)S(1)}, u32[]{:S(2)}, u32[]{:S(2)}) collective-permute-start(bf16[128,512]{1,0:T(8,128)(2,1)S(1)} %collective-permute-done.8.refs_3_), channel_id=1, source_target_pairs={{0,8},{8,0},{16,24},{24,16},{1,9},{9,1},{17,25},{25,17},{2,10},{10... | collective-permute-start | bytes 393224 | tf_op jit(solution)/shard_map/ppermute | solution.py:30
